TPU v7x, 32 devices: a whole 2x2x4 slice. The times are simulated.
32 devices in a mesh: row: 16 (over z, x, core), col: 2 (over y).
Axes of the slice: x: 2, y: 2, z: 4, core: 2. Of those that a mesh axis runs over, the one named last changes fastest.
Arguments:
- amplitudes: bfloat16 [64, 640000], P(('row', 'col')), may hold values from -6 to 6
- integrals: bfloat16 [2, 800, 640000], P(None, None, ('row', 'col')), may hold values from -0.0078125 to 0.0078125
Outputs:
- ladder: float32 [64, 2, 800], P(('row', 'col'))
All inputs are finite; a program needn't handle non-finite values.
Results may differ from a plain program's by a relative error of at most 0.0003.
Values may be sent and summed in bfloat16 or wider, within the bound.
No kernel may reach another device: no remote copies, remote signals or barrier semaphores. Data moves between devices by JAX's collectives and lax.ppermute only.
A program may use at most 128 MiB of HBM per device.

v0:
```python
import jax
import jax.numpy as jnp
from jax import lax
from jax.sharding import PartitionSpec as P


def shards(amplitudes, integrals):
    row_count = lax.axis_size("row")
    col_count = lax.axis_size("col")
    pair_local = amplitudes.shape[0]
    full_width = amplitudes.shape[1]
    slab_width = full_width // (row_count * col_count)
    sectioned = amplitudes.reshape(1, 1, pair_local, row_count, col_count, slab_width)
    remapped = lax.all_to_all(
        lax.all_to_all(sectioned, "row", split_axis=3, concat_axis=0, tiled=True),
        "col",
        split_axis=4,
        concat_axis=1,
        tiled=True,
    )
    local_amps = remapped.reshape(row_count * col_count * pair_local, slab_width)
    window_size = integrals.shape[0]
    virtual_count = integrals.shape[1]
    flat_ints = integrals.reshape(window_size * virtual_count, slab_width)
    product = lax.dot_general(
        local_amps, flat_ints, (((1,), (1,)), ((), ())), preferred_element_type=jnp.float32
    )
    partial_sums = product.reshape(local_amps.shape[0], window_size, virtual_count).reshape(
        row_count, col_count, pair_local, window_size, virtual_count
    )
    reduced = lax.psum_scatter(partial_sums, "row", scatter_dimension=0, tiled=True)
    reduced = lax.psum_scatter(reduced, "col", scatter_dimension=1, tiled=True)
    return reduced.reshape(pair_local, window_size, virtual_count)


def solution(mesh):
    return jax.shard_map(
        shards,
        mesh=mesh,
        in_specs=(P(("row", "col"), None), P(None, None, ("row", "col"))),
        out_specs=P(("row", "col"), None, None),
        check_vma=False,
    )
```

profile of v0, /device:TPU:0, one launch (start us, length us, event | category | flops | bytes accessed | tf_op | source)
XLA Modules:
  0.0 250.7 jit_solution(9376902904713684544)
XLA Ops:
  6.5 0.0 all-reduce.4.cloned.1.call-start
  6.5 4.8 %reshape.19 = bf16[1280000]{0:T(1024)(128)(2,1)} reshape(bf16[2,640000]{1,0:T(2,128)(2,1)} %param.2) | data formatting | bytes 5120000
  11.3 4.3 %reshape.13 = bf16[1,1,2,16,2,20000]{5,4,3,2,1,0:T(2,128)(2,1)S(1)} reshape(bf16[1280000]{0:T(1024)(128)(2,1)} %reshape.19) | data formatting | bytes 5120000 | tf_op jit(solution)/shard_map/reshape | solution.py:13
  15.6 2.0 copy.4
  17.6 64.9 %all_to_all.33 = bf16[1,1,2,16,2,20000]{5,2,4,1,0,3:T(2,128)(2,1)S(1)} all-to-all(bf16[1,1,2,16,2,20000]{5,2,4,1,0,3:T(2,128)(2,1)S(1)} %copy.4), channel_id=1, replica_groups=mesh['row'=16,'col'=2] {'row'}, dimensions={3} | all-to-all | bytes 5120000 | tf_op jit(solution)/shard_map/all_to_all | solution.py:15
  82.5 0.3 copy.5
  82.8 33.7 %all_to_all.34 = bf16[16,1,2,1,2,20000]{5,0,2,3,1,4:T(8,128)(2,1)S(1)} all-to-all(bf16[16,1,2,1,2,20000]{5,0,2,3,1,4:T(8,128)(2,1)S(1)} %copy.5), channel_id=1, replica_groups=mesh['row'=16,'col'=2] {'col'}, dimensions={4} | all-to-all | bytes 5120000 | tf_op jit(solution)/shard_map/all_to_all | solution.py:14
  116.5 0.0 copy-start.1
  116.5 0.0 copy-start
  116.5 26.6 %fusion = f32[16,2,2,2,800]{4,0,3,2,1:T(8,128)S(1)} fusion(bf16[2,800,20000]{2,1,0:T(8,128)(2,1)} %param.3, bf16[16,1,2,1,2,20000]{5,0,2,3,1,4:T(8,128)(2,1)S(1)} %all_to_all.34), kind=kOutput, calls=%fused_computation | convolution fusion | flops 4096000000 | bytes 66969600 | tf_op jit(solution)/shard_map/dot_general | solution.py:25
  143.1 1.0 copy.6
  144.1 0.0 all-reduce.4.cloned.1.call-update
  144.1 0.0 copy-done.1
  144.2 0.6 dynamic-slice
  144.7 0.0 copy-done
  144.7 0.6 dynamic-slice.2
  145.4 87.6 %all-reduce.4.cloned.1.call-done = f32[16,2,2,2,800]{4,3,2,1,0:T(2,128)} async-done(((f32[16,2,2,2,800]{4,3,2,1,0:T(2,128)}), f32[16,2,2,2,800]{4,3,2,1,0:T(2,128)}) %all-reduce.4.cloned.1.call-update) | async-done | bytes 409616
  232.9 1.4 dynamic-slice_bitcast_fusion
  234.3 8.3 %all-reduce.1 = f32[1,2,2,2,800]{4,3,2,0,1:T(2,128)S(1)} all-reduce(f32[1,2,2,2,800]{4,3,2,0,1:T(2,128)S(1)} %dynamic-slice_bitcast_fusion), channel_id=3, replica_groups=mesh['row'=16,'col'=2] {'col'}, use_global_device_ids=true, to_apply=%region_1.0.clone | all-reduce | flops 6400 | bytes 51200
  242.6 1.2 dynamic-slice_bitcast_fusion.1
Async XLA Ops:
  6.5 226.4 %all-reduce.4.cloned.1.call-start = ((), (), s32[]{:S(2)}) async-start(), calls=%async_computation.2 | async-start | bytes 917504
  116.5 27.7 %copy-start.1 = (u32[32]{0:T(128)S(1)}, u32[32]{0:T(128)}, u32[]{:S(2)}) copy-start(u32[32]{0:T(128)} %constant.3) | copy-start | bytes 388
  116.5 28.3 %copy-start = (u32[32]{0:T(128)S(1)}, u32[32]{0:T(128)}, u32[]{:S(2)}) copy-start(u32[32]{0:T(128)} %constant.7) | copy-start | bytes 388
Sparse Core Ops, SparseCore 0:
  144.3 88.6 all-reduce.3
where the time goes:
time: 251 us
  blocking collectives  107 us (43%)
  waiting for transfers between devices  87.6 us (35%)
  matrix products  26.6 us (11%)
  local copies, waits for them, and re-layouts  16.2 us (6%)
  between operations  13.4 us (5%)
    unnamed x2, waiting for transfers between devices  87.6 us
    all_to_all x1, blocking collectives, shards(): lax.all_to_all(sectioned, 'row', split_axis=3, concat_axis=0, tiled=True)  64.9 us
    all_to_all x1, blocking collectives, shards(): lax.all_to_all(lax.all_to_all(sectioned, 'row', split_axis=3, concat_axis...  33.7 us
    dot_general x1, matrix products, shards(): lax.dot_general(local_amps, flat_ints, (((1,), (1,)), ((), ())), preferre...  26.6 us
    unnamed x1, blocking collectives  8.32 us
    reshape x2, local copies, waits for them, and re-layouts, shards(): amplitudes.reshape(1, 1, pair_local, row_count, col_count, slab_width)  6.28 us
    unnamed x7, local copies, waits for them, and re-layouts  6.01 us
  transfers between devices with their start and end apart: 1, of which 1 were waited for; matrix products, arithmetic and copies ran while one was open for 0% of the time, Pallas kernels for 0%

commit v1 on v0

v1 whole, which is shorter than its diff:
```python
import jax
import jax.numpy as jnp
from jax import lax
from jax.sharding import PartitionSpec as P

BOTH = ("row", "col")


def shards(amplitudes, integrals):
    count = lax.axis_size("row") * lax.axis_size("col")
    pair_local, full_width = amplitudes.shape
    slab = full_width // count
    window, virtuals, _ = integrals.shape
    sectioned = amplitudes.reshape(pair_local, count, slab).transpose(1, 0, 2)
    local_amps = lax.all_to_all(sectioned, BOTH, split_axis=0, concat_axis=0, tiled=True)
    local_amps = local_amps.reshape(count * pair_local, slab)
    product = lax.dot_general(
        local_amps,
        integrals.reshape(window * virtuals, slab),
        (((1,), (1,)), ((), ())),
        preferred_element_type=jnp.float32,
    )
    partial = product.reshape(count, pair_local, window * virtuals)
    parts = lax.all_to_all(partial, BOTH, split_axis=0, concat_axis=0, tiled=True)
    return parts.sum(axis=0).reshape(pair_local, window, virtuals)


def solution(mesh):
    return jax.shard_map(
        shards,
        mesh=mesh,
        in_specs=(P(BOTH, None), P(None, None, BOTH)),
        out_specs=P(BOTH, None, None),
        check_vma=False,
    )
```

time: 251 us -> 122 us (0.49)
  waiting for transfers between devices: 87.6 us -> 0 us
  blocking collectives: 107 us -> 82.7 us
  between operations: 13.4 us -> 0.03 us
  local copies, waits for them, and re-layouts: 16.2 us -> 12.6 us
    unnamed x2 -> x0, waiting for transfers between devices: 87.6 us -> none
    all_to_all x2, blocking collectives: 98.6 us -> 82.7 us  [the longest x1 66 us: shards(): lax.all_to_all(sectioned, BOTH, split_axis=0, concat_axis=0, tiled=True)]
    unnamed x1 -> x0, blocking collectives: 8.32 us -> none
    reshape x3 -> x2, local copies, waits for them, and re-layouts: 7.49 us -> 5.47 us  [the longest x1 4.77 us: shards(): sectioned = amplitudes.reshape(pair_local, count, slab).transpose(1, 0, 2)]
    unnamed x7 -> x1, local copies, waits for them, and re-layouts: 6.01 us -> 4.81 us
  transfers between devices with their start and end apart: 1 -> 0, of which waited for: 1 -> 0; matrix products, arithmetic and copies ran while one was open for 0% -> 0% of each run, Pallas kernels for 0% -> 0%
where the time goes in v1:
time: 122 us; the launch traced here: 121 us
  blocking collectives  82.7 us (68%)
  matrix products  25.9 us (21%)
  local copies, waits for them, and re-layouts  12.6 us (10%)
    all_to_all x1, blocking collectives, shards(): lax.all_to_all(sectioned, BOTH, split_axis=0, concat_axis=0, tiled=True)  66 us
    dot_general x1, matrix products, shards(): lax.dot_general(local_amps, integrals.reshape(window * virtuals, slab), (...  25.9 us
    all_to_all x1, blocking collectives, shards(): lax.all_to_all(partial, BOTH, split_axis=0, concat_axis=0, tiled=True)  16.7 us
    unnamed x1, local copies, waits for them, and re-layouts  4.81 us
    reshape x1, local copies, waits for them, and re-layouts, shards(): sectioned = amplitudes.reshape(pair_local, count, slab).transpose(1, 0, 2)  4.77 us

profile of v1, /device:TPU:0, one launch (start us, length us, event | category | flops | bytes accessed | tf_op | source)
XLA Modules:
  0.0 121.4 jit_solution(7823979756191941935)
XLA Ops:
  0.0 4.8 %reshape.17 = bf16[1280000]{0:T(1024)(128)(2,1)} reshape(bf16[2,640000]{1,0:T(2,128)(2,1)} %param.2) | data formatting | bytes 5120000
  4.8 4.8 %reshape.13 = bf16[2,32,20000]{2,1,0:T(8,128)(2,1)S(1)} reshape(bf16[1280000]{0:T(1024)(128)(2,1)} %reshape.17) | data formatting | bytes 5120000 | tf_op jit(solution)/shard_map/reshape | solution.py:14
  9.6 2.0 %copy.5 = bf16[32,2,20000]{2,1,0:T(2,128)(2,1)S(1)} copy(bf16[32,2,20000]{2,0,1:T(8,128)(2,1)S(1)} %bitcast.6) | data formatting | bytes 5120000 | tf_op jit(solution)/shard_map/transpose | solution.py:14
  11.6 66.0 %all_to_all.10 = bf16[32,2,20000]{2,1,0:T(2,128)(2,1)S(1)} all-to-all(bf16[32,2,20000]{2,1,0:T(2,128)(2,1)S(1)} %copy.5), channel_id=1, replica_groups=mesh['row'=16,'col'=2] {'row','col'}, dimensions={0} | all-to-all | bytes 5120000 | tf_op jit(solution)/shard_map/all_to_all | solution.py:15
  77.6 25.9 %fusion = f32[32,2,1600]{2,0,1:T(8,128)S(1)} fusion(bf16[1600,20000,1]{1,0,2:T(8,128)(2,1)} %bitcast.5, bf16[32,2,20000]{2,1,0:T(2,128)(2,1)S(1)} %all_to_all.10), kind=kOutput, calls=%fused_computation | convolution fusion | flops 4096000000 | bytes 66969600 | tf_op jit(solution)/shard_map/dot_general | solution.py:17
  103.5 0.3 copy.7
  103.8 16.7 %all_to_all.11 = f32[32,2,1600]{2,1,0:T(2,128)S(1)} all-to-all(f32[32,2,1600]{2,1,0:T(2,128)S(1)} %copy.7), channel_id=1, replica_groups=mesh['row'=16,'col'=2] {'row','col'}, dimensions={0} | all-to-all | bytes 819200 | tf_op jit(solution)/shard_map/all_to_all | solution.py:24
  120.6 0.1 reduce_sum.9
  120.7 0.7 reshape.15

commit v2 on v1

v2 whole, which is shorter than its diff:
```python
import jax
import jax.numpy as jnp
from jax import lax
from jax.sharding import Mesh, PartitionSpec as P

ALL = ("outer", "core", "col")
CHUNKS = 4


def shards(amplitudes, integrals):
    outer, core, col = (lax.axis_size(name) for name in ALL)
    count = outer * core * col
    pair_local, full_width = amplitudes.shape
    slab = full_width // count
    window, virtuals, _ = integrals.shape
    flat = integrals.reshape(window * virtuals, slab)
    sectioned = amplitudes.reshape(pair_local, count, slab).transpose(1, 0, 2)
    step = -(-slab // CHUNKS // 128) * 128
    product = 0
    for lo in range(0, slab, step):
        hi = min(slab, lo + step)
        part = lax.all_to_all(sectioned[:, :, lo:hi], ALL, split_axis=0, concat_axis=0, tiled=True)
        product += lax.dot_general(
            part.reshape(count * pair_local, hi - lo),
            flat[:, lo:hi],
            (((1,), (1,)), ((), ())),
            preferred_element_type=jnp.float32,
        )
    partial = product.reshape(outer, core, col * pair_local, window * virtuals)
    me = lax.axis_index("core")
    own = lax.dynamic_index_in_dim(partial, me, 1, keepdims=False)
    other = lax.dynamic_index_in_dim(partial, 1 - me, 1, keepdims=False)
    own = own + lax.ppermute(other, "core", [(0, 1), (1, 0)])
    own = own.reshape(outer * col, pair_local, window * virtuals)
    parts = lax.all_to_all(own, ("outer", "col"), split_axis=0, concat_axis=0, tiled=True)
    return parts.sum(axis=0).reshape(pair_local, window, virtuals)


def solution(mesh):
    devices = mesh.devices
    split = Mesh(devices.reshape(devices.shape[0] // 2, 2, devices.shape[1]), ALL)
    return jax.shard_map(
        shards,
        mesh=split,
        in_specs=(P(ALL, None), P(None, None, ALL)),
        out_specs=P(ALL, None, None),
        check_vma=False,
    )
```

time: 122 us -> 137 us (1.12)
  blocking collectives: 82.7 us -> 36.2 us
  waiting for transfers between devices: 0 us -> 31.5 us
  starting transfers between devices: 0 us -> 15.7 us
  matrix products: 25.9 us -> 33.6 us
  local copies, waits for them, and re-layouts: 12.6 us -> 18.9 us
    all_to_all x2, blocking collectives: 82.7 us -> 36.2 us  [the longest x1 21.2 us: shards(): lax.all_to_all(sectioned[:, :, lo:hi], ALL, split_axis=0, concat_axis=0,...]
    all_to_all x0 -> x3, waiting for transfers between devices: none -> 30.4 us  [shards(): lax.all_to_all(sectioned[:, :, lo:hi], ALL, split_axis=0, concat_axis=0,...]
    all_to_all x0 -> x3, starting transfers between devices: none -> 14.8 us  [shards(): lax.all_to_all(sectioned[:, :, lo:hi], ALL, split_axis=0, concat_axis=0,...]
    dot_general x1 -> x4, matrix products: 25.9 us -> 33.6 us  [shards(): lax.dot_general(part.reshape(count * pair_local, hi - lo), flat[:, lo:hi]...]
    reshape x1 -> x2, local copies, waits for them, and re-layouts: 4.77 us -> 8.28 us  [shards(): sectioned = amplitudes.reshape(pair_local, count, slab).transpose(1, 0, 2)]
    slice x0 -> x2, local copies, waits for them, and re-layouts: none -> 3.49 us  [shards(): sectioned[:, :, lo:hi]]
    reshape x0 -> x6, local copies, waits for them, and re-layouts: none -> 3.03 us  [the longest x4 2.75 us: shards(): part.reshape(count * pair_local, hi - lo)]
    transpose x1 -> x0, local copies, waits for them, and re-layouts: 1.98 us -> none  [shards(): sectioned = amplitudes.reshape(pair_local, count, slab).transpose(1, 0, 2)]
  transfers between devices with their start and end apart: 0 -> 4, of which waited for: 0 -> 4; matrix products, arithmetic and copies ran while one was open for 0% -> 16% of each run, Pallas kernels for 0% -> 0%
where the time goes in v2:
time: 137 us; the launch traced here: 136 us
  blocking collectives  36.2 us (26%)
  matrix products  33.6 us (25%)
  waiting for transfers between devices  31.5 us (23%)
  local copies, waits for them, and re-layouts  18.9 us (14%)
  starting transfers between devices  15.7 us (11%)
    dot_general x4, matrix products, shards(): lax.dot_general(part.reshape(count * pair_local, hi - lo), flat[:, lo:hi]...  33.6 us
    all_to_all x3, waiting for transfers between devices, shards(): lax.all_to_all(sectioned[:, :, lo:hi], ALL, split_axis=0, concat_axis=0,...  30.4 us
    all_to_all x1, blocking collectives, shards(): lax.all_to_all(sectioned[:, :, lo:hi], ALL, split_axis=0, concat_axis=0,...  21.2 us
    all_to_all x1, blocking collectives, shards(): lax.all_to_all(own, ('outer', 'col'), split_axis=0, concat_axis=0, tiled=...  15 us
    all_to_all x3, starting transfers between devices, shards(): lax.all_to_all(sectioned[:, :, lo:hi], ALL, split_axis=0, concat_axis=0,...  14.8 us
    reshape x2, local copies, waits for them, and re-layouts, shards(): sectioned = amplitudes.reshape(pair_local, count, slab).transpose(1, 0, 2)  8.28 us
    slice x2, local copies, waits for them, and re-layouts, shards(): sectioned[:, :, lo:hi]  3.49 us
    unnamed x1, local copies, waits for them, and re-layouts  3.34 us
  transfers between devices with their start and end apart: 4, of which 4 were waited for; matrix products, arithmetic and copies ran while one was open for 16% of the time, Pallas kernels for 0%

profile of v2, /device:TPU:0, one launch (start us, length us, event | category | flops | bytes accessed | tf_op | source)
XLA Modules:
  0.0 136.2 jit_solution(16496644794983105894)
XLA Ops:
  0.0 3.3 %reshape.36 = bf16[1280000]{0:T(1024)(128)(2,1)S(1)} reshape(bf16[2,640000]{1,0:T(2,128)(2,1)} %param.2) | data formatting | bytes 5120000
  3.3 4.6 %reshape.27 = bf16[2,32,20000]{2,1,0:T(8,128)(2,1)} reshape(bf16[1280000]{0:T(1024)(128)(2,1)S(1)} %reshape.36) | data formatting | bytes 5120000 | tf_op jit(solution)/shard_map/reshape | solution.py:17
  7.9 3.7 %copy.5 = bf16[2,32,20000]{2,0,1:T(2,128)(2,1)S(1)} copy(bf16[2,32,20000]{2,1,0:T(8,128)(2,1)} %reshape.27) | data formatting | bytes 5120000 | tf_op jit(solution)/shard_map/reshape | solution.py:17
  11.6 1.2 slice.38
  12.9 7.4 %all-to-all-start.3 = ((bf16[32,2,4640]{2,1,0:T(2,128)(2,1)}), bf16[32,2,4640]{2,1,0:T(2,128)(2,1)}, u32[]{:S(2)}, u32[]{:S(2)}) async-start(bf16[32,2,4640]{2,1,0:T(2,128)(2,1)} %slice.38), calls=%async_computation.3 | async-start | bytes 1212416 | tf_op jit(solution)/shard_map/all_to_all | solution.py:22
  20.3 2.2 %fusion.17 = (bf16[32,2,5120]{2,1,0:T(2,128)(2,1)}, bf16[32,2,5120]{2,1,0:T(2,128)(2,1)S(1)}, bf16[32,2,5120]{2,1,0:T(2,128)(2,1)}) fusion(bf16[32,2,20000]{2,1,0:T(2,128)(2,1)S(1)} %bitcast.13), kind=kLoop, calls=%fused_computation.14 | loop fusion | bytes 3932160 | tf_op jit(solution)/shard_map/slice | solution.py:22
  22.5 14.5 %all-to-all-done.3 = bf16[32,2,4640]{2,1,0:T(2,128)(2,1)} async-done(((bf16[32,2,4640]{2,1,0:T(2,128)(2,1)}), bf16[32,2,4640]{2,1,0:T(2,128)(2,1)}, u32[]{:S(2)}, u32[]{:S(2)}) %all-to-all-start.3) | async-done | bytes 593952 | tf_op jit(solution)/shard_map/all_to_all | solution.py:22
  37.0 21.2 %all_to_all.25 = bf16[32,2,5120]{2,1,0:T(2,128)(2,1)S(1)} all-to-all(bf16[32,2,5120]{2,1,0:T(2,128)(2,1)S(1)} %get-tuple-element.6), channel_id=1, replica_groups=mesh['outer'=8,'core'=2,'col'=2] {'outer','core','col'}, dimensions={0} | all-to-all | bytes 1310720 | tf_op jit(solution)/shard_map/all_to_all | solution.py:22
  58.3 3.6 %all-to-all-start = ((bf16[32,2,5120]{2,1,0:T(2,128)(2,1)}), bf16[32,2,5120]{2,1,0:T(2,128)(2,1)S(1)}, u32[]{:S(2)}, u32[]{:S(2)}) async-start(bf16[32,2,5120]{2,1,0:T(2,128)(2,1)} %get-tuple-element.7), calls=%async_computation | async-start | bytes 1310720 | tf_op jit(solution)/shard_map/all_to_all | solution.py:22
  61.9 2.0 %reshape.32 = bf16[64,4640]{1,0:T(8,128)(2,1)S(1)} reshape(bf16[32,2,4640]{2,1,0:T(2,128)(2,1)} %all-to-all-done.3) | data formatting | bytes 1187840 | tf_op jit(solution)/shard_map/reshape | solution.py:24
  63.9 0.2 reshape.30
  64.2 15.5 %all-to-all-done = bf16[32,2,5120]{2,1,0:T(2,128)(2,1)S(1)} async-done(((bf16[32,2,5120]{2,1,0:T(2,128)(2,1)}), bf16[32,2,5120]{2,1,0:T(2,128)(2,1)S(1)}, u32[]{:S(2)}, u32[]{:S(2)}) %all-to-all-start) | async-done | bytes 655392 | tf_op jit(solution)/shard_map/all_to_all | solution.py:22
  79.7 3.8 %all-to-all-start.2 = ((bf16[32,2,5120]{2,1,0:T(2,128)(2,1)}), bf16[32,2,5120]{2,1,0:T(2,128)(2,1)S(1)}, u32[]{:S(2)}, u32[]{:S(2)}) async-start(bf16[32,2,5120]{2,1,0:T(2,128)(2,1)} %get-tuple-element.5), calls=%async_computation.2 | async-start | bytes 1310720 | tf_op jit(solution)/shard_map/all_to_all | solution.py:22
  83.5 8.5 %fusion.2 = f32[64,1600]{1,0:T(8,128)S(1)} fusion(bf16[64,5120]{1,0:T(8,128)(2,1)S(1)} %reshape.30, bf16[1600,20000]{1,0:T(8,128)(2,1)} %bitcast.14), kind=kOutput, calls=%fused_computation.2 | convolution fusion | flops 1048576000 | bytes 17448960 | tf_op jit(solution)/shard_map/dot_general | solution.py:23
  92.0 0.2 reshape.28
  92.3 8.5 %fusion.11 = f32[64,1600]{1,0:T(8,128)S(1)} fusion(f32[64,1600]{1,0:T(8,128)S(1)} %fusion.2, bf16[64,5120]{1,0:T(8,128)(2,1)S(1)} %reshape.28, bf16[1600,20000]{1,0:T(8,128)(2,1)} %bitcast.15), kind=kOutput, calls=%fused_computation.10 | convolution fusion | flops 1048678400 | bytes 17858560 | tf_op jit(solution)/shard_map/dot_general | solution.py:23
  100.8 0.4 all-to-all-done.2
  101.1 0.2 reshape.31
  101.4 8.5 %fusion.14 = f32[64,1600]{1,0:T(8,128)S(1)} fusion(f32[64,1600]{1,0:T(8,128)S(1)} %fusion.11, bf16[64,5120]{1,0:T(8,128)(2,1)S(1)} %reshape.31, bf16[1600,20000]{1,0:T(8,128)(2,1)} %bitcast.16), kind=kOutput, calls=%fused_computation.11 | convolution fusion | flops 1048678400 | bytes 17858560 | tf_op jit(solution)/shard_map/dot_general | solution.py:23
  109.9 8.1 %fusion.8 = f32[64,1600]{1,0:T(8,128)S(1)} fusion(f32[64,1600]{1,0:T(8,128)S(1)} %fusion.14, bf16[64,4640]{1,0:T(8,128)(2,1)S(1)} %reshape.32, bf16[1600,20000]{1,0:T(8,128)(2,1)} %bitcast.17), kind=kOutput, calls=%fused_computation.9 | convolution fusion | flops 950374400 | bytes 16568320 | tf_op jit(solution)/shard_map/dot_general | solution.py:23
  118.1 0.1 reshape.33
  118.2 0.9 collective-permute-start
  119.1 1.1 collective-permute-done
  120.2 0.1 bitcast_add_fusion
  120.3 0.2 reshape.34
  120.4 15.0 %all_to_all.26 = f32[16,2,1600]{2,1,0:T(2,128)S(1)} all-to-all(f32[16,2,1600]{2,1,0:T(2,128)S(1)} %reshape.34), channel_id=1, replica_groups=mesh['outer'=8,'core'=2,'col'=2] {'outer','col'}, dimensions={0} | all-to-all | bytes 409600 | tf_op jit(solution)/shard_map/all_to_all | solution.py:35
  135.4 0.1 reduce_sum.9
  135.5 0.7 reshape.35
  (1 shorter events, 0.0 us)
Async XLA Ops:
  12.9 24.2 %all-to-all-start.3 = ((bf16[32,2,4640]{2,1,0:T(2,128)(2,1)}), bf16[32,2,4640]{2,1,0:T(2,128)(2,1)}, u32[]{:S(2)}, u32[]{:S(2)}) async-start(bf16[32,2,4640]{2,1,0:T(2,128)(2,1)} %slice.38), calls=%async_computation.3 | async-start | bytes 1212416 | tf_op jit(solution)/shard_map/all_to_all | solution.py:22
  58.3 21.4 %all-to-all-start = ((bf16[32,2,5120]{2,1,0:T(2,128)(2,1)}), bf16[32,2,5120]{2,1,0:T(2,128)(2,1)S(1)}, u32[]{:S(2)}, u32[]{:S(2)}) async-start(bf16[32,2,5120]{2,1,0:T(2,128)(2,1)} %get-tuple-element.7), calls=%async_computation | async-start | bytes 1310720 | tf_op jit(solution)/shard_map/all_to_all | solution.py:22
  79.7 21.4 %all-to-all-start.2 = ((bf16[32,2,5120]{2,1,0:T(2,128)(2,1)}), bf16[32,2,5120]{2,1,0:T(2,128)(2,1)S(1)}, u32[]{:S(2)}, u32[]{:S(2)}) async-start(bf16[32,2,5120]{2,1,0:T(2,128)(2,1)} %get-tuple-element.5), calls=%async_computation.2 | async-start | bytes 1310720 | tf_op jit(solution)/shard_map/all_to_all | solution.py:22
  118.2 2.0 %collective-permute-start = (f32[8,4,1600]{2,1,0:T(4,128)S(1)}, f32[8,4,1600]{2,1,0:T(4,128)S(1)}, u32[]{:S(2)}, u32[]{:S(2)}) collective-permute-start(f32[8,4,1600]{2,1,0:T(4,128)S(1)} %dynamic-slice_bitcast_fusion), channel_id=1, source_target_pairs={{0,2},{2,0},{1,3},{3,1},{4,6},{6,4},{5,7},{7,5},{8,10},{10,8},{9,1... | collective-permute-start | bytes 614408 | tf_op jit(solution)/shard_map/ppermute | solution.py:33

commit v3 on v1

v3 whole, which is shorter than its diff:
```python
import functools

import jax
import jax.numpy as jnp
from jax import lax
from jax.experimental import pallas as pl
from jax.experimental.pallas import tpu as pltpu
from jax.sharding import Mesh, PartitionSpec as P

ALL = ("z", "x", "core", "col")
LANES = 128
BLOCK = 1024
FIRST = 0.7


def window_kernel(starts, width, x_ref, o_ref, sems):
    total = x_ref.shape[1]
    copies = []
    for index, start in enumerate(starts):
        size = min(width, total - start)
        copies.append(
            pltpu.make_async_copy(
                x_ref.at[:, pl.ds(start, size)],
                o_ref.at[index, :, pl.ds(0, size)],
                sems.at[index],
            )
        )
    for copy in copies:
        copy.start()
    for copy in copies:
        copy.wait()


def windows(x, starts, width):
    return pl.pallas_call(
        functools.partial(window_kernel, starts, width),
        out_shape=jax.ShapeDtypeStruct((len(starts), x.shape[0], width), x.dtype),
        in_specs=[pl.BlockSpec(memory_space=pl.ANY)],
        out_specs=pl.BlockSpec(memory_space=pl.ANY),
        scratch_shapes=[pltpu.SemaphoreType.DMA((len(starts),))],
        cost_estimate=pl.CostEstimate(
            flops=0, bytes_accessed=4 * len(starts) * x.shape[0] * width, transcendentals=0
        ),
        name="windows",
    )(x)


def product_kernel(steps, tail_width, has_sum, off_ref, amps_ref, ints_ref, *rest):
    sum_ref = rest[0] if has_sum else None
    out_ref, acc_ref = rest[-2:]
    step = pl.program_id(0)
    off = off_ref[0]
    back = off_ref[1]
    pairs = amps_ref.shape[0]
    lane = lax.broadcasted_iota(jnp.int32, (pairs, LANES), 1)
    from_here = lane < LANES - off

    @pl.when(step == 0)
    def _():
        acc_ref[...] = jnp.zeros_like(acc_ref)

    def tiles(base, count, limit):
        rolled = []
        for t in range(min(count + 1, limit)):
            tile = amps_ref[:, pl.ds(pl.multiple_of(base + t * LANES, LANES), LANES)]
            rolled.append(pltpu.roll(tile.astype(jnp.float32), back, 1))
        return [
            jnp.where(from_here, rolled[t], rolled[min(t + 1, len(rolled) - 1)])
            for t in range(count)
        ]

    def dot(ints, amps):
        return lax.dot_general(
            ints, amps, (((1,), (1,)), ((), ())), preferred_element_type=jnp.float32
        )

    def full():
        parts = tiles(step * BLOCK, BLOCK // LANES, BLOCK // LANES + 1)
        amps = jnp.concatenate([p.astype(jnp.bfloat16) for p in parts], axis=1)
        acc_ref[...] += dot(ints_ref[...], amps)

    def tail():
        count = -(-tail_width // LANES)
        base = (steps - 1) * BLOCK
        parts = tiles(base, count, (amps_ref.shape[1] - base) // LANES)
        whole = tail_width // LANES
        if whole:
            amps = jnp.concatenate([p.astype(jnp.bfloat16) for p in parts[:whole]], axis=1)
            acc_ref[...] += dot(ints_ref[:, : whole * LANES], amps)
        if whole < count:
            valid = tail_width - whole * LANES
            amps = jnp.where(lane < valid, parts[whole], 0.0).astype(jnp.bfloat16)
            ints = ints_ref[:, whole * LANES : count * LANES]
            place = lax.broadcasted_iota(jnp.int32, ints.shape, 1)
            ints = jnp.where(place < valid, ints, jnp.zeros_like(ints))
            acc_ref[...] += dot(ints, amps)

    if tail_width == BLOCK:
        full()
    else:
        if steps > 1:
            pl.when(step < steps - 1)(full)
        pl.when(step == steps - 1)(tail)

    @pl.when(step == steps - 1)
    def _():
        result = acc_ref[...].T
        out_ref[...] = result + sum_ref[...] if has_sum else result


def product(shift, amps, flat, low, high, total):
    pairs = amps.shape[0]
    rows = flat.shape[0]
    width = high - low
    steps = -(-width // BLOCK)
    first = low // BLOCK
    whole = pl.BlockSpec((pairs, rows), lambda j: (0, 0))
    sums = [] if total is None else [total]
    return pl.pallas_call(
        functools.partial(product_kernel, steps, width - (steps - 1) * BLOCK, bool(sums)),
        out_shape=jax.ShapeDtypeStruct((pairs, rows), jnp.float32),
        grid=(steps,),
        in_specs=[
            pl.BlockSpec(memory_space=pltpu.SMEM),
            pl.BlockSpec(amps.shape, lambda j: (0, 0)),
            pl.BlockSpec((rows, BLOCK), lambda j: (0, first + j)),
        ]
        + [whole] * len(sums),
        out_specs=whole,
        scratch_shapes=[pltpu.VMEM((rows, pairs), jnp.float32)],
        compiler_params=pltpu.CompilerParams(vmem_limit_bytes=32 * 1024 * 1024),
        cost_estimate=pl.CostEstimate(
            flops=2 * pairs * rows * width, bytes_accessed=2 * rows * width, transcendentals=0
        ),
        name="product",
    )(shift, amps, flat, *sums)


def exchange_sum(blocks, names):
    count = blocks.shape[0]
    me = lax.axis_index(names)
    terms = [lax.dynamic_index_in_dim(blocks, me, 0, keepdims=False)]
    power = count & (count - 1) == 0
    for step in range(count - 1, 0, -1):
        to = (lambda i: i ^ step) if power else (lambda i: (i + step) % count)
        block = lax.dynamic_index_in_dim(blocks, to(me), 0, keepdims=False)
        terms.append(lax.ppermute(block, names, [(i, to(i)) for i in range(count)]))
    return sum(terms[1:], terms[0])


def shards(amplitudes, integrals):
    z, x, core, col = (lax.axis_size(name) for name in ALL)
    count = z * x * core * col
    pair_local, full_width = amplitudes.shape
    slab = full_width // count
    window, virtuals, _ = integrals.shape
    rows = window * virtuals
    flat = integrals.reshape(rows, slab)

    begins = [d * slab // LANES * LANES for d in range(count)]
    most = max(1, max(d * slab - begins[d] for d in range(count)))
    off = lax.rem(lax.axis_index(ALL) * slab, LANES)
    shift = jnp.stack([off, lax.rem(LANES - off, LANES)]).astype(jnp.int32)

    blocks = -(-slab // BLOCK)
    cut = max(1, min(blocks - 1, round(FIRST * blocks))) * BLOCK
    total = None
    for low, high in ((0, cut), (cut, slab)):
        width = -(-(most + high - low) // LANES) * LANES
        sent = windows(amplitudes, [b + low for b in begins], width)
        got = lax.all_to_all(sent, ALL, split_axis=0, concat_axis=0, tiled=True)
        got = got.reshape(count * pair_local, width)
        total = product(shift, got, flat, low, high, total)

    part = total.reshape(z, x, core, col, pair_local, rows)
    part = exchange_sum(part.transpose(2, 0, 1, 3, 4, 5).reshape(core, z, x * col, pair_local, rows), "core")
    part = exchange_sum(part.transpose(1, 0, 2, 3), ("x", "col"))
    part = exchange_sum(part, "z")
    return part.reshape(pair_local, window, virtuals)


def solution(mesh):
    devices = mesh.devices
    row, col = devices.shape
    split = Mesh(devices.reshape(row // 4, 2, 2, col), ALL)
    return jax.shard_map(
        shards,
        mesh=split,
        in_specs=(P(ALL, None), P(None, None, ALL)),
        out_specs=P(ALL, None, None),
        check_vma=False,
    )
```

time: 122 us -> 193 us (1.58)
  Pallas kernels: 0 us -> 115 us
  blocking collectives: 82.7 us -> 0 us
  waiting for transfers between devices: 0 us -> 49.9 us
  matrix products: 25.9 us -> 0 us
  starting transfers between devices: 0 us -> 21.3 us
  local copies, waits for them, and re-layouts: 12.6 us -> 5.24 us
    pallas_call x0 -> x4, Pallas kernels: none -> 115 us  [the longest x2 81.2 us: windows(): pl.pallas_call(functools.partial(window_kernel, starts, width), out_shape...]
    all_to_all x2 -> x0, blocking collectives: 82.7 us -> none  [the longest x1 66 us: shards(): lax.all_to_all(sectioned, BOTH, split_axis=0, concat_axis=0, tiled=True)]
    all_to_all x0 -> x2, waiting for transfers between devices: none -> 43.1 us  [shards(): got = lax.all_to_all(sent, ALL, split_axis=0, concat_axis=0, tiled=True)]
    dot_general x1 -> x0, matrix products: 25.9 us -> none  [shards(): lax.dot_general(local_amps, integrals.reshape(window * virtuals, slab), (...]
    all_to_all x0 -> x2, starting transfers between devices: none -> 13.3 us  [shards(): got = lax.all_to_all(sent, ALL, split_axis=0, concat_axis=0, tiled=True)]
    ppermute x0 -> x7, starting transfers between devices: none -> 8.08 us  [exchange_sum(): terms.append(lax.ppermute(block, names, [(i, to(i)) for i in range(count)]))]
    ppermute x0 -> x7, waiting for transfers between devices: none -> 6.86 us  [exchange_sum(): terms.append(lax.ppermute(block, names, [(i, to(i)) for i in range(count)]))]
    unnamed x1 -> x0, local copies, waits for them, and re-layouts: 4.81 us -> none
  transfers between devices with their start and end apart: 0 -> 9, of which waited for: 0 -> 8; matrix products, arithmetic and copies ran while one was open for 0% -> 0% of each run, Pallas kernels for 0% -> 30%
where the time goes in v3:
time: 193 us; the launch traced here: 192 us
  Pallas kernels  115 us (60%)
  waiting for transfers between devices  49.9 us (26%)
  starting transfers between devices  21.3 us (11%)
  local copies, waits for them, and re-layouts  5.24 us (3%)
    pallas_call x2, Pallas kernels, windows(): pl.pallas_call(functools.partial(window_kernel, starts, width), out_shape...  81.2 us
    all_to_all x2, waiting for transfers between devices, shards(): got = lax.all_to_all(sent, ALL, split_axis=0, concat_axis=0, tiled=True)  43.1 us
    pallas_call x2, Pallas kernels, product(): pl.pallas_call(functools.partial(product_kernel, steps, width - (steps -...  33.8 us
    all_to_all x2, starting transfers between devices, shards(): got = lax.all_to_all(sent, ALL, split_axis=0, concat_axis=0, tiled=True)  13.3 us
    ppermute x7, starting transfers between devices, exchange_sum(): terms.append(lax.ppermute(block, names, [(i, to(i)) for i in range(count)]))  8.08 us
    ppermute x7, waiting for transfers between devices, exchange_sum(): terms.append(lax.ppermute(block, names, [(i, to(i)) for i in range(count)]))  6.86 us
    reshape x2, local copies, waits for them, and re-layouts, shards(): got = got.reshape(count * pair_local, width)  4.19 us
  transfers between devices with their start and end apart: 9, of which 8 were waited for; matrix products, arithmetic and copies ran while one was open for 0% of the time, Pallas kernels for 30%

profile of v3, /device:TPU:0, one launch (start us, length us, event | category | flops | bytes accessed | tf_op | source)
XLA Modules:
  0.0 191.9 jit_solution(12568746965157658328)
XLA Ops:
  0.0 23.7 %windows.2 = bf16[32,2,5760]{2,1,0:T(2,128)(2,1)} custom-call(bf16[2,640000]{1,0:T(2,128)(2,1)} %x_ref.3), custom_call_target="tpu_custom_call" | custom-call | bytes 1474560 | tf_op jit(solution)/shard_map/windows/pallas_call | solution.py:35
  23.7 7.3 %all-to-all-start = ((bf16[32,2,5760]{2,1,0:T(2,128)(2,1)}), bf16[32,2,5760]{2,1,0:T(2,128)(2,1)S(1)}, u32[]{:S(2)}, u32[]{:S(2)}) async-start(bf16[32,2,5760]{2,1,0:T(2,128)(2,1)} %windows.2), calls=%async_computation | async-start | bytes 1474560 | tf_op jit(solution)/shard_map/all_to_all | solution.py:171
  31.1 57.5 %windows.3 = bf16[32,2,14464]{2,1,0:T(2,128)(2,1)} custom-call(bf16[2,640000]{1,0:T(2,128)(2,1)} %x_ref.3), custom_call_target="tpu_custom_call" | custom-call | bytes 3702784 | tf_op jit(solution)/shard_map/windows/pallas_call | solution.py:35
  88.5 0.0 all-to-all-done
  88.5 6.0 %all-to-all-start.1 = ((bf16[32,2,14464]{2,1,0:T(2,128)(2,1)}), bf16[32,2,14464]{2,1,0:T(2,128)(2,1)}, u32[]{:S(2)}, u32[]{:S(2)}) async-start(bf16[32,2,14464]{2,1,0:T(2,128)(2,1)} %windows.3), calls=%async_computation.1 | async-start | bytes 3702784 | tf_op jit(solution)/shard_map/all_to_all | solution.py:171
  94.5 0.1 pad_add_fusion.off_ref
  94.6 0.3 reshape.26.amps_ref
  94.9 43.1 %all-to-all-done.1 = bf16[32,2,14464]{2,1,0:T(2,128)(2,1)} async-done(((bf16[32,2,14464]{2,1,0:T(2,128)(2,1)}), bf16[32,2,14464]{2,1,0:T(2,128)(2,1)}, u32[]{:S(2)}, u32[]{:S(2)}) %all-to-all-start.1) | async-done | bytes 1851424 | tf_op jit(solution)/shard_map/all_to_all | solution.py:171
  137.9 3.9 %reshape.28.amps_ref = bf16[64,14464]{1,0:T(8,128)(2,1)S(1)} reshape(bf16[32,2,14464]{2,1,0:T(2,128)(2,1)} %all-to-all-done.1) | data formatting | bytes 3702784 | tf_op jit(solution)/shard_map/reshape | solution.py:172
  141.9 23.6 %product.2.rest_0_ = f32[64,1600]{1,0:T(8,128)S(1)} custom-call(s32[2]{0:T(128)S(1)} %pad_add_fusion.off_ref, bf16[64,14464]{1,0:T(8,128)(2,1)S(1)} %reshape.28.amps_ref, bf16[1600,20000]{1,0:T(8,128)(2,1)} %bitcast.34), custom_call_target="tpu_custom_call" | custom-call | flops 2936012800 | bytes 45875200 | tf_op jit(solution)/shard_map/product/pallas_call | solution.py:119
  165.4 10.2 %product.3 = f32[64,1600]{1,0:T(8,128)S(1)} custom-call(s32[2]{0:T(128)S(1)} %pad_add_fusion.off_ref, bf16[64,5760]{1,0:T(8,128)(2,1)S(1)} %reshape.26.amps_ref, bf16[1600,20000]{1,0:T(8,128)(2,1)} %bitcast.35, f32[64,1600]{1,0:T(8,128)S(1)} %product.2.rest_0_), custom_call_target="tpu_custom_call" | custom-call | flops 1159987200 | bytes 18124800 | tf_op jit(solution)/shard_map/product/pallas_call | solution.py:119
  175.6 0.2 reshape.29
  176.0 0.1 collective-permute-start
  176.1 1.4 collective-permute-done
  177.5 0.1 bitcast_add_fusion
  177.7 2.5 %collective-permute-start.1 = (f32[4,2,1600]{2,1,0:T(2,128)S(1)}, f32[4,2,1600]{2,1,0:T(2,128)S(1)}, u32[]{:S(2)}, u32[]{:S(2)}) collective-permute-start(f32[4,2,1600]{2,1,0:T(2,128)S(1)} %get-tuple-element.5), channel_id=1, source_target_pairs={{0,5},{1,4},{4,1},{5,0},{2,7},{3,6},{6,3},{7,2},{8,13},{9,12},{12,... | collective-permute-start | bytes 153608 | tf_op jit(solution)/shard_map/ppermute | solution.py:147
  180.2 0.6 collective-permute-start.2
  180.7 0.5 collective-permute-start.3
  181.2 1.8 collective-permute-done.1
  183.0 1.3 collective-permute-done.2
  184.3 0.6 collective-permute-done.3
  184.9 1.5 collective-permute-start.4
  186.4 0.7 collective-permute-start.5
  187.2 2.2 %collective-permute-start.6 = (f32[2,1600]{1,0:T(2,128)S(1)}, f32[2,1600]{1,0:T(2,128)S(1)}, u32[]{:S(2)}, u32[]{:S(2)}) collective-permute-start(f32[2,1600]{1,0:T(2,128)S(1)} %get-tuple-element.9), channel_id=1, source_target_pairs={{0,8},{8,0},{16,24},{24,16},{1,9},{9,1},{17,25},{25,17},{2,10},{10... | collective-permute-start | bytes 38408 | tf_op jit(solution)/shard_map/ppermute | solution.py:147
  189.4 1.1 collective-permute-done.4
  190.5 0.5 collective-permute-done.5
  191.0 0.1 collective-permute-done.6
  191.2 0.7 reshape.31
  (6 shorter events, 0.2 us)
Async XLA Ops:
  23.7 64.8 %all-to-all-start = ((bf16[32,2,5760]{2,1,0:T(2,128)(2,1)}), bf16[32,2,5760]{2,1,0:T(2,128)(2,1)S(1)}, u32[]{:S(2)}, u32[]{:S(2)}) async-start(bf16[32,2,5760]{2,1,0:T(2,128)(2,1)} %windows.2), calls=%async_computation | async-start | bytes 1474560 | tf_op jit(solution)/shard_map/all_to_all | solution.py:171
  88.5 49.4 %all-to-all-start.1 = ((bf16[32,2,14464]{2,1,0:T(2,128)(2,1)}), bf16[32,2,14464]{2,1,0:T(2,128)(2,1)}, u32[]{:S(2)}, u32[]{:S(2)}) async-start(bf16[32,2,14464]{2,1,0:T(2,128)(2,1)} %windows.3), calls=%async_computation.1 | async-start | bytes 3702784 | tf_op jit(solution)/shard_map/all_to_all | solution.py:171
  176.0 1.5 collective-permute-start
  177.7 5.3 %collective-permute-start.1 = (f32[4,2,1600]{2,1,0:T(2,128)S(1)}, f32[4,2,1600]{2,1,0:T(2,128)S(1)}, u32[]{:S(2)}, u32[]{:S(2)}) collective-permute-start(f32[4,2,1600]{2,1,0:T(2,128)S(1)} %get-tuple-element.5), channel_id=1, source_target_pairs={{0,5},{1,4},{4,1},{5,0},{2,7},{3,6},{6,3},{7,2},{8,13},{9,12},{12,... | collective-permute-start | bytes 153608 | tf_op jit(solution)/shard_map/ppermute | solution.py:147
  180.2 4.1 %collective-permute-start.2 = (f32[4,2,1600]{2,1,0:T(2,128)S(1)}, f32[4,2,1600]{2,1,0:T(2,128)S(1)}, u32[]{:S(2)}, u32[]{:S(2)}) collective-permute-start(f32[4,2,1600]{2,1,0:T(2,128)S(1)} %get-tuple-element.7), channel_id=1, source_target_pairs={{0,4},{1,5},{4,0},{5,1},{2,6},{3,7},{6,2},{7,3},{8,12},{9,13},{12,... | collective-permute-start | bytes 153608 | tf_op jit(solution)/shard_map/ppermute | solution.py:147
  180.7 4.1 %collective-permute-start.3 = (f32[4,2,1600]{2,1,0:T(2,128)S(1)}, f32[4,2,1600]{2,1,0:T(2,128)S(1)}, u32[]{:S(2)}, u32[]{:S(2)}) collective-permute-start(f32[4,2,1600]{2,1,0:T(2,128)S(1)} %get-tuple-element.6), channel_id=1, source_target_pairs={{0,1},{1,0},{4,5},{5,4},{2,3},{3,2},{6,7},{7,6},{8,9},{9,8},{12,13... | collective-permute-start | bytes 153608 | tf_op jit(solution)/shard_map/ppermute | solution.py:147
  184.9 5.6 %collective-permute-start.4 = (f32[2,1600]{1,0:T(2,128)S(1)}, f32[2,1600]{1,0:T(2,128)S(1)}, u32[]{:S(2)}, u32[]{:S(2)}) collective-permute-start(f32[2,1600]{1,0:T(2,128)S(1)} %get-tuple-element.8), channel_id=1, source_target_pairs={{0,24},{8,16},{16,8},{24,0},{1,25},{9,17},{17,9},{25,1},{2,26},{10... | collective-permute-start | bytes 38408 | tf_op jit(solution)/shard_map/ppermute | solution.py:147
  186.4 4.6 %collective-permute-start.5 = (f32[2,1600]{1,0:T(2,128)S(1)}, f32[2,1600]{1,0:T(2,128)S(1)}, u32[]{:S(2)}, u32[]{:S(2)}) collective-permute-start(f32[2,1600]{1,0:T(2,128)S(1)} %get-tuple-element.10), channel_id=1, source_target_pairs={{0,16},{8,24},{16,0},{24,8},{1,17},{9,25},{17,1},{25,9},{2,18},{10... | collective-permute-start | bytes 38408 | tf_op jit(solution)/shard_map/ppermute | solution.py:147
  187.2 4.0 %collective-permute-start.6 = (f32[2,1600]{1,0:T(2,128)S(1)}, f32[2,1600]{1,0:T(2,128)S(1)}, u32[]{:S(2)}, u32[]{:S(2)}) collective-permute-start(f32[2,1600]{1,0:T(2,128)S(1)} %get-tuple-element.9), channel_id=1, source_target_pairs={{0,8},{8,0},{16,24},{24,16},{1,9},{9,1},{17,25},{25,17},{2,10},{10... | collective-permute-start | bytes 38408 | tf_op jit(solution)/shard_map/ppermute | solution.py:147

commit v4 on v3

--- a/solution.py
+++ b/solution.py
@@ -9,35 +9,24 @@
 
 ALL = ("z", "x", "core", "col")
 LANES = 128
-BLOCK = 1024
+BLOCK = 2560
 FIRST = 0.7
 
 
-def window_kernel(starts, width, x_ref, o_ref, sems):
-    total = x_ref.shape[1]
-    copies = []
+def window_kernel(starts, x_ref, o_ref):
+    width = o_ref.shape[2]
     for index, start in enumerate(starts):
-        size = min(width, total - start)
-        copies.append(
-            pltpu.make_async_copy(
-                x_ref.at[:, pl.ds(start, size)],
-                o_ref.at[index, :, pl.ds(0, size)],
-                sems.at[index],
-            )
-        )
-    for copy in copies:
-        copy.start()
-    for copy in copies:
-        copy.wait()
+        size = min(width, x_ref.shape[1] - start)
+        o_ref[index, :, pl.ds(0, size)] = x_ref[:, pl.ds(start, size)]
 
 
 def windows(x, starts, width):
     return pl.pallas_call(
-        functools.partial(window_kernel, starts, width),
+        functools.partial(window_kernel, starts),
         out_shape=jax.ShapeDtypeStruct((len(starts), x.shape[0], width), x.dtype),
-        in_specs=[pl.BlockSpec(memory_space=pl.ANY)],
-        out_specs=pl.BlockSpec(memory_space=pl.ANY),
-        scratch_shapes=[pltpu.SemaphoreType.DMA((len(starts),))],
+        in_specs=[pl.BlockSpec(memory_space=pltpu.VMEM)],
+        out_specs=pl.BlockSpec(memory_space=pltpu.VMEM),
+        compiler_params=pltpu.CompilerParams(vmem_limit_bytes=16 * 1024 * 1024),
         cost_estimate=pl.CostEstimate(
             flops=0, bytes_accessed=4 * len(starts) * x.shape[0] * width, transcendentals=0
         ),
@@ -128,7 +117,7 @@
         + [whole] * len(sums),
         out_specs=whole,
         scratch_shapes=[pltpu.VMEM((rows, pairs), jnp.float32)],
-        compiler_params=pltpu.CompilerParams(vmem_limit_bytes=32 * 1024 * 1024),
+        compiler_params=pltpu.CompilerParams(vmem_limit_bytes=36 * 1024 * 1024),
         cost_estimate=pl.CostEstimate(
             flops=2 * pairs * rows * width, bytes_accessed=2 * rows * width, transcendentals=0
         ),
@@ -136,16 +125,19 @@
     )(shift, amps, flat, *sums)
 
 
-def exchange_sum(blocks, names):
+def exchange_sum(blocks, name):
     count = blocks.shape[0]
-    me = lax.axis_index(names)
-    terms = [lax.dynamic_index_in_dim(blocks, me, 0, keepdims=False)]
-    power = count & (count - 1) == 0
-    for step in range(count - 1, 0, -1):
-        to = (lambda i: i ^ step) if power else (lambda i: (i + step) % count)
-        block = lax.dynamic_index_in_dim(blocks, to(me), 0, keepdims=False)
-        terms.append(lax.ppermute(block, names, [(i, to(i)) for i in range(count)]))
-    return sum(terms[1:], terms[0])
+    me = lax.axis_index(name)
+    if count & (count - 1):
+        return lax.psum_scatter(blocks, name, scatter_dimension=0, tiled=False)
+    while blocks.shape[0] > 1:
+        half = blocks.shape[0] // 2
+        halves = blocks.reshape(2, half, *blocks.shape[1:])
+        mine = (me // half) % 2
+        there = lax.dynamic_index_in_dim(halves, 1 - mine, 0, keepdims=False)
+        here = lax.dynamic_index_in_dim(halves, mine, 0, keepdims=False)
+        blocks = here + lax.ppermute(there, name, [(i, i ^ half) for i in range(count)])
+    return blocks[0]
 
 
 def shards(amplitudes, integrals):
@@ -164,17 +156,23 @@
 
     blocks = -(-slab // BLOCK)
     cut = max(1, min(blocks - 1, round(FIRST * blocks))) * BLOCK
+    parts = [(0, cut), (cut, slab)] if cut < slab else [(0, slab)]
+    widths = [-(-(most + high - low) // LANES) * LANES for low, high in parts]
+    sent = [windows(amplitudes, [b + low for b in begins], w) for (low, _), w in zip(parts, widths)]
+    got = []
+    for block in sent:
+        if got:
+            block, got[-1] = lax.optimization_barrier((block, got[-1]))
+        got.append(lax.all_to_all(block, ALL, split_axis=0, concat_axis=0, tiled=True))
     total = None
-    for low, high in ((0, cut), (cut, slab)):
-        width = -(-(most + high - low) // LANES) * LANES
-        sent = windows(amplitudes, [b + low for b in begins], width)
-        got = lax.all_to_all(sent, ALL, split_axis=0, concat_axis=0, tiled=True)
-        got = got.reshape(count * pair_local, width)
-        total = product(shift, got, flat, low, high, total)
+    for (low, high), width, block in zip(parts, widths, got):
+        amps = block.reshape(count * pair_local, width)
+        total = product(shift, amps, flat, low, high, total)
 
     part = total.reshape(z, x, core, col, pair_local, rows)
-    part = exchange_sum(part.transpose(2, 0, 1, 3, 4, 5).reshape(core, z, x * col, pair_local, rows), "core")
-    part = exchange_sum(part.transpose(1, 0, 2, 3), ("x", "col"))
+    part = exchange_sum(part.transpose(2, 1, 3, 0, 4, 5), "core")
+    part = exchange_sum(part, "x")
+    part = exchange_sum(part, "col")
     part = exchange_sum(part, "z")
     return part.reshape(pair_local, window, virtuals)
 

time: 193 us -> 115 us (0.60)
  Pallas kernels: 115 us -> 29.4 us
  waiting for transfers between devices: 49.9 us -> 56.6 us
  local copies, waits for them, and re-layouts: 5.24 us -> 8.36 us
  starting transfers between devices: 21.3 us -> 19.3 us
    pallas_call x2, Pallas kernels: 81.2 us -> 1 us  [windows(): pl.pallas_call(functools.partial(window_kernel, starts), out_shape=jax.Sh...]
    pallas_call x2, Pallas kernels: 33.8 us -> 28.4 us  [product(): pl.pallas_call(functools.partial(product_kernel, steps, width - (steps -...]
    ppermute x7 -> x5, waiting for transfers between devices: 6.86 us -> 11.3 us  [exchange_sum(): lax.ppermute(there, name, [(i, i ^ half) for i in range(count)])]
    unnamed x0 -> x6, local copies, waits for them, and re-layouts: none -> 2.98 us
    all_to_all x2, waiting for transfers between devices: 43.1 us -> 45.4 us  [shards(): lax.all_to_all(block, ALL, split_axis=0, concat_axis=0, tiled=True)]
    all_to_all x2, starting transfers between devices: 13.3 us -> 11.1 us  [shards(): lax.all_to_all(block, ALL, split_axis=0, concat_axis=0, tiled=True)]
    reshape x3 -> x2, local copies, waits for them, and re-layouts: 4.88 us -> 4.35 us  [shards(): amps = block.reshape(count * pair_local, width)]
    ppermute x7 -> x5, starting transfers between devices: 8.08 us -> 8.25 us  [exchange_sum(): lax.ppermute(there, name, [(i, i ^ half) for i in range(count)])]
  transfers between devices with their start and end apart: 9 -> 7, of which waited for: 8 -> 6; matrix products, arithmetic and copies ran while one was open for 0% -> 4% of each run, Pallas kernels for 30% -> 19%
where the time goes in v4:
time: 115 us; the launch traced here: 114 us
  waiting for transfers between devices  56.6 us (49%)
  Pallas kernels  29.4 us (26%)
  starting transfers between devices  19.3 us (17%)
  local copies, waits for them, and re-layouts  8.36 us (7%)
    all_to_all x2, waiting for transfers between devices, shards(): lax.all_to_all(block, ALL, split_axis=0, concat_axis=0, tiled=True)  45.4 us
    pallas_call x2, Pallas kernels, product(): pl.pallas_call(functools.partial(product_kernel, steps, width - (steps -...  28.4 us
    ppermute x5, waiting for transfers between devices, exchange_sum(): lax.ppermute(there, name, [(i, i ^ half) for i in range(count)])  11.3 us
    all_to_all x2, starting transfers between devices, shards(): lax.all_to_all(block, ALL, split_axis=0, concat_axis=0, tiled=True)  11.1 us
    ppermute x5, starting transfers between devices, exchange_sum(): lax.ppermute(there, name, [(i, i ^ half) for i in range(count)])  8.25 us
    reshape x2, local copies, waits for them, and re-layouts, shards(): amps = block.reshape(count * pair_local, width)  4.35 us
    unnamed x6, local copies, waits for them, and re-layouts  2.98 us
  transfers between devices with their start and end apart: 7, of which 6 were waited for; matrix products, arithmetic and copies ran while one was open for 4% of the time, Pallas kernels for 19%

profile of v4, /device:TPU:0, one launch (start us, length us, event | category | flops | bytes accessed | tf_op | source)
XLA Modules:
  0.0 114.2 jit_solution(1382530963374227246)
XLA Ops:
  0.0 0.0 copy-start
  0.0 1.7 %copy-done = bf16[2,640000]{1,0:T(2,128)(2,1)S(1)} copy-done((bf16[2,640000]{1,0:T(2,128)(2,1)S(1)}, bf16[2,640000]{1,0:T(2,128)(2,1)}, u32[]{:S(2)}) %copy-start) | copy-done | bytes 2560024
  1.7 0.1 windows.3
  1.9 0.0 copy-start.2
  1.9 1.3 %copy-done.2 = bf16[32,2,15488]{2,1,0:T(2,128)(2,1)} copy-done((bf16[32,2,15488]{2,1,0:T(2,128)(2,1)}, bf16[32,2,15488]{2,1,0:T(2,128)(2,1)S(1)}, u32[]{:S(2)}) %copy-start.2) | copy-done | bytes 1982488
  3.1 0.0 copy-start.1
  3.1 7.4 %all-to-all-start = ((bf16[32,2,15488]{2,1,0:T(2,128)(2,1)}), bf16[32,2,15488]{2,1,0:T(2,128)(2,1)}, u32[]{:S(2)}, u32[]{:S(2)}) async-start(bf16[32,2,15488]{2,1,0:T(2,128)(2,1)} %copy-done.2), calls=%async_computation | async-start | bytes 3964928 | tf_op jit(solution)/shard_map/all_to_all | solution.py:166
  10.5 0.0 copy-done.1
  10.6 0.9 windows.2
  11.4 45.4 %all-to-all-done = bf16[32,2,15488]{2,1,0:T(2,128)(2,1)} async-done(((bf16[32,2,15488]{2,1,0:T(2,128)(2,1)}), bf16[32,2,15488]{2,1,0:T(2,128)(2,1)}, u32[]{:S(2)}, u32[]{:S(2)}) %all-to-all-start) | async-done | bytes 1982496 | tf_op jit(solution)/shard_map/all_to_all | solution.py:166
  56.8 3.7 %all-to-all-start.1 = ((bf16[32,2,4736]{2,1,0:T(2,128)(2,1)}), bf16[32,2,4736]{2,1,0:T(2,128)(2,1)S(1)}, u32[]{:S(2)}, u32[]{:S(2)}) async-start(bf16[32,2,4736]{2,1,0:T(2,128)(2,1)} %windows.2), calls=%async_computation.1 | async-start | bytes 1212416 | tf_op jit(solution)/shard_map/all_to_all | solution.py:166
  60.5 0.1 pad_add_fusion.off_ref
  60.6 4.1 %reshape.32.amps_ref = bf16[64,15488]{1,0:T(8,128)(2,1)S(1)} reshape(bf16[32,2,15488]{2,1,0:T(2,128)(2,1)} %all-to-all-done) | data formatting | bytes 3964928 | tf_op jit(solution)/shard_map/reshape | solution.py:169
  64.7 20.3 %product.2.rest_0_ = f32[64,1600]{1,0:T(8,128)S(1)} custom-call(s32[2]{0:T(128)S(1)} %pad_add_fusion.off_ref, bf16[64,15488]{1,0:T(8,128)(2,1)S(1)} %reshape.32.amps_ref, bf16[1600,20000]{1,0:T(8,128)(2,1)} %bitcast.20), custom_call_target="tpu_custom_call" | custom-call | flops 3145728000 | bytes 49152000 | tf_op jit(solution)/shard_map/product/pallas_call | solution.py:108
  85.0 0.0 all-to-all-done.1
  85.0 0.2 reshape.30.amps_ref
  85.2 8.1 %product.3 = f32[64,1600]{1,0:T(8,128)S(1)} custom-call(s32[2]{0:T(128)S(1)} %pad_add_fusion.off_ref, bf16[64,4736]{1,0:T(8,128)(2,1)S(1)} %reshape.30.amps_ref, bf16[1600,20000]{1,0:T(8,128)(2,1)} %bitcast.21, f32[64,1600]{1,0:T(8,128)S(1)} %product.2.rest_0_), custom_call_target="tpu_custom_call" | custom-call | flops 950272000 | bytes 14848000 | tf_op jit(solution)/shard_map/product/pallas_call | solution.py:108
  93.3 0.2 reshape.33
  93.6 0.3 collective-permute-start
  93.9 1.2 %collective-permute-done = f32[1,2,2,4,2,1600]{5,4,2,0,1,3:T(2,128)S(1)} collective-permute-done((f32[1,2,2,4,2,1600]{5,4,2,0,1,3:T(2,128)S(1)}, f32[1,2,2,4,2,1600]{5,4,2,0,1,3:T(2,128)S(1)}, u32[]{:S(2)}, u32[]{:S(2)}) %collective-permute-start) | collective-permute-done | bytes 204832 | tf_op jit(solution)/shard_map/ppermute | solution.py:139
  95.1 0.1 bitcast_add_fusion
  95.3 1.8 %collective-permute-start.1 = (f32[1,2,4,2,1600]{4,3,1,2,0:T(2,128)S(1)}, f32[1,2,4,2,1600]{4,3,1,2,0:T(2,128)S(1)}, u32[]{:S(2)}, u32[]{:S(2)}) collective-permute-start(f32[1,2,4,2,1600]{4,3,1,2,0:T(2,128)S(1)} %dynamic-slice_bitcast_fusion.1), channel_id=1, source_target_pairs={{0,4},{4,0},{1,5},{5,1},{2,6},{6,2},{3,7},{7,3},{8,12},{12,8},{9,1... | collective-permute-start | bytes 307208 | tf_op jit(solution)/shard_map/ppermute | solution.py:139
  97.1 3.4 %collective-permute-done.1 = f32[1,2,4,2,1600]{4,3,1,2,0:T(2,128)S(1)} collective-permute-done((f32[1,2,4,2,1600]{4,3,1,2,0:T(2,128)S(1)}, f32[1,2,4,2,1600]{4,3,1,2,0:T(2,128)S(1)}, u32[]{:S(2)}, u32[]{:S(2)}) %collective-permute-start.1) | collective-permute-done | bytes 102432 | tf_op jit(solution)/shard_map/ppermute | solution.py:139
  100.5 0.1 bitcast_add_fusion.1
  100.6 1.7 %collective-permute-start.2 = (f32[1,4,2,1600]{3,2,1,0:T(2,128)S(1)}, f32[1,4,2,1600]{3,2,1,0:T(2,128)S(1)}, u32[]{:S(2)}, u32[]{:S(2)}) collective-permute-start(f32[1,4,2,1600]{3,2,1,0:T(2,128)S(1)} %dynamic-slice_bitcast_fusion.2), channel_id=1, source_target_pairs={{0,1},{1,0},{2,3},{3,2},{4,5},{5,4},{6,7},{7,6},{8,9},{9,8},{10,11... | collective-permute-start | bytes 153608 | tf_op jit(solution)/shard_map/ppermute | solution.py:139
  102.3 2.5 %collective-permute-done.2 = f32[1,4,2,1600]{3,2,1,0:T(2,128)S(1)} collective-permute-done((f32[1,4,2,1600]{3,2,1,0:T(2,128)S(1)}, f32[1,4,2,1600]{3,2,1,0:T(2,128)S(1)}, u32[]{:S(2)}, u32[]{:S(2)}) %collective-permute-start.2) | collective-permute-done | bytes 51232 | tf_op jit(solution)/shard_map/ppermute | solution.py:139
  104.8 2.6 %collective-permute-start.3 = (f32[2,2,1600]{2,1,0:T(2,128)S(1)}, f32[2,2,1600]{2,1,0:T(2,128)S(1)}, u32[]{:S(2)}, u32[]{:S(2)}) collective-permute-start(f32[2,2,1600]{2,1,0:T(2,128)S(1)} %dynamic-slice_bitcast_fusion.3), channel_id=1, source_target_pairs={{0,16},{8,24},{16,0},{24,8},{1,17},{9,25},{17,1},{25,9},{2,18},{10... | collective-permute-start | bytes 76808 | tf_op jit(solution)/shard_map/ppermute | solution.py:139
  107.5 2.2 %collective-permute-done.3 = f32[2,2,1600]{2,1,0:T(2,128)S(1)} collective-permute-done((f32[2,2,1600]{2,1,0:T(2,128)S(1)}, f32[2,2,1600]{2,1,0:T(2,128)S(1)}, u32[]{:S(2)}, u32[]{:S(2)}) %collective-permute-start.3) | collective-permute-done | bytes 25632 | tf_op jit(solution)/shard_map/ppermute | solution.py:139
  109.7 1.7 %collective-permute-start.4 = (f32[1,2,1600]{2,1,0:T(2,128)S(1)}, f32[1,2,1600]{2,1,0:T(2,128)S(1)}, u32[]{:S(2)}, u32[]{:S(2)}) collective-permute-start(f32[1,2,1600]{2,1,0:T(2,128)S(1)} %constant_dynamic-slice_fusion), channel_id=1, source_target_pairs={{0,8},{8,0},{16,24},{24,16},{1,9},{9,1},{17,25},{25,17},{2,10},{10... | collective-permute-start | bytes 38408 | tf_op jit(solution)/shard_map/ppermute | solution.py:139
  111.4 2.0 %collective-permute-done.4 = f32[1,2,1600]{2,1,0:T(2,128)S(1)} collective-permute-done((f32[1,2,1600]{2,1,0:T(2,128)S(1)}, f32[1,2,1600]{2,1,0:T(2,128)S(1)}, u32[]{:S(2)}, u32[]{:S(2)}) %collective-permute-start.4) | collective-permute-done | bytes 12832 | tf_op jit(solution)/shard_map/ppermute | solution.py:139
  113.5 0.7 reshape_squeeze.9
  (8 shorter events, 0.1 us)
Async XLA Ops:
  0.0 1.7 %copy-start = (bf16[2,640000]{1,0:T(2,128)(2,1)S(1)}, bf16[2,640000]{1,0:T(2,128)(2,1)}, u32[]{:S(2)}) copy-start(bf16[2,640000]{1,0:T(2,128)(2,1)} %x_ref.3) | copy-start | bytes 7680004
  1.9 1.3 %copy-start.2 = (bf16[32,2,15488]{2,1,0:T(2,128)(2,1)}, bf16[32,2,15488]{2,1,0:T(2,128)(2,1)S(1)}, u32[]{:S(2)}) copy-start(bf16[32,2,15488]{2,1,0:T(2,128)(2,1)S(1)} %windows.3) | copy-start | bytes 5947396
  3.1 7.4 %copy-start.1 = (bf16[2,640000]{1,0:T(2,128)(2,1)S(1)}, bf16[2,640000]{1,0:T(2,128)(2,1)}, u32[]{:S(2)}) copy-start(bf16[2,640000]{1,0:T(2,128)(2,1)} %x_ref.3) | copy-start | bytes 7680004
  3.1 53.7 %all-to-all-start = ((bf16[32,2,15488]{2,1,0:T(2,128)(2,1)}), bf16[32,2,15488]{2,1,0:T(2,128)(2,1)}, u32[]{:S(2)}, u32[]{:S(2)}) async-start(bf16[32,2,15488]{2,1,0:T(2,128)(2,1)} %copy-done.2), calls=%async_computation | async-start | bytes 3964928 | tf_op jit(solution)/shard_map/all_to_all | solution.py:166
  56.8 28.2 %all-to-all-start.1 = ((bf16[32,2,4736]{2,1,0:T(2,128)(2,1)}), bf16[32,2,4736]{2,1,0:T(2,128)(2,1)S(1)}, u32[]{:S(2)}, u32[]{:S(2)}) async-start(bf16[32,2,4736]{2,1,0:T(2,128)(2,1)} %windows.2), calls=%async_computation.1 | async-start | bytes 1212416 | tf_op jit(solution)/shard_map/all_to_all | solution.py:166
  93.6 1.5 %collective-permute-start = (f32[1,2,2,4,2,1600]{5,4,2,0,1,3:T(2,128)S(1)}, f32[1,2,2,4,2,1600]{5,4,2,0,1,3:T(2,128)S(1)}, u32[]{:S(2)}, u32[]{:S(2)}) collective-permute-start(f32[1,2,2,4,2,1600]{5,4,2,0,1,3:T(2,128)S(1)} %dynamic-slice_bitcast_fusion), channel_id=1, source_target_pairs={{0,2},{2,0},{1,3},{3,1},{4,6},{6,4},{5,7},{7,5},{8,10},{10,8},{9,1... | collective-permute-start | bytes 614408 | tf_op jit(solution)/shard_map/ppermute | solution.py:139
  95.3 5.2 %collective-permute-start.1 = (f32[1,2,4,2,1600]{4,3,1,2,0:T(2,128)S(1)}, f32[1,2,4,2,1600]{4,3,1,2,0:T(2,128)S(1)}, u32[]{:S(2)}, u32[]{:S(2)}) collective-permute-start(f32[1,2,4,2,1600]{4,3,1,2,0:T(2,128)S(1)} %dynamic-slice_bitcast_fusion.1), channel_id=1, source_target_pairs={{0,4},{4,0},{1,5},{5,1},{2,6},{6,2},{3,7},{7,3},{8,12},{12,8},{9,1... | collective-permute-start | bytes 307208 | tf_op jit(solution)/shard_map/ppermute | solution.py:139
  100.6 4.2 %collective-permute-start.2 = (f32[1,4,2,1600]{3,2,1,0:T(2,128)S(1)}, f32[1,4,2,1600]{3,2,1,0:T(2,128)S(1)}, u32[]{:S(2)}, u32[]{:S(2)}) collective-permute-start(f32[1,4,2,1600]{3,2,1,0:T(2,128)S(1)} %dynamic-slice_bitcast_fusion.2), channel_id=1, source_target_pairs={{0,1},{1,0},{2,3},{3,2},{4,5},{5,4},{6,7},{7,6},{8,9},{9,8},{10,11... | collective-permute-start | bytes 153608 | tf_op jit(solution)/shard_map/ppermute | solution.py:139
  104.8 4.8 %collective-permute-start.3 = (f32[2,2,1600]{2,1,0:T(2,128)S(1)}, f32[2,2,1600]{2,1,0:T(2,128)S(1)}, u32[]{:S(2)}, u32[]{:S(2)}) collective-permute-start(f32[2,2,1600]{2,1,0:T(2,128)S(1)} %dynamic-slice_bitcast_fusion.3), channel_id=1, source_target_pairs={{0,16},{8,24},{16,0},{24,8},{1,17},{9,25},{17,1},{25,9},{2,18},{10... | collective-permute-start | bytes 76808 | tf_op jit(solution)/shard_map/ppermute | solution.py:139
  109.7 3.8 %collective-permute-start.4 = (f32[1,2,1600]{2,1,0:T(2,128)S(1)}, f32[1,2,1600]{2,1,0:T(2,128)S(1)}, u32[]{:S(2)}, u32[]{:S(2)}) collective-permute-start(f32[1,2,1600]{2,1,0:T(2,128)S(1)} %constant_dynamic-slice_fusion), channel_id=1, source_target_pairs={{0,8},{8,0},{16,24},{24,16},{1,9},{9,1},{17,25},{25,17},{2,10},{10... | collective-permute-start | bytes 38408 | tf_op jit(solution)/shard_map/ppermute | solution.py:139

commit v5 on v4

v5 whole, which is shorter than its diff:
```python
import functools

import jax
import jax.numpy as jnp
from jax import lax
from jax.experimental import pallas as pl
from jax.experimental.pallas import tpu as pltpu
from jax.sharding import Mesh, PartitionSpec as P

ALL = ("z", "x", "core", "col")
LANES = 128
BLOCK = 1280
BUFFERS = 4
FIRST = 0.75


def window_kernel(starts, x_ref, o_ref):
    width = o_ref.shape[2]
    for index, start in enumerate(starts):
        size = min(width, x_ref.shape[1] - start)
        o_ref[index, :, pl.ds(0, size)] = x_ref[:, pl.ds(start, size)]


def windows(x, starts, width):
    return pl.pallas_call(
        functools.partial(window_kernel, starts),
        out_shape=jax.ShapeDtypeStruct((len(starts), x.shape[0], width), x.dtype),
        in_specs=[pl.BlockSpec(memory_space=pltpu.VMEM)],
        out_specs=pl.BlockSpec(memory_space=pltpu.VMEM),
        compiler_params=pltpu.CompilerParams(vmem_limit_bytes=16 * 1024 * 1024),
        cost_estimate=pl.CostEstimate(
            flops=0, bytes_accessed=4 * len(starts) * x.shape[0] * width, transcendentals=0
        ),
        name="windows",
    )(x)


def product_kernel(first, steps, tail_width, has_sum, off_ref, amps_ref, ints_hbm, *rest):
    sum_ref = rest[0] if has_sum else None
    out_ref, acc_ref = rest[-2:]
    off = off_ref[0]
    back = off_ref[1]
    pairs = amps_ref.shape[0]
    lane = lax.broadcasted_iota(jnp.int32, (pairs, LANES), 1)
    from_here = lane < LANES - off
    acc_ref[...] = jnp.zeros_like(acc_ref)

    def tiles(base, count, limit):
        rolled = []
        for t in range(min(count + 1, limit)):
            tile = amps_ref[:, pl.ds(pl.multiple_of(base + t * LANES, LANES), LANES)]
            rolled.append(pltpu.roll(tile.astype(jnp.float32), back, 1))
        return [
            jnp.where(from_here, rolled[t], rolled[min(t + 1, len(rolled) - 1)])
            for t in range(count)
        ]

    def dot(ints, amps):
        return lax.dot_general(
            ints, amps, (((1,), (1,)), ((), ())), preferred_element_type=jnp.float32
        )

    def body(ints_ref):
        step = pl.program_id(0)

        def full():
            parts = tiles(step * BLOCK, BLOCK // LANES, BLOCK // LANES + 1)
            amps = jnp.concatenate([p.astype(jnp.bfloat16) for p in parts], axis=1)
            acc_ref[...] += dot(ints_ref[...], amps)

        def tail():
            count = -(-tail_width // LANES)
            base = (steps - 1) * BLOCK
            parts = tiles(base, count, (amps_ref.shape[1] - base) // LANES)
            whole = tail_width // LANES
            if whole:
                amps = jnp.concatenate([p.astype(jnp.bfloat16) for p in parts[:whole]], axis=1)
                acc_ref[...] += dot(ints_ref[:, : whole * LANES], amps)
            if whole < count:
                valid = tail_width - whole * LANES
                amps = jnp.where(lane < valid, parts[whole], 0.0).astype(jnp.bfloat16)
                ints = ints_ref[:, whole * LANES : count * LANES]
                place = lax.broadcasted_iota(jnp.int32, ints.shape, 1)
                ints = jnp.where(place < valid, ints, jnp.zeros_like(ints))
                acc_ref[...] += dot(ints, amps)

        if tail_width == BLOCK:
            full()
        else:
            if steps > 1:
                pl.when(step < steps - 1)(full)
            pl.when(step == steps - 1)(tail)

    spec = pl.BlockSpec(
        (ints_hbm.shape[0], BLOCK),
        lambda j: (0, first + j),
        pipeline_mode=pl.Buffered(BUFFERS),
    )
    pltpu.emit_pipeline(body, grid=(steps,), in_specs=[spec])(ints_hbm)
    result = acc_ref[...].T
    out_ref[...] = result + sum_ref[...] if has_sum else result


def product(shift, amps, flat, low, high, total):
    pairs = amps.shape[0]
    rows = flat.shape[0]
    width = high - low
    steps = -(-width // BLOCK)
    whole = pl.BlockSpec(memory_space=pltpu.VMEM)
    sums = [] if total is None else [total]
    tail_width = width - (steps - 1) * BLOCK
    return pl.pallas_call(
        functools.partial(product_kernel, low // BLOCK, steps, tail_width, bool(sums)),
        out_shape=jax.ShapeDtypeStruct((pairs, rows), jnp.float32),
        in_specs=[
            pl.BlockSpec(memory_space=pltpu.SMEM),
            whole,
            pl.BlockSpec(memory_space=pl.ANY),
        ]
        + [whole] * len(sums),
        out_specs=whole,
        scratch_shapes=[pltpu.VMEM((rows, pairs), jnp.float32)],
        compiler_params=pltpu.CompilerParams(vmem_limit_bytes=24 * 1024 * 1024),
        cost_estimate=pl.CostEstimate(
            flops=2 * pairs * rows * width, bytes_accessed=2 * rows * width, transcendentals=0
        ),
        name="product",
    )(shift, amps, flat, *sums)


def exchange_sum(blocks, names):
    count = blocks.shape[0]
    me = lax.axis_index(names)
    terms = [lax.dynamic_index_in_dim(blocks, me, 0, keepdims=False)]
    power = count & (count - 1) == 0
    for step in range(count - 1, 0, -1):
        to = (lambda i: i ^ step) if power else (lambda i: (i + step) % count)
        block = lax.dynamic_index_in_dim(blocks, to(me), 0, keepdims=False)
        terms.append(lax.ppermute(block, names, [(i, to(i)) for i in range(count)]))
    return sum(terms[1:], terms[0])


def shards(amplitudes, integrals):
    z, x, core, col = (lax.axis_size(name) for name in ALL)
    count = z * x * core * col
    pair_local, full_width = amplitudes.shape
    slab = full_width // count
    window, virtuals, _ = integrals.shape
    rows = window * virtuals
    flat = integrals.reshape(rows, slab)

    begins = [d * slab // LANES * LANES for d in range(count)]
    most = max(1, max(d * slab - begins[d] for d in range(count)))
    off = lax.rem(lax.axis_index(ALL) * slab, LANES)
    shift = jnp.stack([off, lax.rem(LANES - off, LANES)]).astype(jnp.int32)

    blocks = -(-slab // BLOCK)
    cut = max(1, min(blocks - 1, round(FIRST * blocks))) * BLOCK
    parts = [(0, cut), (cut, slab)] if cut < slab else [(0, slab)]
    widths = [-(-(most + high - low) // LANES) * LANES for low, high in parts]
    sent = [windows(amplitudes, [b + low for b in begins], w) for (low, _), w in zip(parts, widths)]
    got = []
    for block in sent:
        if got:
            block, got[-1] = lax.optimization_barrier((block, got[-1]))
        got.append(lax.all_to_all(block, ALL, split_axis=0, concat_axis=0, tiled=True))
    total = None
    for (low, high), width, block in zip(parts, widths, got):
        amps = block.reshape(count * pair_local, width)
        total = product(shift, amps, flat, low, high, total)

    part = total.reshape(z, x, core, col, pair_local, rows)
    part = exchange_sum(part.transpose(2, 0, 1, 3, 4, 5).reshape(core, z, x * col, pair_local, rows), "core")
    part = exchange_sum(part.transpose(1, 0, 2, 3), ("x", "col"))
    part = exchange_sum(part, "z")
    return part.reshape(pair_local, window, virtuals)


def solution(mesh):
    devices = mesh.devices
    row, col = devices.shape
    split = Mesh(devices.reshape(row // 4, 2, 2, col), ALL)
    return jax.shard_map(
        shards,
        mesh=split,
        in_specs=(P(ALL, None), P(None, None, ALL)),
        out_specs=P(ALL, None, None),
        check_vma=False,
    )
```

time: 115 us -> 110 us (0.957)
  waiting for transfers between devices: 56.6 us -> 54 us
  Pallas kernels: 29.4 us -> 28 us
    ppermute x5 -> x7, waiting for transfers between devices: 11.3 us -> 8.66 us  [exchange_sum(): terms.append(lax.ppermute(block, names, [(i, to(i)) for i in range(count)]))]
    pallas_call x2, Pallas kernels: 28.4 us -> 27 us  [product(): pl.pallas_call(functools.partial(product_kernel, low // BLOCK, steps, tai...]
    ppermute x5 -> x7, starting transfers between devices: 8.25 us -> 8.29 us  [exchange_sum(): terms.append(lax.ppermute(block, names, [(i, to(i)) for i in range(count)]))]
  transfers between devices with their start and end apart: 7 -> 9, of which waited for: 6 -> 7; matrix products, arithmetic and copies ran while one was open for 4% -> 4% of each run, Pallas kernels for 19% -> 18%
where the time goes in v5:
time: 110 us
  waiting for transfers between devices  54 us (49%)
  Pallas kernels  28 us (25%)
  starting transfers between devices  19.4 us (18%)
  local copies, waits for them, and re-layouts  8.39 us (8%)
    all_to_all x2, waiting for transfers between devices, shards(): lax.all_to_all(block, ALL, split_axis=0, concat_axis=0, tiled=True)  45.4 us
    pallas_call x2, Pallas kernels, product(): pl.pallas_call(functools.partial(product_kernel, low // BLOCK, steps, tai...  27 us
    all_to_all x2, starting transfers between devices, shards(): lax.all_to_all(block, ALL, split_axis=0, concat_axis=0, tiled=True)  11.1 us
    ppermute x7, waiting for transfers between devices, exchange_sum(): terms.append(lax.ppermute(block, names, [(i, to(i)) for i in range(count)]))  8.66 us
    ppermute x7, starting transfers between devices, exchange_sum(): terms.append(lax.ppermute(block, names, [(i, to(i)) for i in range(count)]))  8.29 us
    reshape x2, local copies, waits for them, and re-layouts, shards(): amps = block.reshape(count * pair_local, width)  4.35 us
    unnamed x6, local copies, waits for them, and re-layouts  2.99 us
  transfers between devices with their start and end apart: 9, of which 7 were waited for; matrix products, arithmetic and copies ran while one was open for 4% of the time, Pallas kernels for 18%

profile of v5, /device:TPU:0, one launch (start us, length us, event | category | flops | bytes accessed | tf_op | source)
XLA Modules:
  0.0 110.1 jit_solution(14071945568694920023)
XLA Ops:
  0.0 0.0 copy-start
  0.0 1.7 %copy-done = bf16[2,640000]{1,0:T(2,128)(2,1)S(1)} copy-done((bf16[2,640000]{1,0:T(2,128)(2,1)S(1)}, bf16[2,640000]{1,0:T(2,128)(2,1)}, u32[]{:S(2)}) %copy-start) | copy-done | bytes 2560024
  1.7 0.1 windows.3
  1.9 0.0 copy-start.2
  1.9 1.3 %copy-done.2 = bf16[32,2,15488]{2,1,0:T(2,128)(2,1)} copy-done((bf16[32,2,15488]{2,1,0:T(2,128)(2,1)}, bf16[32,2,15488]{2,1,0:T(2,128)(2,1)S(1)}, u32[]{:S(2)}) %copy-start.2) | copy-done | bytes 1982488
  3.1 0.0 copy-start.1
  3.1 7.4 %all-to-all-start = ((bf16[32,2,15488]{2,1,0:T(2,128)(2,1)}), bf16[32,2,15488]{2,1,0:T(2,128)(2,1)}, u32[]{:S(2)}, u32[]{:S(2)}) async-start(bf16[32,2,15488]{2,1,0:T(2,128)(2,1)} %copy-done.2), calls=%async_computation | async-start | bytes 3964928 | tf_op jit(solution)/shard_map/all_to_all | solution.py:166
  10.6 0.0 copy-done.1
  10.6 0.9 windows.2
  11.4 45.4 %all-to-all-done = bf16[32,2,15488]{2,1,0:T(2,128)(2,1)} async-done(((bf16[32,2,15488]{2,1,0:T(2,128)(2,1)}), bf16[32,2,15488]{2,1,0:T(2,128)(2,1)}, u32[]{:S(2)}, u32[]{:S(2)}) %all-to-all-start) | async-done | bytes 1982496 | tf_op jit(solution)/shard_map/all_to_all | solution.py:166
  56.8 3.7 %all-to-all-start.1 = ((bf16[32,2,4736]{2,1,0:T(2,128)(2,1)}), bf16[32,2,4736]{2,1,0:T(2,128)(2,1)S(1)}, u32[]{:S(2)}, u32[]{:S(2)}) async-start(bf16[32,2,4736]{2,1,0:T(2,128)(2,1)} %windows.2), calls=%async_computation.1 | async-start | bytes 1212416 | tf_op jit(solution)/shard_map/all_to_all | solution.py:166
  60.5 0.1 pad_add_fusion.off_ref
  60.6 4.1 %reshape.28.amps_ref = bf16[64,15488]{1,0:T(8,128)(2,1)S(1)} reshape(bf16[32,2,15488]{2,1,0:T(2,128)(2,1)} %all-to-all-done) | data formatting | bytes 3964928 | tf_op jit(solution)/shard_map/reshape | solution.py:169
  64.7 18.9 %product.2.rest_0_ = f32[64,1600]{1,0:T(8,128)S(1)} custom-call(s32[2]{0:T(128)S(1)} %pad_add_fusion.off_ref, bf16[64,15488]{1,0:T(8,128)(2,1)S(1)} %reshape.28.amps_ref, bf16[1600,20000]{1,0:T(8,128)(2,1)} %bitcast.34), custom_call_target="tpu_custom_call" | custom-call | flops 3145728000 | bytes 49152000 | tf_op jit(solution)/shard_map/product/pallas_call | solution.py:112
  83.6 0.0 all-to-all-done.1
  83.6 0.2 reshape.26.amps_ref
  83.9 8.1 %product.3 = f32[64,1600]{1,0:T(8,128)S(1)} custom-call(s32[2]{0:T(128)S(1)} %pad_add_fusion.off_ref, bf16[64,4736]{1,0:T(8,128)(2,1)S(1)} %reshape.26.amps_ref, bf16[1600,20000]{1,0:T(8,128)(2,1)} %bitcast.35, f32[64,1600]{1,0:T(8,128)S(1)} %product.2.rest_0_), custom_call_target="tpu_custom_call" | custom-call | flops 950272000 | bytes 14848000 | tf_op jit(solution)/shard_map/product/pallas_call | solution.py:112
  91.9 0.2 reshape.29
  92.3 0.3 collective-permute-start
  92.5 1.2 %collective-permute-done = f32[4,4,2,1600]{3,2,1,0:T(2,128)S(1)} collective-permute-done((f32[4,4,2,1600]{3,2,1,0:T(2,128)S(1)}, f32[4,4,2,1600]{3,2,1,0:T(2,128)S(1)}, u32[]{:S(2)}, u32[]{:S(2)}) %collective-permute-start) | collective-permute-done | bytes 204832 | tf_op jit(solution)/shard_map/ppermute | solution.py:139
  93.8 0.1 bitcast_add_fusion
  93.9 2.7 %collective-permute-start.1 = (f32[4,2,1600]{2,1,0:T(2,128)S(1)}, f32[4,2,1600]{2,1,0:T(2,128)S(1)}, u32[]{:S(2)}, u32[]{:S(2)}) collective-permute-start(f32[4,2,1600]{2,1,0:T(2,128)S(1)} %get-tuple-element.9), channel_id=1, source_target_pairs={{0,5},{1,4},{4,1},{5,0},{2,7},{3,6},{6,3},{7,2},{8,13},{9,12},{12,... | collective-permute-start | bytes 153608 | tf_op jit(solution)/shard_map/ppermute | solution.py:139
  96.6 0.6 collective-permute-start.2
  97.2 0.3 collective-permute-start.3
  97.5 1.5 %collective-permute-done.1 = f32[4,2,1600]{2,1,0:T(2,128)S(1)} collective-permute-done((f32[4,2,1600]{2,1,0:T(2,128)S(1)}, f32[4,2,1600]{2,1,0:T(2,128)S(1)}, u32[]{:S(2)}, u32[]{:S(2)}) %collective-permute-start.1) | collective-permute-done | bytes 51232 | tf_op jit(solution)/shard_map/ppermute | solution.py:139
  99.0 1.7 %collective-permute-done.2 = f32[4,2,1600]{2,1,0:T(2,128)S(1)} collective-permute-done((f32[4,2,1600]{2,1,0:T(2,128)S(1)}, f32[4,2,1600]{2,1,0:T(2,128)S(1)}, u32[]{:S(2)}, u32[]{:S(2)}) %collective-permute-start.2) | collective-permute-done | bytes 51232 | tf_op jit(solution)/shard_map/ppermute | solution.py:139
  100.8 0.6 collective-permute-done.3
  101.4 3.4 %collective-permute-start.4 = (f32[2,1600]{1,0:T(2,128)S(1)}, f32[2,1600]{1,0:T(2,128)S(1)}, u32[]{:S(2)}, u32[]{:S(2)}) collective-permute-start(f32[2,1600]{1,0:T(2,128)S(1)} %get-tuple-element.12), channel_id=1, source_target_pairs={{0,24},{8,16},{16,8},{24,0},{1,25},{9,17},{17,9},{25,1},{2,26},{10... | collective-permute-start | bytes 38408 | tf_op jit(solution)/shard_map/ppermute | solution.py:139
  104.8 0.0 collective-permute-start.5
  104.8 1.0 collective-permute-start.6
  105.9 1.1 %collective-permute-done.4 = f32[2,1600]{1,0:T(2,128)S(1)} collective-permute-done((f32[2,1600]{1,0:T(2,128)S(1)}, f32[2,1600]{1,0:T(2,128)S(1)}, u32[]{:S(2)}, u32[]{:S(2)}) %collective-permute-start.4) | collective-permute-done | bytes 12832 | tf_op jit(solution)/shard_map/ppermute | solution.py:139
  107.0 2.4 %collective-permute-done.5 = f32[2,1600]{1,0:T(2,128)S(1)} collective-permute-done((f32[2,1600]{1,0:T(2,128)S(1)}, f32[2,1600]{1,0:T(2,128)S(1)}, u32[]{:S(2)}, u32[]{:S(2)}) %collective-permute-start.5) | collective-permute-done | bytes 12832 | tf_op jit(solution)/shard_map/ppermute | solution.py:139
  109.4 0.0 collective-permute-done.6
  109.5 0.7 reshape.31
  (6 shorter events, 0.2 us)
Async XLA Ops:
  0.0 1.7 %copy-start = (bf16[2,640000]{1,0:T(2,128)(2,1)S(1)}, bf16[2,640000]{1,0:T(2,128)(2,1)}, u32[]{:S(2)}) copy-start(bf16[2,640000]{1,0:T(2,128)(2,1)} %x_ref.3) | copy-start | bytes 7680004
  1.9 1.3 %copy-start.2 = (bf16[32,2,15488]{2,1,0:T(2,128)(2,1)}, bf16[32,2,15488]{2,1,0:T(2,128)(2,1)S(1)}, u32[]{:S(2)}) copy-start(bf16[32,2,15488]{2,1,0:T(2,128)(2,1)S(1)} %windows.3) | copy-start | bytes 5947396
  3.1 7.4 %copy-start.1 = (bf16[2,640000]{1,0:T(2,128)(2,1)S(1)}, bf16[2,640000]{1,0:T(2,128)(2,1)}, u32[]{:S(2)}) copy-start(bf16[2,640000]{1,0:T(2,128)(2,1)} %x_ref.3) | copy-start | bytes 7680004
  3.1 53.7 %all-to-all-start = ((bf16[32,2,15488]{2,1,0:T(2,128)(2,1)}), bf16[32,2,15488]{2,1,0:T(2,128)(2,1)}, u32[]{:S(2)}, u32[]{:S(2)}) async-start(bf16[32,2,15488]{2,1,0:T(2,128)(2,1)} %copy-done.2), calls=%async_computation | async-start | bytes 3964928 | tf_op jit(solution)/shard_map/all_to_all | solution.py:166
  56.8 26.8 %all-to-all-start.1 = ((bf16[32,2,4736]{2,1,0:T(2,128)(2,1)}), bf16[32,2,4736]{2,1,0:T(2,128)(2,1)S(1)}, u32[]{:S(2)}, u32[]{:S(2)}) async-start(bf16[32,2,4736]{2,1,0:T(2,128)(2,1)} %windows.2), calls=%async_computation.1 | async-start | bytes 1212416 | tf_op jit(solution)/shard_map/all_to_all | solution.py:166
  92.3 1.5 %collective-permute-start = (f32[4,4,2,1600]{3,2,1,0:T(2,128)S(1)}, f32[4,4,2,1600]{3,2,1,0:T(2,128)S(1)}, u32[]{:S(2)}, u32[]{:S(2)}) collective-permute-start(f32[4,4,2,1600]{3,2,1,0:T(2,128)S(1)} %dynamic-slice_bitcast_fusion), channel_id=1, source_target_pairs={{0,2},{2,0},{1,3},{3,1},{4,6},{6,4},{5,7},{7,5},{8,10},{10,8},{9,1... | collective-permute-start | bytes 614408 | tf_op jit(solution)/shard_map/ppermute | solution.py:139
  93.9 5.1 %collective-permute-start.1 = (f32[4,2,1600]{2,1,0:T(2,128)S(1)}, f32[4,2,1600]{2,1,0:T(2,128)S(1)}, u32[]{:S(2)}, u32[]{:S(2)}) collective-permute-start(f32[4,2,1600]{2,1,0:T(2,128)S(1)} %get-tuple-element.9), channel_id=1, source_target_pairs={{0,5},{1,4},{4,1},{5,0},{2,7},{3,6},{6,3},{7,2},{8,13},{9,12},{12,... | collective-permute-start | bytes 153608 | tf_op jit(solution)/shard_map/ppermute | solution.py:139
  96.6 4.1 %collective-permute-start.2 = (f32[4,2,1600]{2,1,0:T(2,128)S(1)}, f32[4,2,1600]{2,1,0:T(2,128)S(1)}, u32[]{:S(2)}, u32[]{:S(2)}) collective-permute-start(f32[4,2,1600]{2,1,0:T(2,128)S(1)} %get-tuple-element.11), channel_id=1, source_target_pairs={{0,4},{1,5},{4,0},{5,1},{2,6},{3,7},{6,2},{7,3},{8,12},{9,13},{12,... | collective-permute-start | bytes 153608 | tf_op jit(solution)/shard_map/ppermute | solution.py:139
  97.2 4.1 %collective-permute-start.3 = (f32[4,2,1600]{2,1,0:T(2,128)S(1)}, f32[4,2,1600]{2,1,0:T(2,128)S(1)}, u32[]{:S(2)}, u32[]{:S(2)}) collective-permute-start(f32[4,2,1600]{2,1,0:T(2,128)S(1)} %get-tuple-element.10), channel_id=1, source_target_pairs={{0,1},{1,0},{4,5},{5,4},{2,3},{3,2},{6,7},{7,6},{8,9},{9,8},{12,13... | collective-permute-start | bytes 153608 | tf_op jit(solution)/shard_map/ppermute | solution.py:139
  101.4 5.6 %collective-permute-start.4 = (f32[2,1600]{1,0:T(2,128)S(1)}, f32[2,1600]{1,0:T(2,128)S(1)}, u32[]{:S(2)}, u32[]{:S(2)}) collective-permute-start(f32[2,1600]{1,0:T(2,128)S(1)} %get-tuple-element.12), channel_id=1, source_target_pairs={{0,24},{8,16},{16,8},{24,0},{1,25},{9,17},{17,9},{25,1},{2,26},{10... | collective-permute-start | bytes 38408 | tf_op jit(solution)/shard_map/ppermute | solution.py:139
  104.8 4.6 %collective-permute-start.5 = (f32[2,1600]{1,0:T(2,128)S(1)}, f32[2,1600]{1,0:T(2,128)S(1)}, u32[]{:S(2)}, u32[]{:S(2)}) collective-permute-start(f32[2,1600]{1,0:T(2,128)S(1)} %get-tuple-element.14), channel_id=1, source_target_pairs={{0,16},{8,24},{16,0},{24,8},{1,17},{9,25},{17,1},{25,9},{2,18},{10... | collective-permute-start | bytes 38408 | tf_op jit(solution)/shard_map/ppermute | solution.py:139
  104.8 4.6 %collective-permute-start.6 = (f32[2,1600]{1,0:T(2,128)S(1)}, f32[2,1600]{1,0:T(2,128)S(1)}, u32[]{:S(2)}, u32[]{:S(2)}) collective-permute-start(f32[2,1600]{1,0:T(2,128)S(1)} %get-tuple-element.13), channel_id=1, source_target_pairs={{0,8},{8,0},{16,24},{24,16},{1,9},{9,1},{17,25},{25,17},{2,10},{10... | collective-permute-start | bytes 38408 | tf_op jit(solution)/shard_map/ppermute | solution.py:139

commit v6 on v1

v6 whole, which is shorter than its diff:
```python
import functools

import jax
import jax.numpy as jnp
from jax import lax
from jax.experimental import pallas as pl
from jax.experimental.pallas import tpu as pltpu
from jax.sharding import Mesh, PartitionSpec as P

ALL = ("z", "x", "core", "col")
LANES = 128
BLOCK = 1280
BUFFERS = 3
LIMIT = 20 * 1024 * 1024
FIRST = 0.7


def window_kernel(starts, x_ref, o_ref):
    width = o_ref.shape[2]
    for index, start in enumerate(starts):
        size = min(width, x_ref.shape[1] - start)
        o_ref[index, :, pl.ds(0, size)] = x_ref[:, pl.ds(start, size)]


def windows(x, starts, width):
    return pl.pallas_call(
        functools.partial(window_kernel, starts),
        out_shape=jax.ShapeDtypeStruct((len(starts), x.shape[0], width), x.dtype),
        in_specs=[pl.BlockSpec(memory_space=pltpu.VMEM)],
        out_specs=pl.BlockSpec(memory_space=pltpu.VMEM),
        compiler_params=pltpu.CompilerParams(vmem_limit_bytes=16 * 1024 * 1024),
        cost_estimate=pl.CostEstimate(
            flops=0, bytes_accessed=4 * len(starts) * x.shape[0] * width, transcendentals=0
        ),
        name="windows",
    )(x)


def dot(ints, amps):
    return lax.dot_general(ints, amps, (((1,), (1,)), ((), ())), preferred_element_type=jnp.float32)


def shifted(off_ref, amps_ref, base, count, limit):
    lane = lax.broadcasted_iota(jnp.int32, (amps_ref.shape[0], LANES), 1)
    from_here = lane < LANES - off_ref[0]
    rolled = []
    for t in range(min(count + 1, limit)):
        tile = amps_ref[:, pl.ds(pl.multiple_of(base + t * LANES, LANES), LANES)]
        rolled.append(pltpu.roll(tile.astype(jnp.float32), off_ref[1], 1))
    return [
        jnp.where(from_here, rolled[t], rolled[min(t + 1, len(rolled) - 1)]) for t in range(count)
    ]


def first_kernel(steps, off_ref, amps_ref, ints_hbm, out_ref, acc_ref):
    acc_ref[...] = jnp.zeros_like(acc_ref)

    def body(ints_ref):
        step = pl.program_id(0)
        parts = shifted(off_ref, amps_ref, step * BLOCK, BLOCK // LANES, BLOCK // LANES + 1)
        amps = jnp.concatenate([p.astype(jnp.bfloat16) for p in parts], axis=1)
        acc_ref[...] += dot(ints_ref[...], amps)

    spec = pl.BlockSpec(
        (ints_hbm.shape[0], BLOCK), lambda j: (0, j), pipeline_mode=pl.Buffered(BUFFERS)
    )
    pltpu.emit_pipeline(body, grid=(steps,), in_specs=[spec])(ints_hbm)
    out_ref[...] = acc_ref[...].T


def last_kernel(width, off_ref, amps_ref, kept_ref, sum_ref, out_ref, acc_ref):
    acc_ref[...] = jnp.zeros_like(acc_ref)
    have = amps_ref.shape[1] // LANES
    for base in range(0, width, BLOCK):
        size = min(BLOCK, width - base)
        count = -(-size // LANES)
        parts = shifted(off_ref, amps_ref, base, count, have - base // LANES)
        whole = size // LANES
        if whole:
            amps = jnp.concatenate([p.astype(jnp.bfloat16) for p in parts[:whole]], axis=1)
            acc_ref[...] += dot(kept_ref[:, pl.ds(base, whole * LANES)], amps)
        if whole < count:
            valid = size - whole * LANES
            amps = parts[whole].astype(jnp.bfloat16)[:, :valid]
            acc_ref[...] += dot(kept_ref[:, pl.ds(base + whole * LANES, valid)], amps)
    out_ref[...] = acc_ref[...].T + sum_ref[...]


def products(shift, amps, flat, cut, late, kept):
    pairs = amps.shape[0]
    rows, slab = flat.shape
    vmem = pl.BlockSpec(memory_space=pltpu.VMEM)
    smem = pl.BlockSpec(memory_space=pltpu.SMEM)
    total = jax.ShapeDtypeStruct((pairs, rows), jnp.float32)
    acc = [pltpu.VMEM((rows, pairs), jnp.float32)]
    first = pl.pallas_call(
        functools.partial(first_kernel, cut // BLOCK),
        out_shape=total,
        in_specs=[smem, vmem, pl.BlockSpec(memory_space=pl.ANY)],
        out_specs=vmem,
        scratch_shapes=acc,
        compiler_params=pltpu.CompilerParams(vmem_limit_bytes=LIMIT),
        cost_estimate=pl.CostEstimate(
            flops=2 * pairs * rows * cut, bytes_accessed=2 * rows * cut, transcendentals=0
        ),
        name="first_product",
    )(shift, amps, flat)
    return pl.pallas_call(
        functools.partial(last_kernel, slab - cut),
        out_shape=total,
        in_specs=[smem, vmem, vmem, vmem],
        out_specs=vmem,
        scratch_shapes=acc,
        compiler_params=pltpu.CompilerParams(vmem_limit_bytes=LIMIT),
        cost_estimate=pl.CostEstimate(
            flops=2 * pairs * rows * (slab - cut), bytes_accessed=2 * rows * (slab - cut), transcendentals=0
        ),
        name="last_product",
    )(shift, late, kept, first)


def exchange_sum(blocks, names):
    count = blocks.shape[0]
    me = lax.axis_index(names)
    terms = [lax.dynamic_index_in_dim(blocks, me, 0, keepdims=False)]
    power = count & (count - 1) == 0
    for step in range(count - 1, 0, -1):
        to = (lambda i: i ^ step) if power else (lambda i: (i + step) % count)
        block = lax.dynamic_index_in_dim(blocks, to(me), 0, keepdims=False)
        terms.append(lax.ppermute(block, names, [(i, to(i)) for i in range(count)]))
    return sum(terms[1:], terms[0])


def shards(amplitudes, integrals):
    z, x, core, col = (lax.axis_size(name) for name in ALL)
    count = z * x * core * col
    pair_local, full_width = amplitudes.shape
    slab = full_width // count
    window, virtuals, _ = integrals.shape
    rows = window * virtuals
    flat = integrals.reshape(rows, slab)

    begins = [d * slab // LANES * LANES for d in range(count)]
    most = max(1, max(d * slab - begins[d] for d in range(count)))
    off = lax.rem(lax.axis_index(ALL) * slab, LANES)
    shift = jnp.stack([off, lax.rem(LANES - off, LANES)]).astype(jnp.int32)

    blocks = -(-slab // BLOCK)
    cut = max(1, min(blocks - 1, round(FIRST * blocks))) * BLOCK
    sent, widths = [], []
    for low, high in ((0, cut), (cut, slab)):
        widths.append(-(-(most + high - low) // LANES) * LANES)
        sent.append(windows(amplitudes, [b + low for b in begins], widths[-1]))
    here = lax.all_to_all(sent[0], ALL, split_axis=0, concat_axis=0, tiled=True)
    kept = lax.slice(flat, (0, cut), (rows, slab))
    later, here, kept = lax.optimization_barrier((sent[1], here, kept))
    late = lax.all_to_all(later, ALL, split_axis=0, concat_axis=0, tiled=True)
    pairs = count * pair_local
    here, late = here.reshape(pairs, widths[0]), late.reshape(pairs, widths[1])
    total = products(shift, here, flat, cut, late, kept)

    part = total.reshape(z, x, core, col, pair_local, rows)
    part = exchange_sum(part.transpose(2, 0, 1, 3, 4, 5).reshape(core, z, x * col, pair_local, rows), "core")
    part = exchange_sum(part.transpose(1, 0, 2, 3), ("x", "col"))
    part = exchange_sum(part, "z")
    return part.reshape(pair_local, window, virtuals)


def solution(mesh):
    devices = mesh.devices
    row, col = devices.shape
    split = Mesh(devices.reshape(row // 4, 2, 2, col), ALL)
    return jax.shard_map(
        shards,
        mesh=split,
        in_specs=(P(ALL, None), P(None, None, ALL)),
        out_specs=P(ALL, None, None),
        check_vma=False,
    )
```

time: 122 us -> 112 us (0.918)
  blocking collectives: 82.7 us -> 0 us
  waiting for transfers between devices: 0 us -> 38.6 us
  matrix products: 25.9 us -> 0 us
  Pallas kernels: 0 us -> 24.5 us
  starting transfers between devices: 0 us -> 19.4 us
  local copies, waits for them, and re-layouts: 12.6 us -> 28.8 us
    all_to_all x2 -> x0, blocking collectives: 82.7 us -> none  [the longest x1 66 us: shards(): lax.all_to_all(sectioned, BOTH, split_axis=0, concat_axis=0, tiled=True)]
    all_to_all x0 -> x2, waiting for transfers between devices: none -> 27.6 us  [the longest x1 27.6 us: shards(): here = lax.all_to_all(sent[0], ALL, split_axis=0, concat_axis=0, tiled=True)]
    dot_general x1 -> x0, matrix products: 25.9 us -> none  [shards(): lax.dot_general(local_amps, integrals.reshape(window * virtuals, slab), (...]
    pallas_call x0 -> x4, Pallas kernels: none -> 24.5 us  [the longest x1 17.4 us: products(): pl.pallas_call(functools.partial(first_kernel, cut // BLOCK), out_shape=t...]
    slice x0 -> x1, local copies, waits for them, and re-layouts: none -> 14.2 us  [shards(): kept = lax.slice(flat, (0, cut), (rows, slab))]
    all_to_all x0 -> x2, starting transfers between devices: none -> 11.1 us  [the longest x1 7.41 us: shards(): here = lax.all_to_all(sent[0], ALL, split_axis=0, concat_axis=0, tiled=True)]
    ppermute x0 -> x7, waiting for transfers between devices: none -> 11 us  [exchange_sum(): terms.append(lax.ppermute(block, names, [(i, to(i)) for i in range(count)]))]
    ppermute x0 -> x7, starting transfers between devices: none -> 8.32 us  [exchange_sum(): terms.append(lax.ppermute(block, names, [(i, to(i)) for i in range(count)]))]
  transfers between devices with their start and end apart: 0 -> 9, of which waited for: 0 -> 7; matrix products, arithmetic and copies ran while one was open for 0% -> 16% of each run, Pallas kernels for 0% -> 16%
where the time goes in v6:
time: 112 us
  waiting for transfers between devices  38.6 us (34%)
  local copies, waits for them, and re-layouts  28.8 us (26%)
  Pallas kernels  24.5 us (22%)
  starting transfers between devices  19.4 us (17%)
    all_to_all x1, waiting for transfers between devices, shards(): here = lax.all_to_all(sent[0], ALL, split_axis=0, concat_axis=0, tiled=True)  27.6 us
    pallas_call x1, Pallas kernels, products(): pl.pallas_call(functools.partial(first_kernel, cut // BLOCK), out_shape=t...  17.4 us
    slice x1, local copies, waits for them, and re-layouts, shards(): kept = lax.slice(flat, (0, cut), (rows, slab))  14.2 us
    ppermute x7, waiting for transfers between devices, exchange_sum(): terms.append(lax.ppermute(block, names, [(i, to(i)) for i in range(count)]))  11 us
    unnamed x8, local copies, waits for them, and re-layouts  9.42 us
    ppermute x7, starting transfers between devices, exchange_sum(): terms.append(lax.ppermute(block, names, [(i, to(i)) for i in range(count)]))  8.32 us
    all_to_all x1, starting transfers between devices, shards(): here = lax.all_to_all(sent[0], ALL, split_axis=0, concat_axis=0, tiled=True)  7.41 us
    pallas_call x1, Pallas kernels, products(): pl.pallas_call(functools.partial(last_kernel, slab - cut), out_shape=tota...  5.98 us
  transfers between devices with their start and end apart: 9, of which 7 were waited for; matrix products, arithmetic and copies ran while one was open for 16% of the time, Pallas kernels for 16%

profile of v6, /device:TPU:0, one launch (start us, length us, event | category | flops | bytes accessed | tf_op | source)
XLA Modules:
  0.0 111.7 jit_solution(9623973209094579498)
XLA Ops:
  0.0 0.0 copy-start.1
  0.0 1.7 %copy-done.1 = bf16[2,640000]{1,0:T(2,128)(2,1)S(1)} copy-done((bf16[2,640000]{1,0:T(2,128)(2,1)S(1)}, bf16[2,640000]{1,0:T(2,128)(2,1)}, u32[]{:S(2)}) %copy-start.1) | copy-done | bytes 2560024
  1.7 0.1 windows.3
  1.8 0.0 copy-start.3
  1.9 1.2 %copy-done.3 = bf16[32,2,14208]{2,1,0:T(2,128)(2,1)} copy-done((bf16[32,2,14208]{2,1,0:T(2,128)(2,1)}, bf16[32,2,14208]{2,1,0:T(2,128)(2,1)S(1)}, u32[]{:S(2)}) %copy-start.3) | copy-done | bytes 1818648
  3.1 0.0 copy-start.2
  3.1 7.4 %all-to-all-start = ((bf16[32,2,14208]{2,1,0:T(2,128)(2,1)}), bf16[32,2,14208]{2,1,0:T(2,128)(2,1)}, u32[]{:S(2)}, u32[]{:S(2)}) async-start(bf16[32,2,14208]{2,1,0:T(2,128)(2,1)} %copy-done.3), calls=%async_computation | async-start | bytes 3637248 | tf_op jit(solution)/shard_map/all_to_all | solution.py:154
  10.5 0.0 copy-done.2
  10.5 0.9 windows.2
  11.4 14.2 %slice.4.kept_ref = bf16[1600,5920]{1,0:T(8,128)(2,1)} slice(bf16[1600,20000]{1,0:T(8,128)(2,1)} %bitcast.34), slice={[0:1600], [14080:20000]} | slice | bytes 37888000 | tf_op jit(solution)/shard_map/slice | solution.py:155
  25.7 27.6 %all-to-all-done = bf16[32,2,14208]{2,1,0:T(2,128)(2,1)} async-done(((bf16[32,2,14208]{2,1,0:T(2,128)(2,1)}), bf16[32,2,14208]{2,1,0:T(2,128)(2,1)}, u32[]{:S(2)}, u32[]{:S(2)}) %all-to-all-start) | async-done | bytes 1818656 | tf_op jit(solution)/shard_map/all_to_all | solution.py:154
  53.2 3.7 %all-to-all-start.1 = ((bf16[32,2,6016]{2,1,0:T(2,128)(2,1)}), bf16[32,2,6016]{2,1,0:T(2,128)(2,1)S(1)}, u32[]{:S(2)}, u32[]{:S(2)}) async-start(bf16[32,2,6016]{2,1,0:T(2,128)(2,1)} %windows.2), calls=%async_computation.1 | async-start | bytes 1540096 | tf_op jit(solution)/shard_map/all_to_all | solution.py:157
  56.9 0.1 pad_add_fusion.off_ref
  57.0 3.9 %reshape.28.amps_ref = bf16[64,14208]{1,0:T(8,128)(2,1)S(1)} reshape(bf16[32,2,14208]{2,1,0:T(2,128)(2,1)} %all-to-all-done) | data formatting | bytes 3637248 | tf_op jit(solution)/shard_map/reshape | solution.py:159
  60.9 17.4 %first_product.1.sum_ref = f32[64,1600]{1,0:T(8,128)S(1)} custom-call(s32[2]{0:T(128)S(1)} %pad_add_fusion.off_ref, bf16[64,14208]{1,0:T(8,128)(2,1)S(1)} %reshape.28.amps_ref, bf16[1600,20000]{1,0:T(8,128)(2,1)} %bitcast.35), custom_call_target="tpu_custom_call" | custom-call | flops 2883584000 | bytes 45056000 | tf_op jit(solution)/shard_map/first_product/pallas_call | solution.py:96
  78.3 0.0 all-to-all-done.1
  78.3 0.3 reshape.27.amps_ref
  78.6 0.0 copy-start
  78.6 6.5 %copy-done = bf16[1600,5920]{1,0:T(8,128)(2,1)S(1)} copy-done((bf16[1600,5920]{1,0:T(8,128)(2,1)S(1)}, bf16[1600,5920]{1,0:T(8,128)(2,1)}, u32[]{:S(2)}) %copy-start) | copy-done | bytes 18944024
  85.1 6.0 %last_product.1 = f32[64,1600]{1,0:T(8,128)S(1)} custom-call(s32[2]{0:T(128)S(1)} %pad_add_fusion.off_ref, bf16[64,6016]{1,0:T(8,128)(2,1)S(1)} %reshape.27.amps_ref, bf16[1600,5920]{1,0:T(8,128)(2,1)S(1)} %copy-done, f32[64,1600]{1,0:T(8,128)S(1)} %first_product.1.sum_ref), custom_call_target="tpu_custom_call" | custom-call | flops 1212416000 | bytes 18944000 | tf_op jit(solution)/shard_map/last_product/pallas_call | solution.py:108
  91.1 0.2 reshape.29
  91.4 0.3 collective-permute-start
  91.7 1.2 %collective-permute-done = f32[4,4,2,1600]{3,2,1,0:T(2,128)S(1)} collective-permute-done((f32[4,4,2,1600]{3,2,1,0:T(2,128)S(1)}, f32[4,4,2,1600]{3,2,1,0:T(2,128)S(1)}, u32[]{:S(2)}, u32[]{:S(2)}) %collective-permute-start) | collective-permute-done | bytes 204832 | tf_op jit(solution)/shard_map/ppermute | solution.py:130
  92.9 0.1 bitcast_add_fusion
  93.1 1.8 %collective-permute-start.3 = (f32[4,2,1600]{2,1,0:T(2,128)S(1)}, f32[4,2,1600]{2,1,0:T(2,128)S(1)}, u32[]{:S(2)}, u32[]{:S(2)}) collective-permute-start(f32[4,2,1600]{2,1,0:T(2,128)S(1)} %get-tuple-element.12), channel_id=1, source_target_pairs={{0,1},{1,0},{4,5},{5,4},{2,3},{3,2},{6,7},{7,6},{8,9},{9,8},{12,13... | collective-permute-start | bytes 153608 | tf_op jit(solution)/shard_map/ppermute | solution.py:130
  94.9 1.5 %collective-permute-start.2 = (f32[4,2,1600]{2,1,0:T(2,128)S(1)}, f32[4,2,1600]{2,1,0:T(2,128)S(1)}, u32[]{:S(2)}, u32[]{:S(2)}) collective-permute-start(f32[4,2,1600]{2,1,0:T(2,128)S(1)} %get-tuple-element.13), channel_id=1, source_target_pairs={{0,4},{1,5},{4,0},{5,1},{2,6},{3,7},{6,2},{7,3},{8,12},{9,13},{12,... | collective-permute-start | bytes 153608 | tf_op jit(solution)/shard_map/ppermute | solution.py:130
  96.4 0.3 collective-permute-start.1
  96.6 0.6 collective-permute-done.3
  97.3 2.2 %collective-permute-done.2 = f32[4,2,1600]{2,1,0:T(2,128)S(1)} collective-permute-done((f32[4,2,1600]{2,1,0:T(2,128)S(1)}, f32[4,2,1600]{2,1,0:T(2,128)S(1)}, u32[]{:S(2)}, u32[]{:S(2)}) %collective-permute-start.2) | collective-permute-done | bytes 51232 | tf_op jit(solution)/shard_map/ppermute | solution.py:130
  99.5 1.9 %collective-permute-done.1 = f32[4,2,1600]{2,1,0:T(2,128)S(1)} collective-permute-done((f32[4,2,1600]{2,1,0:T(2,128)S(1)}, f32[4,2,1600]{2,1,0:T(2,128)S(1)}, u32[]{:S(2)}, u32[]{:S(2)}) %collective-permute-start.1) | collective-permute-done | bytes 51232 | tf_op jit(solution)/shard_map/ppermute | solution.py:130
  101.4 0.1 fusion.1
  101.5 1.5 %collective-permute-start.6 = (f32[2,1600]{1,0:T(2,128)S(1)}, f32[2,1600]{1,0:T(2,128)S(1)}, u32[]{:S(2)}, u32[]{:S(2)}) collective-permute-start(f32[2,1600]{1,0:T(2,128)S(1)} %get-tuple-element.15), channel_id=1, source_target_pairs={{0,8},{8,0},{16,24},{24,16},{1,9},{9,1},{17,25},{25,17},{2,10},{10... | collective-permute-start | bytes 38408 | tf_op jit(solution)/shard_map/ppermute | solution.py:130
  103.0 2.5 %collective-permute-start.5 = (f32[2,1600]{1,0:T(2,128)S(1)}, f32[2,1600]{1,0:T(2,128)S(1)}, u32[]{:S(2)}, u32[]{:S(2)}) collective-permute-start(f32[2,1600]{1,0:T(2,128)S(1)} %get-tuple-element.16), channel_id=1, source_target_pairs={{0,16},{8,24},{16,0},{24,8},{1,17},{9,25},{17,1},{25,9},{2,18},{10... | collective-permute-start | bytes 38408 | tf_op jit(solution)/shard_map/ppermute | solution.py:130
  105.5 0.5 collective-permute-start.4
  105.9 0.0 collective-permute-done.6
  105.9 2.0 %collective-permute-done.5 = f32[2,1600]{1,0:T(2,128)S(1)} collective-permute-done((f32[2,1600]{1,0:T(2,128)S(1)}, f32[2,1600]{1,0:T(2,128)S(1)}, u32[]{:S(2)}, u32[]{:S(2)}) %collective-permute-start.5) | collective-permute-done | bytes 12832 | tf_op jit(solution)/shard_map/ppermute | solution.py:130
  107.9 3.1 %collective-permute-done.4 = f32[2,1600]{1,0:T(2,128)S(1)} collective-permute-done((f32[2,1600]{1,0:T(2,128)S(1)}, f32[2,1600]{1,0:T(2,128)S(1)}, u32[]{:S(2)}, u32[]{:S(2)}) %collective-permute-start.4) | collective-permute-done | bytes 12832 | tf_op jit(solution)/shard_map/ppermute | solution.py:130
  111.0 0.7 reshape.31
  (5 shorter events, 0.1 us)
Async XLA Ops:
  0.0 1.7 %copy-start.1 = (bf16[2,640000]{1,0:T(2,128)(2,1)S(1)}, bf16[2,640000]{1,0:T(2,128)(2,1)}, u32[]{:S(2)}) copy-start(bf16[2,640000]{1,0:T(2,128)(2,1)} %x_ref.3) | copy-start | bytes 7680004
  1.8 1.2 %copy-start.3 = (bf16[32,2,14208]{2,1,0:T(2,128)(2,1)}, bf16[32,2,14208]{2,1,0:T(2,128)(2,1)S(1)}, u32[]{:S(2)}) copy-start(bf16[32,2,14208]{2,1,0:T(2,128)(2,1)S(1)} %windows.3) | copy-start | bytes 5455876
  3.1 7.4 %copy-start.2 = (bf16[2,640000]{1,0:T(2,128)(2,1)S(1)}, bf16[2,640000]{1,0:T(2,128)(2,1)}, u32[]{:S(2)}) copy-start(bf16[2,640000]{1,0:T(2,128)(2,1)} %x_ref.3) | copy-start | bytes 7680004
  3.1 50.1 %all-to-all-start = ((bf16[32,2,14208]{2,1,0:T(2,128)(2,1)}), bf16[32,2,14208]{2,1,0:T(2,128)(2,1)}, u32[]{:S(2)}, u32[]{:S(2)}) async-start(bf16[32,2,14208]{2,1,0:T(2,128)(2,1)} %copy-done.3), calls=%async_computation | async-start | bytes 3637248 | tf_op jit(solution)/shard_map/all_to_all | solution.py:154
  53.2 25.1 %all-to-all-start.1 = ((bf16[32,2,6016]{2,1,0:T(2,128)(2,1)}), bf16[32,2,6016]{2,1,0:T(2,128)(2,1)S(1)}, u32[]{:S(2)}, u32[]{:S(2)}) async-start(bf16[32,2,6016]{2,1,0:T(2,128)(2,1)} %windows.2), calls=%async_computation.1 | async-start | bytes 1540096 | tf_op jit(solution)/shard_map/all_to_all | solution.py:157
  78.6 6.5 %copy-start = (bf16[1600,5920]{1,0:T(8,128)(2,1)S(1)}, bf16[1600,5920]{1,0:T(8,128)(2,1)}, u32[]{:S(2)}) copy-start(bf16[1600,5920]{1,0:T(8,128)(2,1)} %slice.4.kept_ref) | copy-start | bytes 56832004
  91.4 1.5 %collective-permute-start = (f32[4,4,2,1600]{3,2,1,0:T(2,128)S(1)}, f32[4,4,2,1600]{3,2,1,0:T(2,128)S(1)}, u32[]{:S(2)}, u32[]{:S(2)}) collective-permute-start(f32[4,4,2,1600]{3,2,1,0:T(2,128)S(1)} %dynamic-slice_bitcast_fusion), channel_id=1, source_target_pairs={{0,2},{2,0},{1,3},{3,1},{4,6},{6,4},{5,7},{7,5},{8,10},{10,8},{9,1... | collective-permute-start | bytes 614408 | tf_op jit(solution)/shard_map/ppermute | solution.py:130
  93.1 4.2 %collective-permute-start.3 = (f32[4,2,1600]{2,1,0:T(2,128)S(1)}, f32[4,2,1600]{2,1,0:T(2,128)S(1)}, u32[]{:S(2)}, u32[]{:S(2)}) collective-permute-start(f32[4,2,1600]{2,1,0:T(2,128)S(1)} %get-tuple-element.12), channel_id=1, source_target_pairs={{0,1},{1,0},{4,5},{5,4},{2,3},{3,2},{6,7},{7,6},{8,9},{9,8},{12,13... | collective-permute-start | bytes 153608 | tf_op jit(solution)/shard_map/ppermute | solution.py:130
  94.9 4.6 %collective-permute-start.2 = (f32[4,2,1600]{2,1,0:T(2,128)S(1)}, f32[4,2,1600]{2,1,0:T(2,128)S(1)}, u32[]{:S(2)}, u32[]{:S(2)}) collective-permute-start(f32[4,2,1600]{2,1,0:T(2,128)S(1)} %get-tuple-element.13), channel_id=1, source_target_pairs={{0,4},{1,5},{4,0},{5,1},{2,6},{3,7},{6,2},{7,3},{8,12},{9,13},{12,... | collective-permute-start | bytes 153608 | tf_op jit(solution)/shard_map/ppermute | solution.py:130
  96.4 5.0 %collective-permute-start.1 = (f32[4,2,1600]{2,1,0:T(2,128)S(1)}, f32[4,2,1600]{2,1,0:T(2,128)S(1)}, u32[]{:S(2)}, u32[]{:S(2)}) collective-permute-start(f32[4,2,1600]{2,1,0:T(2,128)S(1)} %get-tuple-element.11), channel_id=1, source_target_pairs={{0,5},{1,4},{4,1},{5,0},{2,7},{3,6},{6,3},{7,2},{8,13},{9,12},{12,... | collective-permute-start | bytes 153608 | tf_op jit(solution)/shard_map/ppermute | solution.py:130
  101.5 4.5 %collective-permute-start.6 = (f32[2,1600]{1,0:T(2,128)S(1)}, f32[2,1600]{1,0:T(2,128)S(1)}, u32[]{:S(2)}, u32[]{:S(2)}) collective-permute-start(f32[2,1600]{1,0:T(2,128)S(1)} %get-tuple-element.15), channel_id=1, source_target_pairs={{0,8},{8,0},{16,24},{24,16},{1,9},{9,1},{17,25},{25,17},{2,10},{10... | collective-permute-start | bytes 38408 | tf_op jit(solution)/shard_map/ppermute | solution.py:130
  103.0 4.9 %collective-permute-start.5 = (f32[2,1600]{1,0:T(2,128)S(1)}, f32[2,1600]{1,0:T(2,128)S(1)}, u32[]{:S(2)}, u32[]{:S(2)}) collective-permute-start(f32[2,1600]{1,0:T(2,128)S(1)} %get-tuple-element.16), channel_id=1, source_target_pairs={{0,16},{8,24},{16,0},{24,8},{1,17},{9,25},{17,1},{25,9},{2,18},{10... | collective-permute-start | bytes 38408 | tf_op jit(solution)/shard_map/ppermute | solution.py:130
  105.5 5.5 %collective-permute-start.4 = (f32[2,1600]{1,0:T(2,128)S(1)}, f32[2,1600]{1,0:T(2,128)S(1)}, u32[]{:S(2)}, u32[]{:S(2)}) collective-permute-start(f32[2,1600]{1,0:T(2,128)S(1)} %get-tuple-element.14), channel_id=1, source_target_pairs={{0,24},{8,16},{16,8},{24,0},{1,25},{9,17},{17,9},{25,1},{2,26},{10... | collective-permute-start | bytes 38408 | tf_op jit(solution)/shard_map/ppermute | solution.py:130

commit v7 on v6

--- a/solution.py
+++ b/solution.py
@@ -11,6 +11,7 @@
 LANES = 128
 BLOCK = 1280
 BUFFERS = 3
+AHEAD = 2
 LIMIT = 20 * 1024 * 1024
 FIRST = 0.7
 
@@ -68,25 +69,31 @@
     out_ref[...] = acc_ref[...].T
 
 
-def last_kernel(width, off_ref, amps_ref, kept_ref, sum_ref, out_ref, acc_ref):
+def last_kernel(pieces, off_ref, amps_ref, ints_hbm, sum_ref, out_ref, acc_ref, sems, *buffers):
+    low = pieces[0][0]
+    copies = [
+        pltpu.make_async_copy(
+            ints_hbm.at[:, pl.ds(start, size)], buffers[i], sems.at[i]
+        )
+        for i, (start, size) in enumerate(pieces)
+    ]
+    for copy in copies[:AHEAD]:
+        copy.start()
     acc_ref[...] = jnp.zeros_like(acc_ref)
     have = amps_ref.shape[1] // LANES
-    for base in range(0, width, BLOCK):
-        size = min(BLOCK, width - base)
+    for i, (start, size) in enumerate(pieces):
+        base = start - low
         count = -(-size // LANES)
         parts = shifted(off_ref, amps_ref, base, count, have - base // LANES)
-        whole = size // LANES
-        if whole:
-            amps = jnp.concatenate([p.astype(jnp.bfloat16) for p in parts[:whole]], axis=1)
-            acc_ref[...] += dot(kept_ref[:, pl.ds(base, whole * LANES)], amps)
-        if whole < count:
-            valid = size - whole * LANES
-            amps = parts[whole].astype(jnp.bfloat16)[:, :valid]
-            acc_ref[...] += dot(kept_ref[:, pl.ds(base + whole * LANES, valid)], amps)
+        amps = jnp.concatenate([p.astype(jnp.bfloat16) for p in parts], axis=1)[:, :size]
+        copies[i].wait()
+        if i + AHEAD < len(copies):
+            copies[i + AHEAD].start()
+        acc_ref[...] += dot(buffers[i][...], amps)
     out_ref[...] = acc_ref[...].T + sum_ref[...]
 
 
-def products(shift, amps, flat, cut, late, kept):
+def products(shift, amps, flat, cut, late):
     pairs = amps.shape[0]
     rows, slab = flat.shape
     vmem = pl.BlockSpec(memory_space=pltpu.VMEM)
@@ -105,18 +112,26 @@
         ),
         name="first_product",
     )(shift, amps, flat)
+    pieces = [(cut, min(BLOCK // 2, slab - cut))]
+    while sum(pieces[-1]) < slab:
+        start = sum(pieces[-1])
+        pieces.append((start, min(BLOCK, slab - start)))
     return pl.pallas_call(
-        functools.partial(last_kernel, slab - cut),
+        functools.partial(last_kernel, pieces),
         out_shape=total,
-        in_specs=[smem, vmem, vmem, vmem],
+        in_specs=[smem, vmem, pl.BlockSpec(memory_space=pl.ANY), vmem],
         out_specs=vmem,
-        scratch_shapes=acc,
-        compiler_params=pltpu.CompilerParams(vmem_limit_bytes=LIMIT),
+        scratch_shapes=acc
+        + [pltpu.SemaphoreType.DMA((len(pieces),))]
+        + [pltpu.VMEM((rows, size), flat.dtype) for _, size in pieces],
+        compiler_params=pltpu.CompilerParams(vmem_limit_bytes=36 * 1024 * 1024),
         cost_estimate=pl.CostEstimate(
-            flops=2 * pairs * rows * (slab - cut), bytes_accessed=2 * rows * (slab - cut), transcendentals=0
+            flops=2 * pairs * rows * (slab - cut),
+            bytes_accessed=2 * rows * (slab - cut),
+            transcendentals=0,
         ),
         name="last_product",
-    )(shift, late, kept, first)
+    )(shift, late, flat, first)
 
 
 def exchange_sum(blocks, names):
@@ -152,17 +167,17 @@
         widths.append(-(-(most + high - low) // LANES) * LANES)
         sent.append(windows(amplitudes, [b + low for b in begins], widths[-1]))
     here = lax.all_to_all(sent[0], ALL, split_axis=0, concat_axis=0, tiled=True)
-    kept = lax.slice(flat, (0, cut), (rows, slab))
-    later, here, kept = lax.optimization_barrier((sent[1], here, kept))
+    later, here = lax.optimization_barrier((sent[1], here))
     late = lax.all_to_all(later, ALL, split_axis=0, concat_axis=0, tiled=True)
     pairs = count * pair_local
     here, late = here.reshape(pairs, widths[0]), late.reshape(pairs, widths[1])
-    total = products(shift, here, flat, cut, late, kept)
+    total = products(shift, here, flat, cut, late)
 
     part = total.reshape(z, x, core, col, pair_local, rows)
     part = exchange_sum(part.transpose(2, 0, 1, 3, 4, 5).reshape(core, z, x * col, pair_local, rows), "core")
-    part = exchange_sum(part.transpose(1, 0, 2, 3), ("x", "col"))
-    part = exchange_sum(part, "z")
+    part = part.transpose(1, 0, 2, 3)
+    part = lax.all_to_all(part, ("x", "col"), split_axis=0, concat_axis=0, tiled=True).sum(axis=0)
+    part = lax.all_to_all(part, "z", split_axis=0, concat_axis=0, tiled=True).sum(axis=0)
     return part.reshape(pair_local, window, virtuals)
 
 

time: 112 us -> 111 us (level)
  local copies, waits for them, and re-layouts: 28.8 us -> 8.12 us
  blocking collectives: 0 us -> 19.5 us
  starting transfers between devices: 19.4 us -> 11.4 us
  waiting for transfers between devices: 38.6 us -> 43 us
  Pallas kernels: 24.5 us -> 28.4 us
    all_to_all x0 -> x2, blocking collectives: none -> 19.5 us  [the longest x1 10.1 us: shards(): lax.all_to_all(part, 'z', split_axis=0, concat_axis=0, tiled=True)]
    slice x1 -> x0, local copies, waits for them, and re-layouts: 14.2 us -> none  [shards(): kept = lax.slice(flat, (0, cut), (rows, slab))]
    all_to_all x1, waiting for transfers between devices: 27.6 us -> 41.8 us  [shards(): here = lax.all_to_all(sent[0], ALL, split_axis=0, concat_axis=0, tiled=True)]
    ppermute x7 -> x1, waiting for transfers between devices: 11 us -> 1.2 us  [exchange_sum(): terms.append(lax.ppermute(block, names, [(i, to(i)) for i in range(count)]))]
    ppermute x7 -> x1, starting transfers between devices: 8.32 us -> 0.33 us  [exchange_sum(): terms.append(lax.ppermute(block, names, [(i, to(i)) for i in range(count)]))]
    unnamed x8 -> x6, local copies, waits for them, and re-layouts: 9.42 us -> 2.94 us
    pallas_call x1, Pallas kernels: 5.98 us -> 9.91 us  [products(): pl.pallas_call(functools.partial(last_kernel, pieces), out_shape=total, i...]
  transfers between devices with their start and end apart: 9 -> 3, of which waited for: 7 -> 2; matrix products, arithmetic and copies ran while one was open for 16% -> 4% of each run, Pallas kernels for 16% -> 17%
where the time goes in v7:
time: 111 us
  waiting for transfers between devices  43 us (39%)
  Pallas kernels  28.4 us (26%)
  blocking collectives  19.5 us (18%)
  starting transfers between devices  11.4 us (10%)
  local copies, waits for them, and re-layouts  8.12 us (7%)
    all_to_all x1, waiting for transfers between devices, shards(): here = lax.all_to_all(sent[0], ALL, split_axis=0, concat_axis=0, tiled=True)  41.8 us
    pallas_call x1, Pallas kernels, products(): pl.pallas_call(functools.partial(first_kernel, cut // BLOCK), out_shape=t...  17.4 us
    all_to_all x1, blocking collectives, shards(): lax.all_to_all(part, 'z', split_axis=0, concat_axis=0, tiled=True)  10.1 us
    pallas_call x1, Pallas kernels, products(): pl.pallas_call(functools.partial(last_kernel, pieces), out_shape=total, i...  9.91 us
    all_to_all x1, blocking collectives, shards(): lax.all_to_all(part, ('x', 'col'), split_axis=0, concat_axis=0, tiled=True)  9.37 us
    all_to_all x1, starting transfers between devices, shards(): here = lax.all_to_all(sent[0], ALL, split_axis=0, concat_axis=0, tiled=True)  7.41 us
    reshape x1, local copies, waits for them, and re-layouts, shards(): here.reshape(pairs, widths[0])  3.86 us
    all_to_all x1, starting transfers between devices, shards(): late = lax.all_to_all(later, ALL, split_axis=0, concat_axis=0, tiled=True)  3.66 us
  transfers between devices with their start and end apart: 3, of which 2 were waited for; matrix products, arithmetic and copies ran while one was open for 4% of the time, Pallas kernels for 17%

profile of v7, /device:TPU:0, one launch (start us, length us, event | category | flops | bytes accessed | tf_op | source)
XLA Modules:
  0.0 110.8 jit_solution(2647725413758651509)
XLA Ops:
  0.0 0.0 copy-start
  0.0 1.7 %copy-done = bf16[2,640000]{1,0:T(2,128)(2,1)S(1)} copy-done((bf16[2,640000]{1,0:T(2,128)(2,1)S(1)}, bf16[2,640000]{1,0:T(2,128)(2,1)}, u32[]{:S(2)}) %copy-start) | copy-done | bytes 2560024
  1.7 0.1 windows.3
  1.8 0.0 copy-start.2
  1.9 1.2 %copy-done.2 = bf16[32,2,14208]{2,1,0:T(2,128)(2,1)} copy-done((bf16[32,2,14208]{2,1,0:T(2,128)(2,1)}, bf16[32,2,14208]{2,1,0:T(2,128)(2,1)S(1)}, u32[]{:S(2)}) %copy-start.2) | copy-done | bytes 1818648
  3.1 0.0 copy-start.1
  3.1 7.4 %all-to-all-start = ((bf16[32,2,14208]{2,1,0:T(2,128)(2,1)}), bf16[32,2,14208]{2,1,0:T(2,128)(2,1)}, u32[]{:S(2)}, u32[]{:S(2)}) async-start(bf16[32,2,14208]{2,1,0:T(2,128)(2,1)} %copy-done.2), calls=%async_computation | async-start | bytes 3637248 | tf_op jit(solution)/shard_map/all_to_all | solution.py:169
  10.5 0.0 copy-done.1
  10.5 0.9 windows.2
  11.4 41.8 %all-to-all-done = bf16[32,2,14208]{2,1,0:T(2,128)(2,1)} async-done(((bf16[32,2,14208]{2,1,0:T(2,128)(2,1)}), bf16[32,2,14208]{2,1,0:T(2,128)(2,1)}, u32[]{:S(2)}, u32[]{:S(2)}) %all-to-all-start) | async-done | bytes 1818656 | tf_op jit(solution)/shard_map/all_to_all | solution.py:169
  53.2 3.7 %all-to-all-start.1 = ((bf16[32,2,6016]{2,1,0:T(2,128)(2,1)}), bf16[32,2,6016]{2,1,0:T(2,128)(2,1)S(1)}, u32[]{:S(2)}, u32[]{:S(2)}) async-start(bf16[32,2,6016]{2,1,0:T(2,128)(2,1)} %windows.2), calls=%async_computation.1 | async-start | bytes 1540096 | tf_op jit(solution)/shard_map/all_to_all | solution.py:171
  56.9 0.1 pad_add_fusion.off_ref
  57.0 3.9 %reshape.20.amps_ref = bf16[64,14208]{1,0:T(8,128)(2,1)S(1)} reshape(bf16[32,2,14208]{2,1,0:T(2,128)(2,1)} %all-to-all-done) | data formatting | bytes 3637248 | tf_op jit(solution)/shard_map/reshape | solution.py:173
  60.8 17.4 %first_product.1.sum_ref = f32[64,1600]{1,0:T(8,128)S(1)} custom-call(s32[2]{0:T(128)S(1)} %pad_add_fusion.off_ref, bf16[64,14208]{1,0:T(8,128)(2,1)S(1)} %reshape.20.amps_ref, bf16[1600,20000]{1,0:T(8,128)(2,1)} %bitcast.14), custom_call_target="tpu_custom_call" | custom-call | flops 2883584000 | bytes 45056000 | tf_op jit(solution)/shard_map/first_product/pallas_call | solution.py:103
  78.3 0.0 all-to-all-done.1
  78.3 0.3 reshape.18.amps_ref
  78.6 9.9 %last_product.1 = f32[64,1600]{1,0:T(8,128)S(1)} custom-call(s32[2]{0:T(128)S(1)} %pad_add_fusion.off_ref, bf16[64,6016]{1,0:T(8,128)(2,1)S(1)} %reshape.18.amps_ref, bf16[1600,20000]{1,0:T(8,128)(2,1)} %bitcast.15, f32[64,1600]{1,0:T(8,128)S(1)} %first_product.1.sum_ref), custom_call_target="tpu_custom_call" | custom-call | flops 1212416000 | bytes 18944000 | tf_op jit(solution)/shard_map/last_product/pallas_call | solution.py:119
  88.5 0.2 reshape.21
  88.8 0.3 collective-permute-start
  89.2 1.2 %collective-permute-done = f32[4,4,2,1600]{3,2,1,0:T(2,128)S(1)} collective-permute-done((f32[4,4,2,1600]{3,2,1,0:T(2,128)S(1)}, f32[4,4,2,1600]{3,2,1,0:T(2,128)S(1)}, u32[]{:S(2)}, u32[]{:S(2)}) %collective-permute-start) | collective-permute-done | bytes 204832 | tf_op jit(solution)/shard_map/ppermute | solution.py:145
  90.4 0.1 fusion
  90.5 9.4 %all_to_all.20 = f32[4,4,2,1600]{3,2,1,0:T(2,128)S(1)} all-to-all(f32[4,4,2,1600]{3,2,1,0:T(2,128)S(1)} %copy.10), channel_id=1, replica_groups=mesh['z'=4,'x'=2,'core'=2,'col'=2] {'x','col'}, dimensions={0} | all-to-all | bytes 409600 | tf_op jit(solution)/shard_map/all_to_all | solution.py:179
  99.9 0.1 reduce_sum.18
  100.0 10.1 %all_to_all.21 = f32[4,2,1600]{2,1,0:T(2,128)S(1)} all-to-all(f32[4,2,1600]{2,1,0:T(2,128)S(1)} %reduce_sum.18), channel_id=1, replica_groups=mesh['z'=4,'x'=2,'core'=2,'col'=2] {'z'}, dimensions={0} | all-to-all | bytes 102400 | tf_op jit(solution)/shard_map/all_to_all | solution.py:180
  110.1 0.7 reshape.23
  (4 shorter events, 0.1 us)
Async XLA Ops:
  0.0 1.7 %copy-start = (bf16[2,640000]{1,0:T(2,128)(2,1)S(1)}, bf16[2,640000]{1,0:T(2,128)(2,1)}, u32[]{:S(2)}) copy-start(bf16[2,640000]{1,0:T(2,128)(2,1)} %x_ref.3) | copy-start | bytes 7680004
  1.8 1.2 %copy-start.2 = (bf16[32,2,14208]{2,1,0:T(2,128)(2,1)}, bf16[32,2,14208]{2,1,0:T(2,128)(2,1)S(1)}, u32[]{:S(2)}) copy-start(bf16[32,2,14208]{2,1,0:T(2,128)(2,1)S(1)} %windows.3) | copy-start | bytes 5455876
  3.1 7.4 %copy-start.1 = (bf16[2,640000]{1,0:T(2,128)(2,1)S(1)}, bf16[2,640000]{1,0:T(2,128)(2,1)}, u32[]{:S(2)}) copy-start(bf16[2,640000]{1,0:T(2,128)(2,1)} %x_ref.3) | copy-start | bytes 7680004
  3.1 50.1 %all-to-all-start = ((bf16[32,2,14208]{2,1,0:T(2,128)(2,1)}), bf16[32,2,14208]{2,1,0:T(2,128)(2,1)}, u32[]{:S(2)}, u32[]{:S(2)}) async-start(bf16[32,2,14208]{2,1,0:T(2,128)(2,1)} %copy-done.2), calls=%async_computation | async-start | bytes 3637248 | tf_op jit(solution)/shard_map/all_to_all | solution.py:169
  53.2 25.1 %all-to-all-start.1 = ((bf16[32,2,6016]{2,1,0:T(2,128)(2,1)}), bf16[32,2,6016]{2,1,0:T(2,128)(2,1)S(1)}, u32[]{:S(2)}, u32[]{:S(2)}) async-start(bf16[32,2,6016]{2,1,0:T(2,128)(2,1)} %windows.2), calls=%async_computation.1 | async-start | bytes 1540096 | tf_op jit(solution)/shard_map/all_to_all | solution.py:171
  88.8 1.5 %collective-permute-start = (f32[4,4,2,1600]{3,2,1,0:T(2,128)S(1)}, f32[4,4,2,1600]{3,2,1,0:T(2,128)S(1)}, u32[]{:S(2)}, u32[]{:S(2)}) collective-permute-start(f32[4,4,2,1600]{3,2,1,0:T(2,128)S(1)} %dynamic-slice_bitcast_fusion), channel_id=1, source_target_pairs={{0,2},{2,0},{1,3},{3,1},{4,6},{6,4},{5,7},{7,5},{8,10},{10,8},{9,1... | collective-permute-start | bytes 614408 | tf_op jit(solution)/shard_map/ppermute | solution.py:145

commit v8 on v7

--- a/solution.py
+++ b/solution.py
@@ -5,13 +5,13 @@
 from jax import lax
 from jax.experimental import pallas as pl
 from jax.experimental.pallas import tpu as pltpu
-from jax.sharding import Mesh, PartitionSpec as P
+from jax.sharding import PartitionSpec as P
 
-ALL = ("z", "x", "core", "col")
+ALL = ("row", "col")
 LANES = 128
 BLOCK = 1280
 BUFFERS = 3
-AHEAD = 2
+PIECE = 768
 LIMIT = 20 * 1024 * 1024
 FIRST = 0.7
 
@@ -77,7 +77,7 @@
         )
         for i, (start, size) in enumerate(pieces)
     ]
-    for copy in copies[:AHEAD]:
+    for copy in copies:
         copy.start()
     acc_ref[...] = jnp.zeros_like(acc_ref)
     have = amps_ref.shape[1] // LANES
@@ -87,8 +87,6 @@
         parts = shifted(off_ref, amps_ref, base, count, have - base // LANES)
         amps = jnp.concatenate([p.astype(jnp.bfloat16) for p in parts], axis=1)[:, :size]
         copies[i].wait()
-        if i + AHEAD < len(copies):
-            copies[i + AHEAD].start()
         acc_ref[...] += dot(buffers[i][...], amps)
     out_ref[...] = acc_ref[...].T + sum_ref[...]
 
@@ -112,10 +110,7 @@
         ),
         name="first_product",
     )(shift, amps, flat)
-    pieces = [(cut, min(BLOCK // 2, slab - cut))]
-    while sum(pieces[-1]) < slab:
-        start = sum(pieces[-1])
-        pieces.append((start, min(BLOCK, slab - start)))
+    pieces = [(start, min(PIECE, slab - start)) for start in range(cut, slab, PIECE)]
     return pl.pallas_call(
         functools.partial(last_kernel, pieces),
         out_shape=total,
@@ -134,21 +129,8 @@
     )(shift, late, flat, first)
 
 
-def exchange_sum(blocks, names):
-    count = blocks.shape[0]
-    me = lax.axis_index(names)
-    terms = [lax.dynamic_index_in_dim(blocks, me, 0, keepdims=False)]
-    power = count & (count - 1) == 0
-    for step in range(count - 1, 0, -1):
-        to = (lambda i: i ^ step) if power else (lambda i: (i + step) % count)
-        block = lax.dynamic_index_in_dim(blocks, to(me), 0, keepdims=False)
-        terms.append(lax.ppermute(block, names, [(i, to(i)) for i in range(count)]))
-    return sum(terms[1:], terms[0])
-
-
 def shards(amplitudes, integrals):
-    z, x, core, col = (lax.axis_size(name) for name in ALL)
-    count = z * x * core * col
+    count = lax.axis_size("row") * lax.axis_size("col")
     pair_local, full_width = amplitudes.shape
     slab = full_width // count
     window, virtuals, _ = integrals.shape
@@ -173,21 +155,15 @@
     here, late = here.reshape(pairs, widths[0]), late.reshape(pairs, widths[1])
     total = products(shift, here, flat, cut, late)
 
-    part = total.reshape(z, x, core, col, pair_local, rows)
-    part = exchange_sum(part.transpose(2, 0, 1, 3, 4, 5).reshape(core, z, x * col, pair_local, rows), "core")
-    part = part.transpose(1, 0, 2, 3)
-    part = lax.all_to_all(part, ("x", "col"), split_axis=0, concat_axis=0, tiled=True).sum(axis=0)
-    part = lax.all_to_all(part, "z", split_axis=0, concat_axis=0, tiled=True).sum(axis=0)
+    part = total.reshape(count, pair_local, rows)
+    part = lax.all_to_all(part, ALL, split_axis=0, concat_axis=0, tiled=True).sum(axis=0)
     return part.reshape(pair_local, window, virtuals)
 
 
 def solution(mesh):
-    devices = mesh.devices
-    row, col = devices.shape
-    split = Mesh(devices.reshape(row // 4, 2, 2, col), ALL)
     return jax.shard_map(
         shards,
-        mesh=split,
+        mesh=mesh,
         in_specs=(P(ALL, None), P(None, None, ALL)),
         out_specs=P(ALL, None, None),
         check_vma=False,

time: 111 us -> 110 us (level)
  waiting for transfers between devices: 43 us -> 41.8 us
    ppermute x1 -> x0, waiting for transfers between devices: 1.2 us -> none  [exchange_sum(): terms.append(lax.ppermute(block, names, [(i, to(i)) for i in range(count)]))]
    all_to_all x2 -> x1, blocking collectives: 19.5 us -> 18.9 us  [shards(): lax.all_to_all(part, ALL, split_axis=0, concat_axis=0, tiled=True)]
  transfers between devices with their start and end apart: 3 -> 2, of which waited for: 2 -> 1; matrix products, arithmetic and copies ran while one was open for 4% -> 4% of each run, Pallas kernels for 17% -> 17%
where the time goes in v8:
time: 110 us; the launch traced here: 109 us
  waiting for transfers between devices  41.8 us (38%)
  Pallas kernels  29.1 us (26%)
  blocking collectives  18.9 us (17%)
  starting transfers between devices  11.1 us (10%)
  local copies, waits for them, and re-layouts  8.04 us (7%)
    all_to_all x1, waiting for transfers between devices, shards(): here = lax.all_to_all(sent[0], ALL, split_axis=0, concat_axis=0, tiled=True)  41.8 us
    all_to_all x1, blocking collectives, shards(): lax.all_to_all(part, ALL, split_axis=0, concat_axis=0, tiled=True)  18.9 us
    pallas_call x1, Pallas kernels, products(): pl.pallas_call(functools.partial(first_kernel, cut // BLOCK), out_shape=t...  17.4 us
    pallas_call x1, Pallas kernels, products(): pl.pallas_call(functools.partial(last_kernel, pieces), out_shape=total, i...  10.6 us
    all_to_all x1, starting transfers between devices, shards(): here = lax.all_to_all(sent[0], ALL, split_axis=0, concat_axis=0, tiled=True)  7.41 us
    reshape x1, local copies, waits for them, and re-layouts, shards(): here.reshape(pairs, widths[0])  3.86 us
    all_to_all x1, starting transfers between devices, shards(): late = lax.all_to_all(later, ALL, split_axis=0, concat_axis=0, tiled=True)  3.66 us
    unnamed x6, local copies, waits for them, and re-layouts  2.95 us
  transfers between devices with their start and end apart: 2, of which 1 were waited for; matrix products, arithmetic and copies ran while one was open for 4% of the time, Pallas kernels for 17%

profile of v8, /device:TPU:0, one launch (start us, length us, event | category | flops | bytes accessed | tf_op | source)
XLA Modules:
  0.0 109.2 jit_solution(174692170158362750)
XLA Ops:
  0.0 0.0 copy-start
  0.0 1.7 %copy-done = bf16[2,640000]{1,0:T(2,128)(2,1)S(1)} copy-done((bf16[2,640000]{1,0:T(2,128)(2,1)S(1)}, bf16[2,640000]{1,0:T(2,128)(2,1)}, u32[]{:S(2)}) %copy-start) | copy-done | bytes 2560024
  1.7 0.1 windows.3
  1.8 0.0 copy-start.2
  1.9 1.2 %copy-done.2 = bf16[32,2,14208]{2,1,0:T(2,128)(2,1)} copy-done((bf16[32,2,14208]{2,1,0:T(2,128)(2,1)}, bf16[32,2,14208]{2,1,0:T(2,128)(2,1)S(1)}, u32[]{:S(2)}) %copy-start.2) | copy-done | bytes 1818648
  3.1 0.0 copy-start.1
  3.1 7.4 %all-to-all-start = ((bf16[32,2,14208]{2,1,0:T(2,128)(2,1)}), bf16[32,2,14208]{2,1,0:T(2,128)(2,1)}, u32[]{:S(2)}, u32[]{:S(2)}) async-start(bf16[32,2,14208]{2,1,0:T(2,128)(2,1)} %copy-done.2), calls=%async_computation | async-start | bytes 3637248 | tf_op jit(solution)/shard_map/all_to_all | solution.py:151
  10.5 0.0 copy-done.1
  10.5 0.9 windows.2
  11.4 41.8 %all-to-all-done = bf16[32,2,14208]{2,1,0:T(2,128)(2,1)} async-done(((bf16[32,2,14208]{2,1,0:T(2,128)(2,1)}), bf16[32,2,14208]{2,1,0:T(2,128)(2,1)}, u32[]{:S(2)}, u32[]{:S(2)}) %all-to-all-start) | async-done | bytes 1818656 | tf_op jit(solution)/shard_map/all_to_all | solution.py:151
  53.2 3.7 %all-to-all-start.1 = ((bf16[32,2,6016]{2,1,0:T(2,128)(2,1)}), bf16[32,2,6016]{2,1,0:T(2,128)(2,1)S(1)}, u32[]{:S(2)}, u32[]{:S(2)}) async-start(bf16[32,2,6016]{2,1,0:T(2,128)(2,1)} %windows.2), calls=%async_computation.1 | async-start | bytes 1540096 | tf_op jit(solution)/shard_map/all_to_all | solution.py:153
  56.9 0.1 pad_add_fusion.off_ref
  57.0 3.9 %reshape.17.amps_ref = bf16[64,14208]{1,0:T(8,128)(2,1)S(1)} reshape(bf16[32,2,14208]{2,1,0:T(2,128)(2,1)} %all-to-all-done) | data formatting | bytes 3637248 | tf_op jit(solution)/shard_map/reshape | solution.py:155
  60.8 17.4 %first_product.1.sum_ref = f32[64,1600]{1,0:T(8,128)S(1)} custom-call(s32[2]{0:T(128)S(1)} %pad_add_fusion.off_ref, bf16[64,14208]{1,0:T(8,128)(2,1)S(1)} %reshape.17.amps_ref, bf16[1600,20000]{1,0:T(8,128)(2,1)} %bitcast.3), custom_call_target="tpu_custom_call" | custom-call | flops 2883584000 | bytes 45056000 | tf_op jit(solution)/shard_map/first_product/pallas_call | solution.py:101
  78.3 0.0 all-to-all-done.1
  78.3 0.3 reshape.15.amps_ref
  78.6 10.6 %last_product.1 = f32[64,1600]{1,0:T(8,128)S(1)} custom-call(s32[2]{0:T(128)S(1)} %pad_add_fusion.off_ref, bf16[64,6016]{1,0:T(8,128)(2,1)S(1)} %reshape.15.amps_ref, bf16[1600,20000]{1,0:T(8,128)(2,1)} %bitcast.4, f32[64,1600]{1,0:T(8,128)S(1)} %first_product.1.sum_ref), custom_call_target="tpu_custom_call" | custom-call | flops 1212416000 | bytes 18944000 | tf_op jit(solution)/shard_map/last_product/pallas_call | solution.py:114
  89.2 0.2 reshape.18
  89.5 18.9 %all_to_all.15 = f32[32,2,1600]{2,1,0:T(2,128)S(1)} all-to-all(f32[32,2,1600]{2,1,0:T(2,128)S(1)} %reshape.18), channel_id=1, replica_groups=mesh['row'=16,'col'=2] {'row','col'}, dimensions={0} | all-to-all | bytes 819200 | tf_op jit(solution)/shard_map/all_to_all | solution.py:159
  108.4 0.1 reduce_sum.9
  108.5 0.7 reshape.19
Async XLA Ops:
  0.0 1.7 %copy-start = (bf16[2,640000]{1,0:T(2,128)(2,1)S(1)}, bf16[2,640000]{1,0:T(2,128)(2,1)}, u32[]{:S(2)}) copy-start(bf16[2,640000]{1,0:T(2,128)(2,1)} %x_ref.3) | copy-start | bytes 7680004
  1.8 1.2 %copy-start.2 = (bf16[32,2,14208]{2,1,0:T(2,128)(2,1)}, bf16[32,2,14208]{2,1,0:T(2,128)(2,1)S(1)}, u32[]{:S(2)}) copy-start(bf16[32,2,14208]{2,1,0:T(2,128)(2,1)S(1)} %windows.3) | copy-start | bytes 5455876
  3.1 7.4 %copy-start.1 = (bf16[2,640000]{1,0:T(2,128)(2,1)S(1)}, bf16[2,640000]{1,0:T(2,128)(2,1)}, u32[]{:S(2)}) copy-start(bf16[2,640000]{1,0:T(2,128)(2,1)} %x_ref.3) | copy-start | bytes 7680004
  3.1 50.1 %all-to-all-start = ((bf16[32,2,14208]{2,1,0:T(2,128)(2,1)}), bf16[32,2,14208]{2,1,0:T(2,128)(2,1)}, u32[]{:S(2)}, u32[]{:S(2)}) async-start(bf16[32,2,14208]{2,1,0:T(2,128)(2,1)} %copy-done.2), calls=%async_computation | async-start | bytes 3637248 | tf_op jit(solution)/shard_map/all_to_all | solution.py:151
  53.2 25.1 %all-to-all-start.1 = ((bf16[32,2,6016]{2,1,0:T(2,128)(2,1)}), bf16[32,2,6016]{2,1,0:T(2,128)(2,1)S(1)}, u32[]{:S(2)}, u32[]{:S(2)}) async-start(bf16[32,2,6016]{2,1,0:T(2,128)(2,1)} %windows.2), calls=%async_computation.1 | async-start | bytes 1540096 | tf_op jit(solution)/shard_map/all_to_all | solution.py:153

commit v9 on v7

--- a/solution.py
+++ b/solution.py
@@ -37,8 +37,8 @@
     )(x)
 
 
-def dot(ints, amps):
-    return lax.dot_general(ints, amps, (((1,), (1,)), ((), ())), preferred_element_type=jnp.float32)
+def dot(amps, ints):
+    return lax.dot_general(amps, ints, (((1,), (1,)), ((), ())), preferred_element_type=jnp.float32)
 
 
 def shifted(off_ref, amps_ref, base, count, limit):
@@ -60,13 +60,13 @@
         step = pl.program_id(0)
         parts = shifted(off_ref, amps_ref, step * BLOCK, BLOCK // LANES, BLOCK // LANES + 1)
         amps = jnp.concatenate([p.astype(jnp.bfloat16) for p in parts], axis=1)
-        acc_ref[...] += dot(ints_ref[...], amps)
+        acc_ref[...] += dot(amps, ints_ref[...])
 
     spec = pl.BlockSpec(
         (ints_hbm.shape[0], BLOCK), lambda j: (0, j), pipeline_mode=pl.Buffered(BUFFERS)
     )
     pltpu.emit_pipeline(body, grid=(steps,), in_specs=[spec])(ints_hbm)
-    out_ref[...] = acc_ref[...].T
+    out_ref[...] = acc_ref[...]
 
 
 def last_kernel(pieces, off_ref, amps_ref, ints_hbm, sum_ref, out_ref, acc_ref, sems, *buffers):
@@ -89,8 +89,8 @@
         copies[i].wait()
         if i + AHEAD < len(copies):
             copies[i + AHEAD].start()
-        acc_ref[...] += dot(buffers[i][...], amps)
-    out_ref[...] = acc_ref[...].T + sum_ref[...]
+        acc_ref[...] += dot(amps, buffers[i][...])
+    out_ref[...] = acc_ref[...] + sum_ref[...]
 
 
 def products(shift, amps, flat, cut, late):
@@ -99,7 +99,7 @@
     vmem = pl.BlockSpec(memory_space=pltpu.VMEM)
     smem = pl.BlockSpec(memory_space=pltpu.SMEM)
     total = jax.ShapeDtypeStruct((pairs, rows), jnp.float32)
-    acc = [pltpu.VMEM((rows, pairs), jnp.float32)]
+    acc = [pltpu.VMEM((pairs, rows), jnp.float32)]
     first = pl.pallas_call(
         functools.partial(first_kernel, cut // BLOCK),
         out_shape=total,
@@ -175,9 +175,8 @@
 
     part = total.reshape(z, x, core, col, pair_local, rows)
     part = exchange_sum(part.transpose(2, 0, 1, 3, 4, 5).reshape(core, z, x * col, pair_local, rows), "core")
-    part = part.transpose(1, 0, 2, 3)
-    part = lax.all_to_all(part, ("x", "col"), split_axis=0, concat_axis=0, tiled=True).sum(axis=0)
-    part = lax.all_to_all(part, "z", split_axis=0, concat_axis=0, tiled=True).sum(axis=0)
+    part = exchange_sum(part.transpose(1, 0, 2, 3), ("x", "col"))
+    part = exchange_sum(part, "z")
     return part.reshape(pair_local, window, virtuals)
 
 

time: 111 us -> 107 us (0.964)
  blocking collectives: 19.5 us -> 0 us
  starting transfers between devices: 11.4 us -> 19.4 us
  waiting for transfers between devices: 43 us -> 50.5 us
    all_to_all x2 -> x0, blocking collectives: 19.5 us -> none  [the longest x1 10.1 us: shards(): lax.all_to_all(part, 'z', split_axis=0, concat_axis=0, tiled=True)]
    ppermute x1 -> x7, starting transfers between devices: 0.33 us -> 8.33 us  [exchange_sum(): terms.append(lax.ppermute(block, names, [(i, to(i)) for i in range(count)]))]
    ppermute x1 -> x7, waiting for transfers between devices: 1.2 us -> 8.66 us  [exchange_sum(): terms.append(lax.ppermute(block, names, [(i, to(i)) for i in range(count)]))]
  transfers between devices with their start and end apart: 3 -> 9, of which waited for: 2 -> 7; matrix products, arithmetic and copies ran while one was open for 4% -> 4% of each run, Pallas kernels for 17% -> 18%
where the time goes in v9:
time: 107 us
  waiting for transfers between devices  50.5 us (47%)
  Pallas kernels  28.4 us (27%)
  starting transfers between devices  19.4 us (18%)
  local copies, waits for them, and re-layouts  8.16 us (8%)
    all_to_all x1, waiting for transfers between devices, shards(): here = lax.all_to_all(sent[0], ALL, split_axis=0, concat_axis=0, tiled=True)  41.8 us
    pallas_call x1, Pallas kernels, products(): pl.pallas_call(functools.partial(first_kernel, cut // BLOCK), out_shape=t...  18.1 us
    pallas_call x1, Pallas kernels, products(): pl.pallas_call(functools.partial(last_kernel, pieces), out_shape=total, i...  9.34 us
    ppermute x7, waiting for transfers between devices, exchange_sum(): terms.append(lax.ppermute(block, names, [(i, to(i)) for i in range(count)]))  8.66 us
    ppermute x7, starting transfers between devices, exchange_sum(): terms.append(lax.ppermute(block, names, [(i, to(i)) for i in range(count)]))  8.33 us
    all_to_all x1, starting transfers between devices, shards(): here = lax.all_to_all(sent[0], ALL, split_axis=0, concat_axis=0, tiled=True)  7.41 us
    reshape x1, local copies, waits for them, and re-layouts, shards(): here.reshape(pairs, widths[0])  3.86 us
    all_to_all x1, starting transfers between devices, shards(): late = lax.all_to_all(later, ALL, split_axis=0, concat_axis=0, tiled=True)  3.66 us
  transfers between devices with their start and end apart: 9, of which 7 were waited for; matrix products, arithmetic and copies ran while one was open for 4% of the time, Pallas kernels for 18%

profile of v9, /device:TPU:0, one launch (start us, length us, event | category | flops | bytes accessed | tf_op | source)
XLA Modules:
  0.0 106.9 jit_solution(2859215576637696616)
XLA Ops:
  0.0 0.0 copy-start
  0.0 1.7 %copy-done = bf16[2,640000]{1,0:T(2,128)(2,1)S(1)} copy-done((bf16[2,640000]{1,0:T(2,128)(2,1)S(1)}, bf16[2,640000]{1,0:T(2,128)(2,1)}, u32[]{:S(2)}) %copy-start) | copy-done | bytes 2560024
  1.7 0.1 windows.3
  1.8 0.0 copy-start.2
  1.9 1.2 %copy-done.2 = bf16[32,2,14208]{2,1,0:T(2,128)(2,1)} copy-done((bf16[32,2,14208]{2,1,0:T(2,128)(2,1)}, bf16[32,2,14208]{2,1,0:T(2,128)(2,1)S(1)}, u32[]{:S(2)}) %copy-start.2) | copy-done | bytes 1818648
  3.1 0.0 copy-start.1
  3.1 7.4 %all-to-all-start = ((bf16[32,2,14208]{2,1,0:T(2,128)(2,1)}), bf16[32,2,14208]{2,1,0:T(2,128)(2,1)}, u32[]{:S(2)}, u32[]{:S(2)}) async-start(bf16[32,2,14208]{2,1,0:T(2,128)(2,1)} %copy-done.2), calls=%async_computation | async-start | bytes 3637248 | tf_op jit(solution)/shard_map/all_to_all | solution.py:169
  10.5 0.0 copy-done.1
  10.5 0.9 windows.2
  11.4 41.8 %all-to-all-done = bf16[32,2,14208]{2,1,0:T(2,128)(2,1)} async-done(((bf16[32,2,14208]{2,1,0:T(2,128)(2,1)}), bf16[32,2,14208]{2,1,0:T(2,128)(2,1)}, u32[]{:S(2)}, u32[]{:S(2)}) %all-to-all-start) | async-done | bytes 1818656 | tf_op jit(solution)/shard_map/all_to_all | solution.py:169
  53.2 3.7 %all-to-all-start.1 = ((bf16[32,2,6016]{2,1,0:T(2,128)(2,1)}), bf16[32,2,6016]{2,1,0:T(2,128)(2,1)S(1)}, u32[]{:S(2)}, u32[]{:S(2)}) async-start(bf16[32,2,6016]{2,1,0:T(2,128)(2,1)} %windows.2), calls=%async_computation.1 | async-start | bytes 1540096 | tf_op jit(solution)/shard_map/all_to_all | solution.py:171
  56.9 0.1 pad_add_fusion.off_ref
  57.0 3.9 %reshape.28.amps_ref = bf16[64,14208]{1,0:T(8,128)(2,1)S(1)} reshape(bf16[32,2,14208]{2,1,0:T(2,128)(2,1)} %all-to-all-done) | data formatting | bytes 3637248 | tf_op jit(solution)/shard_map/reshape | solution.py:173
  60.9 18.1 %first_product.1.sum_ref = f32[64,1600]{1,0:T(8,128)S(1)} custom-call(s32[2]{0:T(128)S(1)} %pad_add_fusion.off_ref, bf16[64,14208]{1,0:T(8,128)(2,1)S(1)} %reshape.28.amps_ref, bf16[1600,20000]{1,0:T(8,128)(2,1)} %bitcast.34), custom_call_target="tpu_custom_call" | custom-call | flops 2883584000 | bytes 45056000 | tf_op jit(solution)/shard_map/first_product/pallas_call | solution.py:103
  79.0 0.0 all-to-all-done.1
  79.0 0.3 reshape.26.amps_ref
  79.3 9.3 %last_product.1 = f32[64,1600]{1,0:T(8,128)S(1)} custom-call(s32[2]{0:T(128)S(1)} %pad_add_fusion.off_ref, bf16[64,6016]{1,0:T(8,128)(2,1)S(1)} %reshape.26.amps_ref, bf16[1600,20000]{1,0:T(8,128)(2,1)} %bitcast.35, f32[64,1600]{1,0:T(8,128)S(1)} %first_product.1.sum_ref), custom_call_target="tpu_custom_call" | custom-call | flops 1212416000 | bytes 18944000 | tf_op jit(solution)/shard_map/last_product/pallas_call | solution.py:119
  88.6 0.2 reshape.29
  88.9 0.3 collective-permute-start
  89.3 1.2 %collective-permute-done = f32[4,4,2,1600]{3,2,1,0:T(2,128)S(1)} collective-permute-done((f32[4,4,2,1600]{3,2,1,0:T(2,128)S(1)}, f32[4,4,2,1600]{3,2,1,0:T(2,128)S(1)}, u32[]{:S(2)}, u32[]{:S(2)}) %collective-permute-start) | collective-permute-done | bytes 204832 | tf_op jit(solution)/shard_map/ppermute | solution.py:145
  90.5 0.1 bitcast_add_fusion
  90.6 2.7 %collective-permute-start.1 = (f32[4,2,1600]{2,1,0:T(2,128)S(1)}, f32[4,2,1600]{2,1,0:T(2,128)S(1)}, u32[]{:S(2)}, u32[]{:S(2)}) collective-permute-start(f32[4,2,1600]{2,1,0:T(2,128)S(1)} %get-tuple-element.9), channel_id=1, source_target_pairs={{0,5},{1,4},{4,1},{5,0},{2,7},{3,6},{6,3},{7,2},{8,13},{9,12},{12,... | collective-permute-start | bytes 153608 | tf_op jit(solution)/shard_map/ppermute | solution.py:145
  93.4 0.6 collective-permute-start.2
  93.9 0.3 collective-permute-start.3
  94.2 1.5 %collective-permute-done.1 = f32[4,2,1600]{2,1,0:T(2,128)S(1)} collective-permute-done((f32[4,2,1600]{2,1,0:T(2,128)S(1)}, f32[4,2,1600]{2,1,0:T(2,128)S(1)}, u32[]{:S(2)}, u32[]{:S(2)}) %collective-permute-start.1) | collective-permute-done | bytes 51232 | tf_op jit(solution)/shard_map/ppermute | solution.py:145
  95.7 1.8 %collective-permute-done.2 = f32[4,2,1600]{2,1,0:T(2,128)S(1)} collective-permute-done((f32[4,2,1600]{2,1,0:T(2,128)S(1)}, f32[4,2,1600]{2,1,0:T(2,128)S(1)}, u32[]{:S(2)}, u32[]{:S(2)}) %collective-permute-start.2) | collective-permute-done | bytes 51232 | tf_op jit(solution)/shard_map/ppermute | solution.py:145
  97.5 0.6 collective-permute-done.3
  98.1 3.4 %collective-permute-start.4 = (f32[2,1600]{1,0:T(2,128)S(1)}, f32[2,1600]{1,0:T(2,128)S(1)}, u32[]{:S(2)}, u32[]{:S(2)}) collective-permute-start(f32[2,1600]{1,0:T(2,128)S(1)} %get-tuple-element.12), channel_id=1, source_target_pairs={{0,24},{8,16},{16,8},{24,0},{1,25},{9,17},{17,9},{25,1},{2,26},{10... | collective-permute-start | bytes 38408 | tf_op jit(solution)/shard_map/ppermute | solution.py:145
  101.6 0.0 collective-permute-start.5
  101.6 1.0 collective-permute-start.6
  102.6 1.1 %collective-permute-done.4 = f32[2,1600]{1,0:T(2,128)S(1)} collective-permute-done((f32[2,1600]{1,0:T(2,128)S(1)}, f32[2,1600]{1,0:T(2,128)S(1)}, u32[]{:S(2)}, u32[]{:S(2)}) %collective-permute-start.4) | collective-permute-done | bytes 12832 | tf_op jit(solution)/shard_map/ppermute | solution.py:145
  103.7 2.5 %collective-permute-done.5 = f32[2,1600]{1,0:T(2,128)S(1)} collective-permute-done((f32[2,1600]{1,0:T(2,128)S(1)}, f32[2,1600]{1,0:T(2,128)S(1)}, u32[]{:S(2)}, u32[]{:S(2)}) %collective-permute-start.5) | collective-permute-done | bytes 12832 | tf_op jit(solution)/shard_map/ppermute | solution.py:145
  106.2 0.0 collective-permute-done.6
  106.2 0.7 reshape.31
  (6 shorter events, 0.2 us)
Async XLA Ops:
  0.0 1.7 %copy-start = (bf16[2,640000]{1,0:T(2,128)(2,1)S(1)}, bf16[2,640000]{1,0:T(2,128)(2,1)}, u32[]{:S(2)}) copy-start(bf16[2,640000]{1,0:T(2,128)(2,1)} %x_ref.3) | copy-start | bytes 7680004
  1.8 1.2 %copy-start.2 = (bf16[32,2,14208]{2,1,0:T(2,128)(2,1)}, bf16[32,2,14208]{2,1,0:T(2,128)(2,1)S(1)}, u32[]{:S(2)}) copy-start(bf16[32,2,14208]{2,1,0:T(2,128)(2,1)S(1)} %windows.3) | copy-start | bytes 5455876
  3.1 7.4 %copy-start.1 = (bf16[2,640000]{1,0:T(2,128)(2,1)S(1)}, bf16[2,640000]{1,0:T(2,128)(2,1)}, u32[]{:S(2)}) copy-start(bf16[2,640000]{1,0:T(2,128)(2,1)} %x_ref.3) | copy-start | bytes 7680004
  3.1 50.1 %all-to-all-start = ((bf16[32,2,14208]{2,1,0:T(2,128)(2,1)}), bf16[32,2,14208]{2,1,0:T(2,128)(2,1)}, u32[]{:S(2)}, u32[]{:S(2)}) async-start(bf16[32,2,14208]{2,1,0:T(2,128)(2,1)} %copy-done.2), calls=%async_computation | async-start | bytes 3637248 | tf_op jit(solution)/shard_map/all_to_all | solution.py:169
  53.2 25.7 %all-to-all-start.1 = ((bf16[32,2,6016]{2,1,0:T(2,128)(2,1)}), bf16[32,2,6016]{2,1,0:T(2,128)(2,1)S(1)}, u32[]{:S(2)}, u32[]{:S(2)}) async-start(bf16[32,2,6016]{2,1,0:T(2,128)(2,1)} %windows.2), calls=%async_computation.1 | async-start | bytes 1540096 | tf_op jit(solution)/shard_map/all_to_all | solution.py:171
  88.9 1.5 %collective-permute-start = (f32[4,4,2,1600]{3,2,1,0:T(2,128)S(1)}, f32[4,4,2,1600]{3,2,1,0:T(2,128)S(1)}, u32[]{:S(2)}, u32[]{:S(2)}) collective-permute-start(f32[4,4,2,1600]{3,2,1,0:T(2,128)S(1)} %dynamic-slice_bitcast_fusion), channel_id=1, source_target_pairs={{0,2},{2,0},{1,3},{3,1},{4,6},{6,4},{5,7},{7,5},{8,10},{10,8},{9,1... | collective-permute-start | bytes 614408 | tf_op jit(solution)/shard_map/ppermute | solution.py:145
  90.6 5.1 %collective-permute-start.1 = (f32[4,2,1600]{2,1,0:T(2,128)S(1)}, f32[4,2,1600]{2,1,0:T(2,128)S(1)}, u32[]{:S(2)}, u32[]{:S(2)}) collective-permute-start(f32[4,2,1600]{2,1,0:T(2,128)S(1)} %get-tuple-element.9), channel_id=1, source_target_pairs={{0,5},{1,4},{4,1},{5,0},{2,7},{3,6},{6,3},{7,2},{8,13},{9,12},{12,... | collective-permute-start | bytes 153608 | tf_op jit(solution)/shard_map/ppermute | solution.py:145
  93.4 4.1 %collective-permute-start.2 = (f32[4,2,1600]{2,1,0:T(2,128)S(1)}, f32[4,2,1600]{2,1,0:T(2,128)S(1)}, u32[]{:S(2)}, u32[]{:S(2)}) collective-permute-start(f32[4,2,1600]{2,1,0:T(2,128)S(1)} %get-tuple-element.11), channel_id=1, source_target_pairs={{0,4},{1,5},{4,0},{5,1},{2,6},{3,7},{6,2},{7,3},{8,12},{9,13},{12,... | collective-permute-start | bytes 153608 | tf_op jit(solution)/shard_map/ppermute | solution.py:145
  93.9 4.1 %collective-permute-start.3 = (f32[4,2,1600]{2,1,0:T(2,128)S(1)}, f32[4,2,1600]{2,1,0:T(2,128)S(1)}, u32[]{:S(2)}, u32[]{:S(2)}) collective-permute-start(f32[4,2,1600]{2,1,0:T(2,128)S(1)} %get-tuple-element.10), channel_id=1, source_target_pairs={{0,1},{1,0},{4,5},{5,4},{2,3},{3,2},{6,7},{7,6},{8,9},{9,8},{12,13... | collective-permute-start | bytes 153608 | tf_op jit(solution)/shard_map/ppermute | solution.py:145
  98.1 5.6 %collective-permute-start.4 = (f32[2,1600]{1,0:T(2,128)S(1)}, f32[2,1600]{1,0:T(2,128)S(1)}, u32[]{:S(2)}, u32[]{:S(2)}) collective-permute-start(f32[2,1600]{1,0:T(2,128)S(1)} %get-tuple-element.12), channel_id=1, source_target_pairs={{0,24},{8,16},{16,8},{24,0},{1,25},{9,17},{17,9},{25,1},{2,26},{10... | collective-permute-start | bytes 38408 | tf_op jit(solution)/shard_map/ppermute | solution.py:145
  101.6 4.6 %collective-permute-start.5 = (f32[2,1600]{1,0:T(2,128)S(1)}, f32[2,1600]{1,0:T(2,128)S(1)}, u32[]{:S(2)}, u32[]{:S(2)}) collective-permute-start(f32[2,1600]{1,0:T(2,128)S(1)} %get-tuple-element.14), channel_id=1, source_target_pairs={{0,16},{8,24},{16,0},{24,8},{1,17},{9,25},{17,1},{25,9},{2,18},{10... | collective-permute-start | bytes 38408 | tf_op jit(solution)/shard_map/ppermute | solution.py:145
  101.6 4.6 %collective-permute-start.6 = (f32[2,1600]{1,0:T(2,128)S(1)}, f32[2,1600]{1,0:T(2,128)S(1)}, u32[]{:S(2)}, u32[]{:S(2)}) collective-permute-start(f32[2,1600]{1,0:T(2,128)S(1)} %get-tuple-element.13), channel_id=1, source_target_pairs={{0,8},{8,0},{16,24},{24,16},{1,9},{9,1},{17,25},{25,17},{2,10},{10... | collective-permute-start | bytes 38408 | tf_op jit(solution)/shard_map/ppermute | solution.py:145

commit v10 on v9

--- a/solution.py
+++ b/solution.py
@@ -37,8 +37,8 @@
     )(x)
 
 
-def dot(amps, ints):
-    return lax.dot_general(amps, ints, (((1,), (1,)), ((), ())), preferred_element_type=jnp.float32)
+def dot(left, right):
+    return lax.dot_general(left, right, (((1,), (1,)), ((), ())), preferred_element_type=jnp.float32)
 
 
 def shifted(off_ref, amps_ref, base, count, limit):
@@ -60,13 +60,13 @@
         step = pl.program_id(0)
         parts = shifted(off_ref, amps_ref, step * BLOCK, BLOCK // LANES, BLOCK // LANES + 1)
         amps = jnp.concatenate([p.astype(jnp.bfloat16) for p in parts], axis=1)
-        acc_ref[...] += dot(amps, ints_ref[...])
+        acc_ref[...] += dot(ints_ref[...], amps)
 
     spec = pl.BlockSpec(
         (ints_hbm.shape[0], BLOCK), lambda j: (0, j), pipeline_mode=pl.Buffered(BUFFERS)
     )
     pltpu.emit_pipeline(body, grid=(steps,), in_specs=[spec])(ints_hbm)
-    out_ref[...] = acc_ref[...]
+    out_ref[...] = acc_ref[...].T
 
 
 def last_kernel(pieces, off_ref, amps_ref, ints_hbm, sum_ref, out_ref, acc_ref, sems, *buffers):
@@ -99,29 +99,30 @@
     vmem = pl.BlockSpec(memory_space=pltpu.VMEM)
     smem = pl.BlockSpec(memory_space=pltpu.SMEM)
     total = jax.ShapeDtypeStruct((pairs, rows), jnp.float32)
-    acc = [pltpu.VMEM((pairs, rows), jnp.float32)]
     first = pl.pallas_call(
         functools.partial(first_kernel, cut // BLOCK),
         out_shape=total,
         in_specs=[smem, vmem, pl.BlockSpec(memory_space=pl.ANY)],
         out_specs=vmem,
-        scratch_shapes=acc,
+        scratch_shapes=[pltpu.VMEM((rows, pairs), jnp.float32)],
         compiler_params=pltpu.CompilerParams(vmem_limit_bytes=LIMIT),
         cost_estimate=pl.CostEstimate(
             flops=2 * pairs * rows * cut, bytes_accessed=2 * rows * cut, transcendentals=0
         ),
         name="first_product",
     )(shift, amps, flat)
-    pieces = [(cut, min(BLOCK // 2, slab - cut))]
-    while sum(pieces[-1]) < slab:
-        start = sum(pieces[-1])
-        pieces.append((start, min(BLOCK, slab - start)))
+    pieces = []
+    start = cut
+    while start < slab:
+        size = min((384, 768)[len(pieces)] if len(pieces) < 2 else BLOCK, slab - start)
+        pieces.append((start, size))
+        start += size
     return pl.pallas_call(
         functools.partial(last_kernel, pieces),
         out_shape=total,
         in_specs=[smem, vmem, pl.BlockSpec(memory_space=pl.ANY), vmem],
         out_specs=vmem,
-        scratch_shapes=acc
+        scratch_shapes=[pltpu.VMEM((pairs, rows), jnp.float32)]
         + [pltpu.SemaphoreType.DMA((len(pieces),))]
         + [pltpu.VMEM((rows, size), flat.dtype) for _, size in pieces],
         compiler_params=pltpu.CompilerParams(vmem_limit_bytes=36 * 1024 * 1024),

time: 107 us -> 107 us (level)
  transfers between devices with their start and end apart: 9 -> 9, of which waited for: 7 -> 7; matrix products, arithmetic and copies ran while one was open for 4% -> 4% of each run, Pallas kernels for 18% -> 17%
where the time goes in v10:
time: 107 us; the launch traced here: 106 us
  waiting for transfers between devices  50.5 us (47%)
  Pallas kernels  27.9 us (26%)
  starting transfers between devices  19.4 us (18%)
  local copies, waits for them, and re-layouts  8.16 us (8%)
    all_to_all x1, waiting for transfers between devices, shards(): here = lax.all_to_all(sent[0], ALL, split_axis=0, concat_axis=0, tiled=True)  41.8 us
    pallas_call x1, Pallas kernels, products(): pl.pallas_call(functools.partial(first_kernel, cut // BLOCK), out_shape=t...  17.4 us
    pallas_call x1, Pallas kernels, products(): pl.pallas_call(functools.partial(last_kernel, pieces), out_shape=total, i...  9.46 us
    ppermute x7, waiting for transfers between devices, exchange_sum(): terms.append(lax.ppermute(block, names, [(i, to(i)) for i in range(count)]))  8.66 us
    ppermute x7, starting transfers between devices, exchange_sum(): terms.append(lax.ppermute(block, names, [(i, to(i)) for i in range(count)]))  8.34 us
    all_to_all x1, starting transfers between devices, shards(): here = lax.all_to_all(sent[0], ALL, split_axis=0, concat_axis=0, tiled=True)  7.41 us
    reshape x1, local copies, waits for them, and re-layouts, shards(): here.reshape(pairs, widths[0])  3.86 us
    all_to_all x1, starting transfers between devices, shards(): late = lax.all_to_all(later, ALL, split_axis=0, concat_axis=0, tiled=True)  3.66 us
  transfers between devices with their start and end apart: 9, of which 7 were waited for; matrix products, arithmetic and copies ran while one was open for 4% of the time, Pallas kernels for 17%

profile of v10, /device:TPU:0, one launch (start us, length us, event | category | flops | bytes accessed | tf_op | source)
XLA Modules:
  0.0 106.3 jit_solution(11490446736570061082)
XLA Ops:
  0.0 0.0 copy-start
  0.0 1.7 %copy-done = bf16[2,640000]{1,0:T(2,128)(2,1)S(1)} copy-done((bf16[2,640000]{1,0:T(2,128)(2,1)S(1)}, bf16[2,640000]{1,0:T(2,128)(2,1)}, u32[]{:S(2)}) %copy-start) | copy-done | bytes 2560024
  1.7 0.1 windows.3
  1.8 0.0 copy-start.2
  1.9 1.2 %copy-done.2 = bf16[32,2,14208]{2,1,0:T(2,128)(2,1)} copy-done((bf16[32,2,14208]{2,1,0:T(2,128)(2,1)}, bf16[32,2,14208]{2,1,0:T(2,128)(2,1)S(1)}, u32[]{:S(2)}) %copy-start.2) | copy-done | bytes 1818648
  3.1 0.0 copy-start.1
  3.1 7.4 %all-to-all-start = ((bf16[32,2,14208]{2,1,0:T(2,128)(2,1)}), bf16[32,2,14208]{2,1,0:T(2,128)(2,1)}, u32[]{:S(2)}, u32[]{:S(2)}) async-start(bf16[32,2,14208]{2,1,0:T(2,128)(2,1)} %copy-done.2), calls=%async_computation | async-start | bytes 3637248 | tf_op jit(solution)/shard_map/all_to_all | solution.py:170
  10.5 0.0 copy-done.1
  10.5 0.9 windows.2
  11.4 41.8 %all-to-all-done = bf16[32,2,14208]{2,1,0:T(2,128)(2,1)} async-done(((bf16[32,2,14208]{2,1,0:T(2,128)(2,1)}), bf16[32,2,14208]{2,1,0:T(2,128)(2,1)}, u32[]{:S(2)}, u32[]{:S(2)}) %all-to-all-start) | async-done | bytes 1818656 | tf_op jit(solution)/shard_map/all_to_all | solution.py:170
  53.2 3.7 %all-to-all-start.1 = ((bf16[32,2,6016]{2,1,0:T(2,128)(2,1)}), bf16[32,2,6016]{2,1,0:T(2,128)(2,1)S(1)}, u32[]{:S(2)}, u32[]{:S(2)}) async-start(bf16[32,2,6016]{2,1,0:T(2,128)(2,1)} %windows.2), calls=%async_computation.1 | async-start | bytes 1540096 | tf_op jit(solution)/shard_map/all_to_all | solution.py:172
  56.9 0.1 pad_add_fusion.off_ref
  57.0 3.9 %reshape.28.amps_ref = bf16[64,14208]{1,0:T(8,128)(2,1)S(1)} reshape(bf16[32,2,14208]{2,1,0:T(2,128)(2,1)} %all-to-all-done) | data formatting | bytes 3637248 | tf_op jit(solution)/shard_map/reshape | solution.py:174
  60.9 17.4 %first_product.1.sum_ref = f32[64,1600]{1,0:T(8,128)S(1)} custom-call(s32[2]{0:T(128)S(1)} %pad_add_fusion.off_ref, bf16[64,14208]{1,0:T(8,128)(2,1)S(1)} %reshape.28.amps_ref, bf16[1600,20000]{1,0:T(8,128)(2,1)} %bitcast.34), custom_call_target="tpu_custom_call" | custom-call | flops 2883584000 | bytes 45056000 | tf_op jit(solution)/shard_map/first_product/pallas_call | solution.py:102
  78.3 0.0 all-to-all-done.1
  78.3 0.3 reshape.26.amps_ref
  78.6 9.5 %last_product.1 = f32[64,1600]{1,0:T(8,128)S(1)} custom-call(s32[2]{0:T(128)S(1)} %pad_add_fusion.off_ref, bf16[64,6016]{1,0:T(8,128)(2,1)S(1)} %reshape.26.amps_ref, bf16[1600,20000]{1,0:T(8,128)(2,1)} %bitcast.35, f32[64,1600]{1,0:T(8,128)S(1)} %first_product.1.sum_ref), custom_call_target="tpu_custom_call" | custom-call | flops 1212416000 | bytes 18944000 | tf_op jit(solution)/shard_map/last_product/pallas_call | solution.py:120
  88.1 0.2 reshape.29
  88.4 0.3 collective-permute-start
  88.7 1.2 %collective-permute-done = f32[4,4,2,1600]{3,2,1,0:T(2,128)S(1)} collective-permute-done((f32[4,4,2,1600]{3,2,1,0:T(2,128)S(1)}, f32[4,4,2,1600]{3,2,1,0:T(2,128)S(1)}, u32[]{:S(2)}, u32[]{:S(2)}) %collective-permute-start) | collective-permute-done | bytes 204832 | tf_op jit(solution)/shard_map/ppermute | solution.py:146
  89.9 0.1 bitcast_add_fusion
  90.1 2.7 %collective-permute-start.1 = (f32[4,2,1600]{2,1,0:T(2,128)S(1)}, f32[4,2,1600]{2,1,0:T(2,128)S(1)}, u32[]{:S(2)}, u32[]{:S(2)}) collective-permute-start(f32[4,2,1600]{2,1,0:T(2,128)S(1)} %get-tuple-element.9), channel_id=1, source_target_pairs={{0,5},{1,4},{4,1},{5,0},{2,7},{3,6},{6,3},{7,2},{8,13},{9,12},{12,... | collective-permute-start | bytes 153608 | tf_op jit(solution)/shard_map/ppermute | solution.py:146
  92.8 0.6 collective-permute-start.2
  93.4 0.3 collective-permute-start.3
  93.6 1.5 %collective-permute-done.1 = f32[4,2,1600]{2,1,0:T(2,128)S(1)} collective-permute-done((f32[4,2,1600]{2,1,0:T(2,128)S(1)}, f32[4,2,1600]{2,1,0:T(2,128)S(1)}, u32[]{:S(2)}, u32[]{:S(2)}) %collective-permute-start.1) | collective-permute-done | bytes 51232 | tf_op jit(solution)/shard_map/ppermute | solution.py:146
  95.2 1.8 %collective-permute-done.2 = f32[4,2,1600]{2,1,0:T(2,128)S(1)} collective-permute-done((f32[4,2,1600]{2,1,0:T(2,128)S(1)}, f32[4,2,1600]{2,1,0:T(2,128)S(1)}, u32[]{:S(2)}, u32[]{:S(2)}) %collective-permute-start.2) | collective-permute-done | bytes 51232 | tf_op jit(solution)/shard_map/ppermute | solution.py:146
  97.0 0.6 collective-permute-done.3
  97.6 3.4 %collective-permute-start.4 = (f32[2,1600]{1,0:T(2,128)S(1)}, f32[2,1600]{1,0:T(2,128)S(1)}, u32[]{:S(2)}, u32[]{:S(2)}) collective-permute-start(f32[2,1600]{1,0:T(2,128)S(1)} %get-tuple-element.12), channel_id=1, source_target_pairs={{0,24},{8,16},{16,8},{24,0},{1,25},{9,17},{17,9},{25,1},{2,26},{10... | collective-permute-start | bytes 38408 | tf_op jit(solution)/shard_map/ppermute | solution.py:146
  101.0 0.0 collective-permute-start.5
  101.0 1.0 collective-permute-start.6
  102.1 1.1 %collective-permute-done.4 = f32[2,1600]{1,0:T(2,128)S(1)} collective-permute-done((f32[2,1600]{1,0:T(2,128)S(1)}, f32[2,1600]{1,0:T(2,128)S(1)}, u32[]{:S(2)}, u32[]{:S(2)}) %collective-permute-start.4) | collective-permute-done | bytes 12832 | tf_op jit(solution)/shard_map/ppermute | solution.py:146
  103.2 2.5 %collective-permute-done.5 = f32[2,1600]{1,0:T(2,128)S(1)} collective-permute-done((f32[2,1600]{1,0:T(2,128)S(1)}, f32[2,1600]{1,0:T(2,128)S(1)}, u32[]{:S(2)}, u32[]{:S(2)}) %collective-permute-start.5) | collective-permute-done | bytes 12832 | tf_op jit(solution)/shard_map/ppermute | solution.py:146
  105.6 0.0 collective-permute-done.6
  105.7 0.7 reshape.31
  (6 shorter events, 0.2 us)
Async XLA Ops:
  0.0 1.7 %copy-start = (bf16[2,640000]{1,0:T(2,128)(2,1)S(1)}, bf16[2,640000]{1,0:T(2,128)(2,1)}, u32[]{:S(2)}) copy-start(bf16[2,640000]{1,0:T(2,128)(2,1)} %x_ref.3) | copy-start | bytes 7680004
  1.8 1.2 %copy-start.2 = (bf16[32,2,14208]{2,1,0:T(2,128)(2,1)}, bf16[32,2,14208]{2,1,0:T(2,128)(2,1)S(1)}, u32[]{:S(2)}) copy-start(bf16[32,2,14208]{2,1,0:T(2,128)(2,1)S(1)} %windows.3) | copy-start | bytes 5455876
  3.1 7.4 %copy-start.1 = (bf16[2,640000]{1,0:T(2,128)(2,1)S(1)}, bf16[2,640000]{1,0:T(2,128)(2,1)}, u32[]{:S(2)}) copy-start(bf16[2,640000]{1,0:T(2,128)(2,1)} %x_ref.3) | copy-start | bytes 7680004
  3.1 50.1 %all-to-all-start = ((bf16[32,2,14208]{2,1,0:T(2,128)(2,1)}), bf16[32,2,14208]{2,1,0:T(2,128)(2,1)}, u32[]{:S(2)}, u32[]{:S(2)}) async-start(bf16[32,2,14208]{2,1,0:T(2,128)(2,1)} %copy-done.2), calls=%async_computation | async-start | bytes 3637248 | tf_op jit(solution)/shard_map/all_to_all | solution.py:170
  53.2 25.1 %all-to-all-start.1 = ((bf16[32,2,6016]{2,1,0:T(2,128)(2,1)}), bf16[32,2,6016]{2,1,0:T(2,128)(2,1)S(1)}, u32[]{:S(2)}, u32[]{:S(2)}) async-start(bf16[32,2,6016]{2,1,0:T(2,128)(2,1)} %windows.2), calls=%async_computation.1 | async-start | bytes 1540096 | tf_op jit(solution)/shard_map/all_to_all | solution.py:172
  88.4 1.5 %collective-permute-start = (f32[4,4,2,1600]{3,2,1,0:T(2,128)S(1)}, f32[4,4,2,1600]{3,2,1,0:T(2,128)S(1)}, u32[]{:S(2)}, u32[]{:S(2)}) collective-permute-start(f32[4,4,2,1600]{3,2,1,0:T(2,128)S(1)} %dynamic-slice_bitcast_fusion), channel_id=1, source_target_pairs={{0,2},{2,0},{1,3},{3,1},{4,6},{6,4},{5,7},{7,5},{8,10},{10,8},{9,1... | collective-permute-start | bytes 614408 | tf_op jit(solution)/shard_map/ppermute | solution.py:146
  90.1 5.1 %collective-permute-start.1 = (f32[4,2,1600]{2,1,0:T(2,128)S(1)}, f32[4,2,1600]{2,1,0:T(2,128)S(1)}, u32[]{:S(2)}, u32[]{:S(2)}) collective-permute-start(f32[4,2,1600]{2,1,0:T(2,128)S(1)} %get-tuple-element.9), channel_id=1, source_target_pairs={{0,5},{1,4},{4,1},{5,0},{2,7},{3,6},{6,3},{7,2},{8,13},{9,12},{12,... | collective-permute-start | bytes 153608 | tf_op jit(solution)/shard_map/ppermute | solution.py:146
  92.8 4.1 %collective-permute-start.2 = (f32[4,2,1600]{2,1,0:T(2,128)S(1)}, f32[4,2,1600]{2,1,0:T(2,128)S(1)}, u32[]{:S(2)}, u32[]{:S(2)}) collective-permute-start(f32[4,2,1600]{2,1,0:T(2,128)S(1)} %get-tuple-element.11), channel_id=1, source_target_pairs={{0,4},{1,5},{4,0},{5,1},{2,6},{3,7},{6,2},{7,3},{8,12},{9,13},{12,... | collective-permute-start | bytes 153608 | tf_op jit(solution)/shard_map/ppermute | solution.py:146
  93.4 4.1 %collective-permute-start.3 = (f32[4,2,1600]{2,1,0:T(2,128)S(1)}, f32[4,2,1600]{2,1,0:T(2,128)S(1)}, u32[]{:S(2)}, u32[]{:S(2)}) collective-permute-start(f32[4,2,1600]{2,1,0:T(2,128)S(1)} %get-tuple-element.10), channel_id=1, source_target_pairs={{0,1},{1,0},{4,5},{5,4},{2,3},{3,2},{6,7},{7,6},{8,9},{9,8},{12,13... | collective-permute-start | bytes 153608 | tf_op jit(solution)/shard_map/ppermute | solution.py:146
  97.6 5.6 %collective-permute-start.4 = (f32[2,1600]{1,0:T(2,128)S(1)}, f32[2,1600]{1,0:T(2,128)S(1)}, u32[]{:S(2)}, u32[]{:S(2)}) collective-permute-start(f32[2,1600]{1,0:T(2,128)S(1)} %get-tuple-element.12), channel_id=1, source_target_pairs={{0,24},{8,16},{16,8},{24,0},{1,25},{9,17},{17,9},{25,1},{2,26},{10... | collective-permute-start | bytes 38408 | tf_op jit(solution)/shard_map/ppermute | solution.py:146
  101.0 4.6 %collective-permute-start.5 = (f32[2,1600]{1,0:T(2,128)S(1)}, f32[2,1600]{1,0:T(2,128)S(1)}, u32[]{:S(2)}, u32[]{:S(2)}) collective-permute-start(f32[2,1600]{1,0:T(2,128)S(1)} %get-tuple-element.14), channel_id=1, source_target_pairs={{0,16},{8,24},{16,0},{24,8},{1,17},{9,25},{17,1},{25,9},{2,18},{10... | collective-permute-start | bytes 38408 | tf_op jit(solution)/shard_map/ppermute | solution.py:146
  101.0 4.6 %collective-permute-start.6 = (f32[2,1600]{1,0:T(2,128)S(1)}, f32[2,1600]{1,0:T(2,128)S(1)}, u32[]{:S(2)}, u32[]{:S(2)}) collective-permute-start(f32[2,1600]{1,0:T(2,128)S(1)} %get-tuple-element.13), channel_id=1, source_target_pairs={{0,8},{8,0},{16,24},{24,16},{1,9},{9,1},{17,25},{25,17},{2,10},{10... | collective-permute-start | bytes 38408 | tf_op jit(solution)/shard_map/ppermute | solution.py:146

commit v11 on v10

--- a/solution.py
+++ b/solution.py
@@ -11,7 +11,7 @@
 LANES = 128
 BLOCK = 1280
 BUFFERS = 3
-AHEAD = 2
+AHEAD = 3
 LIMIT = 20 * 1024 * 1024
 FIRST = 0.7
 

time: 107 us -> 106 us (level)
  no operation moved by 1% of the time
where the time goes in v11:
time: 106 us
  waiting for transfers between devices  50.5 us (48%)
  Pallas kernels  27.6 us (26%)
  starting transfers between devices  19.4 us (18%)
  local copies, waits for them, and re-layouts  8.16 us (8%)
    all_to_all x1, waiting for transfers between devices, shards(): here = lax.all_to_all(sent[0], ALL, split_axis=0, concat_axis=0, tiled=True)  41.8 us
    pallas_call x1, Pallas kernels, products(): pl.pallas_call(functools.partial(first_kernel, cut // BLOCK), out_shape=t...  17.4 us
    pallas_call x1, Pallas kernels, products(): pl.pallas_call(functools.partial(last_kernel, pieces), out_shape=total, i...  9.13 us
    ppermute x7, waiting for transfers between devices, exchange_sum(): terms.append(lax.ppermute(block, names, [(i, to(i)) for i in range(count)]))  8.66 us
    ppermute x7, starting transfers between devices, exchange_sum(): terms.append(lax.ppermute(block, names, [(i, to(i)) for i in range(count)]))  8.34 us
    all_to_all x1, starting transfers between devices, shards(): here = lax.all_to_all(sent[0], ALL, split_axis=0, concat_axis=0, tiled=True)  7.41 us
    reshape x1, local copies, waits for them, and re-layouts, shards(): here.reshape(pairs, widths[0])  3.86 us
    all_to_all x1, starting transfers between devices, shards(): late = lax.all_to_all(later, ALL, split_axis=0, concat_axis=0, tiled=True)  3.66 us
  transfers between devices with their start and end apart: 9, of which 7 were waited for; matrix products, arithmetic and copies ran while one was open for 4% of the time, Pallas kernels for 17%

profile of v11, /device:TPU:0, one launch (start us, length us, event | category | flops | bytes accessed | tf_op | source)
XLA Modules:
  0.0 106.0 jit_solution(13330471655351784469)
XLA Ops:
  0.0 0.0 copy-start
  0.0 1.7 %copy-done = bf16[2,640000]{1,0:T(2,128)(2,1)S(1)} copy-done((bf16[2,640000]{1,0:T(2,128)(2,1)S(1)}, bf16[2,640000]{1,0:T(2,128)(2,1)}, u32[]{:S(2)}) %copy-start) | copy-done | bytes 2560024
  1.7 0.1 windows.3
  1.8 0.0 copy-start.2
  1.9 1.2 %copy-done.2 = bf16[32,2,14208]{2,1,0:T(2,128)(2,1)} copy-done((bf16[32,2,14208]{2,1,0:T(2,128)(2,1)}, bf16[32,2,14208]{2,1,0:T(2,128)(2,1)S(1)}, u32[]{:S(2)}) %copy-start.2) | copy-done | bytes 1818648
  3.1 0.0 copy-start.1
  3.1 7.4 %all-to-all-start = ((bf16[32,2,14208]{2,1,0:T(2,128)(2,1)}), bf16[32,2,14208]{2,1,0:T(2,128)(2,1)}, u32[]{:S(2)}, u32[]{:S(2)}) async-start(bf16[32,2,14208]{2,1,0:T(2,128)(2,1)} %copy-done.2), calls=%async_computation | async-start | bytes 3637248 | tf_op jit(solution)/shard_map/all_to_all | solution.py:170
  10.5 0.0 copy-done.1
  10.5 0.9 windows.2
  11.4 41.8 %all-to-all-done = bf16[32,2,14208]{2,1,0:T(2,128)(2,1)} async-done(((bf16[32,2,14208]{2,1,0:T(2,128)(2,1)}), bf16[32,2,14208]{2,1,0:T(2,128)(2,1)}, u32[]{:S(2)}, u32[]{:S(2)}) %all-to-all-start) | async-done | bytes 1818656 | tf_op jit(solution)/shard_map/all_to_all | solution.py:170
  53.2 3.7 %all-to-all-start.1 = ((bf16[32,2,6016]{2,1,0:T(2,128)(2,1)}), bf16[32,2,6016]{2,1,0:T(2,128)(2,1)S(1)}, u32[]{:S(2)}, u32[]{:S(2)}) async-start(bf16[32,2,6016]{2,1,0:T(2,128)(2,1)} %windows.2), calls=%async_computation.1 | async-start | bytes 1540096 | tf_op jit(solution)/shard_map/all_to_all | solution.py:172
  56.9 0.1 pad_add_fusion.off_ref
  57.0 3.9 %reshape.28.amps_ref = bf16[64,14208]{1,0:T(8,128)(2,1)S(1)} reshape(bf16[32,2,14208]{2,1,0:T(2,128)(2,1)} %all-to-all-done) | data formatting | bytes 3637248 | tf_op jit(solution)/shard_map/reshape | solution.py:174
  60.9 17.4 %first_product.1.sum_ref = f32[64,1600]{1,0:T(8,128)S(1)} custom-call(s32[2]{0:T(128)S(1)} %pad_add_fusion.off_ref, bf16[64,14208]{1,0:T(8,128)(2,1)S(1)} %reshape.28.amps_ref, bf16[1600,20000]{1,0:T(8,128)(2,1)} %bitcast.34), custom_call_target="tpu_custom_call" | custom-call | flops 2883584000 | bytes 45056000 | tf_op jit(solution)/shard_map/first_product/pallas_call | solution.py:102
  78.3 0.0 all-to-all-done.1
  78.3 0.3 reshape.26.amps_ref
  78.6 9.1 %last_product.1 = f32[64,1600]{1,0:T(8,128)S(1)} custom-call(s32[2]{0:T(128)S(1)} %pad_add_fusion.off_ref, bf16[64,6016]{1,0:T(8,128)(2,1)S(1)} %reshape.26.amps_ref, bf16[1600,20000]{1,0:T(8,128)(2,1)} %bitcast.35, f32[64,1600]{1,0:T(8,128)S(1)} %first_product.1.sum_ref), custom_call_target="tpu_custom_call" | custom-call | flops 1212416000 | bytes 18944000 | tf_op jit(solution)/shard_map/last_product/pallas_call | solution.py:120
  87.7 0.2 reshape.29
  88.1 0.3 collective-permute-start
  88.4 1.2 %collective-permute-done = f32[4,4,2,1600]{3,2,1,0:T(2,128)S(1)} collective-permute-done((f32[4,4,2,1600]{3,2,1,0:T(2,128)S(1)}, f32[4,4,2,1600]{3,2,1,0:T(2,128)S(1)}, u32[]{:S(2)}, u32[]{:S(2)}) %collective-permute-start) | collective-permute-done | bytes 204832 | tf_op jit(solution)/shard_map/ppermute | solution.py:146
  89.6 0.1 bitcast_add_fusion
  89.8 2.7 %collective-permute-start.1 = (f32[4,2,1600]{2,1,0:T(2,128)S(1)}, f32[4,2,1600]{2,1,0:T(2,128)S(1)}, u32[]{:S(2)}, u32[]{:S(2)}) collective-permute-start(f32[4,2,1600]{2,1,0:T(2,128)S(1)} %get-tuple-element.9), channel_id=1, source_target_pairs={{0,5},{1,4},{4,1},{5,0},{2,7},{3,6},{6,3},{7,2},{8,13},{9,12},{12,... | collective-permute-start | bytes 153608 | tf_op jit(solution)/shard_map/ppermute | solution.py:146
  92.5 0.6 collective-permute-start.2
  93.1 0.3 collective-permute-start.3
  93.3 1.5 %collective-permute-done.1 = f32[4,2,1600]{2,1,0:T(2,128)S(1)} collective-permute-done((f32[4,2,1600]{2,1,0:T(2,128)S(1)}, f32[4,2,1600]{2,1,0:T(2,128)S(1)}, u32[]{:S(2)}, u32[]{:S(2)}) %collective-permute-start.1) | collective-permute-done | bytes 51232 | tf_op jit(solution)/shard_map/ppermute | solution.py:146
  94.9 1.8 %collective-permute-done.2 = f32[4,2,1600]{2,1,0:T(2,128)S(1)} collective-permute-done((f32[4,2,1600]{2,1,0:T(2,128)S(1)}, f32[4,2,1600]{2,1,0:T(2,128)S(1)}, u32[]{:S(2)}, u32[]{:S(2)}) %collective-permute-start.2) | collective-permute-done | bytes 51232 | tf_op jit(solution)/shard_map/ppermute | solution.py:146
  96.6 0.6 collective-permute-done.3
  97.3 3.4 %collective-permute-start.4 = (f32[2,1600]{1,0:T(2,128)S(1)}, f32[2,1600]{1,0:T(2,128)S(1)}, u32[]{:S(2)}, u32[]{:S(2)}) collective-permute-start(f32[2,1600]{1,0:T(2,128)S(1)} %get-tuple-element.12), channel_id=1, source_target_pairs={{0,24},{8,16},{16,8},{24,0},{1,25},{9,17},{17,9},{25,1},{2,26},{10... | collective-permute-start | bytes 38408 | tf_op jit(solution)/shard_map/ppermute | solution.py:146
  100.7 0.0 collective-permute-start.5
  100.7 1.0 collective-permute-start.6
  101.7 1.1 %collective-permute-done.4 = f32[2,1600]{1,0:T(2,128)S(1)} collective-permute-done((f32[2,1600]{1,0:T(2,128)S(1)}, f32[2,1600]{1,0:T(2,128)S(1)}, u32[]{:S(2)}, u32[]{:S(2)}) %collective-permute-start.4) | collective-permute-done | bytes 12832 | tf_op jit(solution)/shard_map/ppermute | solution.py:146
  102.8 2.5 %collective-permute-done.5 = f32[2,1600]{1,0:T(2,128)S(1)} collective-permute-done((f32[2,1600]{1,0:T(2,128)S(1)}, f32[2,1600]{1,0:T(2,128)S(1)}, u32[]{:S(2)}, u32[]{:S(2)}) %collective-permute-start.5) | collective-permute-done | bytes 12832 | tf_op jit(solution)/shard_map/ppermute | solution.py:146
  105.3 0.0 collective-permute-done.6
  105.3 0.7 reshape.31
  (6 shorter events, 0.2 us)
Async XLA Ops:
  0.0 1.7 %copy-start = (bf16[2,640000]{1,0:T(2,128)(2,1)S(1)}, bf16[2,640000]{1,0:T(2,128)(2,1)}, u32[]{:S(2)}) copy-start(bf16[2,640000]{1,0:T(2,128)(2,1)} %x_ref.3) | copy-start | bytes 7680004
  1.8 1.2 %copy-start.2 = (bf16[32,2,14208]{2,1,0:T(2,128)(2,1)}, bf16[32,2,14208]{2,1,0:T(2,128)(2,1)S(1)}, u32[]{:S(2)}) copy-start(bf16[32,2,14208]{2,1,0:T(2,128)(2,1)S(1)} %windows.3) | copy-start | bytes 5455876
  3.1 7.4 %copy-start.1 = (bf16[2,640000]{1,0:T(2,128)(2,1)S(1)}, bf16[2,640000]{1,0:T(2,128)(2,1)}, u32[]{:S(2)}) copy-start(bf16[2,640000]{1,0:T(2,128)(2,1)} %x_ref.3) | copy-start | bytes 7680004
  3.1 50.1 %all-to-all-start = ((bf16[32,2,14208]{2,1,0:T(2,128)(2,1)}), bf16[32,2,14208]{2,1,0:T(2,128)(2,1)}, u32[]{:S(2)}, u32[]{:S(2)}) async-start(bf16[32,2,14208]{2,1,0:T(2,128)(2,1)} %copy-done.2), calls=%async_computation | async-start | bytes 3637248 | tf_op jit(solution)/shard_map/all_to_all | solution.py:170
  53.2 25.1 %all-to-all-start.1 = ((bf16[32,2,6016]{2,1,0:T(2,128)(2,1)}), bf16[32,2,6016]{2,1,0:T(2,128)(2,1)S(1)}, u32[]{:S(2)}, u32[]{:S(2)}) async-start(bf16[32,2,6016]{2,1,0:T(2,128)(2,1)} %windows.2), calls=%async_computation.1 | async-start | bytes 1540096 | tf_op jit(solution)/shard_map/all_to_all | solution.py:172
  88.1 1.5 %collective-permute-start = (f32[4,4,2,1600]{3,2,1,0:T(2,128)S(1)}, f32[4,4,2,1600]{3,2,1,0:T(2,128)S(1)}, u32[]{:S(2)}, u32[]{:S(2)}) collective-permute-start(f32[4,4,2,1600]{3,2,1,0:T(2,128)S(1)} %dynamic-slice_bitcast_fusion), channel_id=1, source_target_pairs={{0,2},{2,0},{1,3},{3,1},{4,6},{6,4},{5,7},{7,5},{8,10},{10,8},{9,1... | collective-permute-start | bytes 614408 | tf_op jit(solution)/shard_map/ppermute | solution.py:146
  89.8 5.1 %collective-permute-start.1 = (f32[4,2,1600]{2,1,0:T(2,128)S(1)}, f32[4,2,1600]{2,1,0:T(2,128)S(1)}, u32[]{:S(2)}, u32[]{:S(2)}) collective-permute-start(f32[4,2,1600]{2,1,0:T(2,128)S(1)} %get-tuple-element.9), channel_id=1, source_target_pairs={{0,5},{1,4},{4,1},{5,0},{2,7},{3,6},{6,3},{7,2},{8,13},{9,12},{12,... | collective-permute-start | bytes 153608 | tf_op jit(solution)/shard_map/ppermute | solution.py:146
  92.5 4.1 %collective-permute-start.2 = (f32[4,2,1600]{2,1,0:T(2,128)S(1)}, f32[4,2,1600]{2,1,0:T(2,128)S(1)}, u32[]{:S(2)}, u32[]{:S(2)}) collective-permute-start(f32[4,2,1600]{2,1,0:T(2,128)S(1)} %get-tuple-element.11), channel_id=1, source_target_pairs={{0,4},{1,5},{4,0},{5,1},{2,6},{3,7},{6,2},{7,3},{8,12},{9,13},{12,... | collective-permute-start | bytes 153608 | tf_op jit(solution)/shard_map/ppermute | solution.py:146
  93.1 4.1 %collective-permute-start.3 = (f32[4,2,1600]{2,1,0:T(2,128)S(1)}, f32[4,2,1600]{2,1,0:T(2,128)S(1)}, u32[]{:S(2)}, u32[]{:S(2)}) collective-permute-start(f32[4,2,1600]{2,1,0:T(2,128)S(1)} %get-tuple-element.10), channel_id=1, source_target_pairs={{0,1},{1,0},{4,5},{5,4},{2,3},{3,2},{6,7},{7,6},{8,9},{9,8},{12,13... | collective-permute-start | bytes 153608 | tf_op jit(solution)/shard_map/ppermute | solution.py:146
  97.3 5.6 %collective-permute-start.4 = (f32[2,1600]{1,0:T(2,128)S(1)}, f32[2,1600]{1,0:T(2,128)S(1)}, u32[]{:S(2)}, u32[]{:S(2)}) collective-permute-start(f32[2,1600]{1,0:T(2,128)S(1)} %get-tuple-element.12), channel_id=1, source_target_pairs={{0,24},{8,16},{16,8},{24,0},{1,25},{9,17},{17,9},{25,1},{2,26},{10... | collective-permute-start | bytes 38408 | tf_op jit(solution)/shard_map/ppermute | solution.py:146
  100.7 4.6 %collective-permute-start.5 = (f32[2,1600]{1,0:T(2,128)S(1)}, f32[2,1600]{1,0:T(2,128)S(1)}, u32[]{:S(2)}, u32[]{:S(2)}) collective-permute-start(f32[2,1600]{1,0:T(2,128)S(1)} %get-tuple-element.14), channel_id=1, source_target_pairs={{0,16},{8,24},{16,0},{24,8},{1,17},{9,25},{17,1},{25,9},{2,18},{10... | collective-permute-start | bytes 38408 | tf_op jit(solution)/shard_map/ppermute | solution.py:146
  100.7 4.6 %collective-permute-start.6 = (f32[2,1600]{1,0:T(2,128)S(1)}, f32[2,1600]{1,0:T(2,128)S(1)}, u32[]{:S(2)}, u32[]{:S(2)}) collective-permute-start(f32[2,1600]{1,0:T(2,128)S(1)} %get-tuple-element.13), channel_id=1, source_target_pairs={{0,8},{8,0},{16,24},{24,16},{1,9},{9,1},{17,25},{25,17},{2,10},{10... | collective-permute-start | bytes 38408 | tf_op jit(solution)/shard_map/ppermute | solution.py:146
